TPU v7x, 256 devices: a whole 4x4x8 slice. The times are simulated.
256 devices in a mesh: dom: 64 (over y, z_hi, x, core), sub: 4 (over z_lo).
Axes of the slice: x: 4, y: 4, z: 8 (z_hi: 2, z_lo: 4; z = z_hi * 4 + z_lo), core: 2. Of those that a mesh axis runs over, the one named last changes fastest.
Arguments:
- nodes: bfloat16 [524288, 128], P(('dom', 'sub')), may hold values from -6 to 6
- weights: bfloat16 [4, 6, 128, 128], replicated, may hold values from -0.5 to 0.5
- edge_src: int32 [256, 12288], P(('dom', 'sub')), may hold values from 0 to 2303, as said below
- edge_dst: int32 [256, 12288], P(('dom', 'sub')), may hold values from 0 to 2047, as said below
- edge_valid: int32 [256, 12288], P(('dom', 'sub')), may hold values 0 or 1
- ghost_list: int32 [256, 2, 128], P(('dom', 'sub')), may hold values from 0 to 2047
- cluster_of: int32 [256, 2048], P(('dom', 'sub')), may hold values from 0 to 127
- owner: int32 [256, 128, 1], P(('dom', 'sub')), may hold values from 0 to 63; in each aligned block of 128 rows (0 to 127, 128 to 255, ..., all dimensions but the last counted through in order) at most 4 rows name the same one
- coarse_row: int32 [256, 128], P(('dom', 'sub')), may hold values from 0 to 127
- coarse_src: int32 [64, 768], P('dom'), may hold values from 0 to 159
- coarse_dst: int32 [64, 768], P('dom'), may hold values from 0 to 127
- coarse_ghosts: int32 [64, 2, 16], P('dom'), may hold values from 0 to 127
Outputs:
- fine_out: bfloat16 [524288, 128], P(('dom', 'sub'))
- coarse_out: bfloat16 [8192, 128], P('dom')
Inputs may be any that keep to these rules, and one draw needn't show every extreme that they name: Among the 128 clusters of any one device at most 4 have the same owner, and some owner has exactly 4 of them. `edge_dst`: A device's edge slots come in blocks of 768 slots; the slots of block b have destinations among rows b * 128 to b * 128 + 127. `edge_src`: read the device's table as the line of its lower neighbour's ghost rows, then its own 2048 rows, then its upper neighbour's ghost rows; the slots of edge block b have sources among positions b * 128 to b * 128 + 3 * 128 - 1 of that line.
All inputs are finite; a program needn't handle non-finite values. No bound on the sum of `edge_valid` on one device may be relied on, other than what follows from the above.
Results may differ from a plain program's by a relative error of at most 0.022.
Values may be sent and summed in bfloat16 or wider, within the bound.
No kernel may reach another device: no remote copies, remote signals or barrier semaphores. Data moves between devices by JAX's collectives and lax.ppermute only.
A program may use at most 64 MiB of HBM per device.

v0:
```python
import jax
import jax.numpy as jnp
from jax import lax
from jax.sharding import PartitionSpec as P


def with_halo(shard, sides, width):
    for axis, dim in sides:
        devices, length = (lax.axis_size(axis), shard.shape[dim])
        up = [(i, (i + 1) % devices) for i in range(devices - 1)]
        down = [(j, i) for i, j in up]
        last = lax.slice_in_dim(shard, length - width, length, axis=dim)
        first = lax.slice_in_dim(shard, 0, width, axis=dim)
        before = lax.ppermute(last, axis, up)
        after = lax.ppermute(first, axis, down)
        shard = jnp.concatenate([before, shard, after], axis=dim)
    return shard


def layer_norm(values):
    average = jnp.mean(values, axis=-1, keepdims=True)
    centred = values - average
    spread = jnp.mean(centred * centred, axis=-1, keepdims=True)
    return centred * lax.rsqrt(spread + 1e-05)


def node_update(block_rows, windows, local_from, local_to, valid, layer_weights):
    row_count, width_now = block_rows.shape
    block_count = windows.shape[0]
    block_rows_each = row_count // block_count
    window_size = windows.shape[1]
    target = jnp.dot(block_rows, layer_weights[1], preferred_element_type=jnp.float32).astype(
        jnp.bfloat16
    )
    target = target.reshape(block_count, block_rows_each, width_now)
    from_table = (
        local_from[:, :, None] == jnp.arange(window_size, dtype=jnp.int32)[None, None, :]
    ).astype(jnp.bfloat16)
    to_table = (
        local_to[:, :, None] == jnp.arange(block_rows_each, dtype=jnp.int32)[None, None, :]
    ).astype(jnp.bfloat16)
    picked_source = jnp.einsum(
        "bes,bsh->beh", from_table, windows, preferred_element_type=jnp.float32
    )
    picked_target = jnp.einsum("ber,brh->beh", to_table, target, preferred_element_type=jnp.float32)
    activated = jax.nn.silu(picked_source + picked_target).astype(jnp.bfloat16)
    message = jnp.einsum(
        "beh,hk->bek", activated, layer_weights[2], preferred_element_type=jnp.float32
    )
    message = (message * valid[:, :, None].astype(jnp.float32)).astype(jnp.bfloat16)
    gathered = jnp.einsum("ber,beh->brh", to_table, message, preferred_element_type=jnp.float32)
    gathered = gathered.reshape(row_count, width_now).astype(jnp.bfloat16)
    hidden = jnp.dot(block_rows, layer_weights[3], preferred_element_type=jnp.float32)
    hidden = hidden + jnp.dot(gathered, layer_weights[4], preferred_element_type=jnp.float32)
    hidden = jax.nn.silu(hidden).astype(jnp.bfloat16)
    update = jnp.dot(hidden, layer_weights[5], preferred_element_type=jnp.float32)
    return (block_rows.astype(jnp.float32) + layer_norm(update)).astype(jnp.bfloat16)


def pick_rows(rows_from, indices):
    chooser = (indices[:, None] == jnp.arange(rows_from.shape[0], dtype=jnp.int32)[None, :]).astype(
        jnp.bfloat16
    )
    return jnp.dot(chooser, rows_from, preferred_element_type=jnp.float32).astype(jnp.bfloat16)


def fine_layer(block_rows, lists, edge_from, edge_to, valid, layer_weights):
    row_count, width_now = block_rows.shape
    ghost_width = lists.shape[1]
    outgoing = pick_rows(block_rows, lists.reshape(-1))
    extended = with_halo(outgoing, ((("dom", "sub"), 0),), ghost_width)
    line = jnp.concatenate(
        [extended[:ghost_width], block_rows, extended[3 * ghost_width :]], axis=0
    )
    source = jnp.dot(line, layer_weights[0], preferred_element_type=jnp.float32).astype(
        jnp.bfloat16
    )
    block_count = row_count // ghost_width
    pieces = source.reshape(block_count + 2, ghost_width, width_now)
    windows = jnp.concatenate([pieces[:-2], pieces[1:-1], pieces[2:]], axis=1)
    position = jnp.where(
        edge_from < row_count,
        edge_from + ghost_width,
        jnp.where(edge_from < row_count + ghost_width, edge_from - row_count, edge_from),
    )
    starts = (jnp.arange(block_count, dtype=jnp.int32) * ghost_width)[:, None]
    local_from = position.reshape(block_count, -1) - starts
    local_to = edge_to.reshape(block_count, -1) - starts
    return node_update(
        block_rows, windows, local_from, local_to, valid.reshape(block_count, -1), layer_weights
    )


def coarse_layer(block_rows, lists, edge_from, edge_to, valid, layer_weights):
    ghost_width = lists.shape[1]
    outgoing = pick_rows(block_rows, lists.reshape(-1))
    extended = with_halo(outgoing, (("dom", 0),), ghost_width)
    incoming = jnp.concatenate(
        [block_rows, extended[:ghost_width], extended[3 * ghost_width :]], axis=0
    )
    source = jnp.dot(incoming, layer_weights[0], preferred_element_type=jnp.float32).astype(
        jnp.bfloat16
    )
    return node_update(
        block_rows, source[None], edge_from[None], edge_to[None], valid[None], layer_weights
    )


def on_device(
    nodes,
    weights,
    edge_src,
    edge_dst,
    edge_valid,
    ghost_list,
    cluster_of,
    owner,
    coarse_row,
    coarse_src,
    coarse_dst,
    coarse_ghosts,
):
    lists = ghost_list[0]
    edge_from = edge_src[0]
    edge_to = edge_dst[0]
    valid = edge_valid[0]
    states = nodes
    for layer_id in range(2):
        states = fine_layer(states, lists, edge_from, edge_to, valid, weights[layer_id])
    width_now = states.shape[1]
    dom_count = lax.axis_size("dom")
    clusters = owner.shape[1]
    capacity = 2 * clusters // dom_count
    slot_total = dom_count * capacity
    coarse_count = clusters * lax.axis_size("sub") // 4
    members = cluster_of[0]
    member_table = (members[None, :] == jnp.arange(clusters)[:, None]).astype(jnp.bfloat16)
    partial_sums = jnp.dot(member_table, states, preferred_element_type=jnp.float32)
    member_counts = jnp.sum(member_table.astype(jnp.float32), axis=1)
    owners = owner[0, :, 0]
    owner_table = (owners[:, None] == jnp.arange(dom_count)[None, :]).astype(jnp.float32)
    lower_table = (jnp.arange(clusters)[:, None] > jnp.arange(clusters)[None, :]).astype(
        jnp.float32
    )
    earlier = jnp.dot(lower_table, owner_table, precision=lax.Precision.HIGHEST)
    position = jnp.sum(earlier * owner_table, axis=1).astype(jnp.int32)
    slot_index = owners * capacity + position
    slot_table = (jnp.arange(slot_total)[:, None] == slot_index[None, :]).astype(jnp.float32)
    send_rows = jnp.dot(slot_table, partial_sums, precision=lax.Precision.HIGHEST).reshape(
        dom_count, capacity, width_now
    )
    send_counts = jnp.dot(slot_table, member_counts, precision=lax.Precision.HIGHEST).reshape(
        dom_count, capacity
    )
    send_ids = jnp.sum(slot_table.astype(jnp.int32) * coarse_row[0][None, :], axis=1).reshape(
        dom_count, capacity
    )
    got_rows, got_counts, got_ids = (
        lax.all_to_all(
            send_rows.astype(jnp.bfloat16), "dom", split_axis=0, concat_axis=0, tiled=True
        ).astype(send_rows.dtype),
        lax.all_to_all(
            send_counts.astype(jnp.bfloat16), "dom", split_axis=0, concat_axis=0, tiled=True
        ).astype(send_counts.dtype),
        lax.all_to_all(send_ids, "dom", split_axis=0, concat_axis=0, tiled=True),
    )
    flat_ids = got_ids.reshape(-1)
    id_table = (jnp.arange(coarse_count)[:, None] == flat_ids[None, :]).astype(jnp.float32)
    local_sums = jnp.dot(
        id_table, got_rows.reshape(slot_total, width_now), precision=lax.Precision.HIGHEST
    )
    local_counts = jnp.dot(id_table, got_counts.reshape(-1), precision=lax.Precision.HIGHEST)
    pooled_sums, counts = (
        lax.psum(local_sums.astype(jnp.bfloat16), "sub").astype(jnp.float32),
        lax.psum(local_counts.astype(jnp.bfloat16), "sub").astype(jnp.float32),
    )
    coarse = (pooled_sums / jnp.maximum(counts, 1.0)[:, None]).astype(jnp.bfloat16)
    coarse_valid = jnp.ones(coarse_src.shape[1:], jnp.int32)
    coarse = coarse_layer(
        coarse, coarse_ghosts[0], coarse_src[0], coarse_dst[0], coarse_valid, weights[2]
    )
    return_table = (flat_ids[:, None] == jnp.arange(coarse_count)[None, :]).astype(jnp.bfloat16)
    returned_rows = jnp.dot(return_table, coarse, preferred_element_type=jnp.float32).astype(
        jnp.bfloat16
    )
    returned_rows = lax.all_to_all(
        returned_rows.reshape(dom_count, capacity, width_now),
        "dom",
        split_axis=0,
        concat_axis=0,
        tiled=True,
    )
    cluster_table = (slot_index[:, None] == jnp.arange(slot_total)[None, :]).astype(jnp.bfloat16)
    cluster_rows = jnp.dot(
        cluster_table,
        returned_rows.reshape(slot_total, width_now),
        preferred_element_type=jnp.float32,
    ).astype(jnp.bfloat16)
    spread_table = (members[:, None] == jnp.arange(clusters)[None, :]).astype(jnp.bfloat16)
    fine_rows = jnp.dot(spread_table, cluster_rows, preferred_element_type=jnp.float32)
    lifted = (states.astype(jnp.float32) + fine_rows).astype(jnp.bfloat16)
    states = fine_layer(lifted, lists, edge_from, edge_to, valid, weights[3])
    return (states, coarse)


def solution(mesh):
    placed = (
        P(("dom", "sub"), None),
        P(),
        P(("dom", "sub"), None),
        P(("dom", "sub"), None),
        P(("dom", "sub"), None),
        P(("dom", "sub"), None, None),
        P(("dom", "sub"), None),
        P(("dom", "sub"), None, None),
        P(("dom", "sub"), None),
        P("dom", None),
        P("dom", None),
        P("dom", None, None),
    )
    return jax.shard_map(
        on_device,
        mesh=mesh,
        in_specs=placed,
        out_specs=(P(("dom", "sub"), None), P("dom", None)),
        check_vma=False,
    )
```

profile of v0, /device:TPU:1, one launch (start us, length us, event | category | flops | bytes accessed | tf_op | source)
XLA Modules:
  0.0 241.0 jit_solution(11393428760082592514)
XLA Ops:
  2.3 4.4 %collective-permute-start = (bf16[128,128]{1,0:T(8,128)(2,1)S(1)}, bf16[128,128]{1,0:T(8,128)(2,1)S(1)}, u32[]{:S(2)}, u32[]{:S(2)}) collective-permute-start(bf16[128,128]{1,0:T(8,128)(2,1)S(1)} %get-tuple-element.17), channel_id=1, source_target_pairs={{0,1},{1,2},{2,3},{3,4},{4,5},{5,6},{6,7},{7,8},{8,9},{9,10},{10,1... | collective-permute-start | bytes 98312 | tf_op jit(solution)/shard_map/ppermute | solution.py:14
  6.7 5.2 %collective-permute-start.1 = (bf16[128,128]{1,0:T(8,128)(2,1)S(1)}, bf16[128,128]{1,0:T(8,128)(2,1)S(1)}, u32[]{:S(2)}, u32[]{:S(2)}) collective-permute-start(bf16[128,128]{1,0:T(8,128)(2,1)S(1)} %get-tuple-element.18), channel_id=1, source_target_pairs={{1,0},{2,1},{3,2},{4,3},{5,4},{6,5},{7,6},{8,7},{9,8},{10,9},{11,1... | collective-permute-start | bytes 98312 | tf_op jit(solution)/shard_map/ppermute | solution.py:15
  15.5 14.3 %all-to-all-start.2 = ((bf16[64,1,4]{2,1,0:T(2,128)(2,1)}), bf16[64,1,4]{2,1,0:T(2,128)(2,1)S(1)}, u32[]{:S(2)}, u32[]{:S(2)}) async-start(bf16[64,1,4]{2,1,0:T(2,128)(2,1)} %copy.45), calls=%async_computation.2 | async-start | bytes 65536 | tf_op jit(solution)/shard_map/all_to_all | solution.py:162
  37.3 4.2 %all-to-all-done.2 = bf16[64,1,4]{2,1,0:T(2,128)(2,1)S(1)} async-done(((bf16[64,1,4]{2,1,0:T(2,128)(2,1)}), bf16[64,1,4]{2,1,0:T(2,128)(2,1)S(1)}, u32[]{:S(2)}, u32[]{:S(2)}) %all-to-all-start.2) | async-done | bytes 544 | tf_op jit(solution)/shard_map/all_to_all | solution.py:162
  41.4 8.6 %all-to-all-start = ((s32[64,1,4]{2,1,0:T(1,128)}), s32[64,1,4]{2,1,0:T(1,128)S(1)}, u32[]{:S(2)}, u32[]{:S(2)}) async-start(s32[64,1,4]{2,1,0:T(1,128)} %bitcast.28), calls=%async_computation | async-start | bytes 65536 | tf_op jit(solution)/shard_map/all_to_all | solution.py:165
  50.6 11.1 %all-to-all-done = s32[64,1,4]{2,1,0:T(1,128)S(1)} async-done(((s32[64,1,4]{2,1,0:T(1,128)}), s32[64,1,4]{2,1,0:T(1,128)S(1)}, u32[]{:S(2)}, u32[]{:S(2)}) %all-to-all-start) | async-done | bytes 1056 | tf_op jit(solution)/shard_map/all_to_all | solution.py:165
  63.8 6.5 %fusion.2 = f32[16,768,128]{2,1,0:T(8,128)} fusion(s32[16,768]{1,0:T(8,128)S(1)} %get-tuple-element.22, bf16[16,128,128]{2,1,0:T(8,128)(2,1)S(1)} %bitcast.171, bf16[16,128,128]{2,1,0:T(8,128)(2,1)S(1)} %bitcast.172, bf16[16,128,128]{2,1,0:T(8,128)(2,1)S(1)} %bitcast.170), kind=kOutput, calls=%fused_computation.3 | convolution fusion | flops 1217396736 | bytes 7913472 | tf_op jit(solution)/shard_map/bes,bsh->beh/dot_general | solution.py:42
  70.4 8.5 %fusion.21 = f32[16,768,128]{2,1,0:T(8,128)} fusion(f32[16,768,128]{2,1,0:T(8,128)} %fusion.2, bf16[16,128,128]{2,1,0:T(8,128)(2,1)S(1)} %bitcast.164, s32[16,768]{1,0:T(8,128)S(1)} %get-tuple-element.21, bf16[4,6,128,128]{3,2,1,0:T(8,128)(2,1)} %param.13), kind=kOutput, calls=%fused_computation.32 | convolution fusion | flops 816316416 | bytes 13189120 | tf_op jit(solution)/shard_map/beh,hk->bek/dot_general | solution.py:47
  78.8 4.2 %fusion.43 = bf16[16,128,128]{2,1,0:T(8,128)(2,1)S(1)} fusion(f32[16,768,128]{2,1,0:T(8,128)} %fusion.21, f32[16,768]{1,0:T(8,128)S(1)} %convert_element_type.218, s32[16,768]{1,0:T(8,128)S(1)} %get-tuple-element.21), kind=kOutput, calls=%fused_computation.62 | convolution fusion | flops 407633920 | bytes 6914048 | tf_op jit(solution)/shard_map/ber,beh->brh/dot_general | solution.py:51
  87.3 1.9 collective-permute-start.2
  89.2 5.6 %collective-permute-start.3 = (bf16[128,128]{1,0:T(8,128)(2,1)S(1)}, bf16[128,128]{1,0:T(8,128)(2,1)S(1)}, u32[]{:S(2)}, u32[]{:S(2)}) collective-permute-start(bf16[128,128]{1,0:T(8,128)(2,1)S(1)} %get-tuple-element.16), channel_id=1, source_target_pairs={{1,0},{2,1},{3,2},{4,3},{5,4},{6,5},{7,6},{8,7},{9,8},{10,9},{11,1... | collective-permute-start | bytes 98312 | tf_op jit(solution)/shard_map/ppermute | solution.py:15
  97.2 6.5 %fusion.1 = f32[16,768,128]{2,1,0:T(8,128)} fusion(s32[16,768]{1,0:T(8,128)S(1)} %get-tuple-element.22, bf16[16,128,128]{2,1,0:T(8,128)(2,1)S(1)} %bitcast.174, bf16[16,128,128]{2,1,0:T(8,128)(2,1)S(1)} %bitcast.175, bf16[16,128,128]{2,1,0:T(8,128)(2,1)S(1)} %bitcast.173), kind=kOutput, calls=%fused_computation.2 | convolution fusion | flops 1217396736 | bytes 7913472 | tf_op jit(solution)/shard_map/bes,bsh->beh/dot_general | solution.py:42
  103.7 8.5 %fusion.22 = f32[16,768,128]{2,1,0:T(8,128)} fusion(f32[16,768,128]{2,1,0:T(8,128)} %fusion.1, bf16[16,128,128]{2,1,0:T(8,128)(2,1)S(1)} %bitcast.166, s32[16,768]{1,0:T(8,128)S(1)} %get-tuple-element.21, bf16[4,6,128,128]{3,2,1,0:T(8,128)(2,1)} %param.13), kind=kOutput, calls=%fused_computation.33 | convolution fusion | flops 816316416 | bytes 13189120 | tf_op jit(solution)/shard_map/beh,hk->bek/dot_general | solution.py:47
  112.2 4.2 %fusion.44 = bf16[16,128,128]{2,1,0:T(8,128)(2,1)S(1)} fusion(f32[16,768,128]{2,1,0:T(8,128)} %fusion.22, f32[16,768]{1,0:T(8,128)S(1)} %convert_element_type.218, s32[16,768]{1,0:T(8,128)S(1)} %get-tuple-element.21), kind=kOutput, calls=%fused_computation.63 | convolution fusion | flops 407633920 | bytes 6914048 | tf_op jit(solution)/shard_map/ber,beh->brh/dot_general | solution.py:51
  120.5 6.5 %all-to-all-start.1 = ((bf16[64,4,128]{2,1,0:T(4,128)(2,1)}), bf16[64,4,128]{2,1,0:T(4,128)(2,1)S(1)}, u32[]{:S(2)}, u32[]{:S(2)}) async-start(bf16[64,4,128]{2,1,0:T(4,128)(2,1)} %bitcast.29), calls=%async_computation.1 | async-start | bytes 131072 | tf_op jit(solution)/shard_map/all_to_all | solution.py:159
  127.2 12.3 %all-to-all-done.1 = bf16[64,4,128]{2,1,0:T(4,128)(2,1)S(1)} async-done(((bf16[64,4,128]{2,1,0:T(4,128)(2,1)}), bf16[64,4,128]{2,1,0:T(4,128)(2,1)S(1)}, u32[]{:S(2)}, u32[]{:S(2)}) %all-to-all-start.1) | async-done | bytes 65568 | tf_op jit(solution)/shard_map/all_to_all | solution.py:159
  139.6 20.2 %all-reduce = (bf16[128,128]{1,0:T(8,128)(2,1)S(1)}, bf16[128]{0:T(256)(128)(2,1)S(1)}) all-reduce(bf16[128,128]{1,0:T(8,128)(2,1)S(1)} %convolution_convert_fusion.12, bf16[128]{0:T(256)(128)(2,1)S(1)} %fusion.53), channel_id=1, replica_groups=mesh['dom'=64,'sub'=4] {'sub'}, use_global_device_ids=true, to_apply=%region_6.7 | all-reduce | flops 16512 | bytes 66048 | tf_op jit(solution)/shard_map/psum | solution.py:174
  160.1 6.3 %collective-permute-start.4 = (bf16[16,128]{1,0:T(8,128)(2,1)S(1)}, bf16[16,128]{1,0:T(8,128)(2,1)S(1)}, u32[]{:S(2)}, u32[]{:S(2)}) collective-permute-start(bf16[16,128]{1,0:T(8,128)(2,1)S(1)} %get-tuple-element.19), channel_id=1, source_target_pairs={{0,4},{4,8},{8,12},{12,16},{16,20},{20,24},{24,28},{28,32},{32,36}... | collective-permute-start | bytes 12296 | tf_op jit(solution)/shard_map/ppermute | solution.py:14
  169.3 2.1 collective-permute-done.5
  176.7 29.6 %all_to_all.28 = bf16[64,4,128]{2,1,0:T(4,128)(2,1)S(1)} all-to-all(bf16[64,4,128]{2,1,0:T(4,128)(2,1)S(1)} %bitcast.181), channel_id=1, replica_groups=mesh['dom'=64,'sub'=4] {'dom'}, dimensions={0} | all-to-all | bytes 131072 | tf_op jit(solution)/shard_map/all_to_all | solution.py:186
  210.3 5.4 %collective-permute-start.7 = (bf16[128,128]{1,0:T(8,128)(2,1)S(1)}, bf16[128,128]{1,0:T(8,128)(2,1)S(1)}, u32[]{:S(2)}, u32[]{:S(2)}) collective-permute-start(bf16[128,128]{1,0:T(8,128)(2,1)S(1)} %get-tuple-element.14), channel_id=1, source_target_pairs={{1,0},{2,1},{3,2},{4,3},{5,4},{6,5},{7,6},{8,7},{9,8},{10,9},{11,1... | collective-permute-start | bytes 98312 | tf_op jit(solution)/shard_map/ppermute | solution.py:15
  218.1 6.5 %fusion = f32[16,768,128]{2,1,0:T(8,128)} fusion(s32[16,768]{1,0:T(8,128)S(1)} %get-tuple-element.22, bf16[16,128,128]{2,1,0:T(8,128)(2,1)S(1)} %bitcast.168, bf16[16,128,128]{2,1,0:T(8,128)(2,1)S(1)} %bitcast.169, bf16[16,128,128]{2,1,0:T(8,128)(2,1)S(1)} %bitcast.167), kind=kOutput, calls=%fused_computation.1 | convolution fusion | flops 1217396736 | bytes 7913472 | tf_op jit(solution)/shard_map/bes,bsh->beh/dot_general | solution.py:42
  224.6 8.5 %fusion.23 = f32[16,768,128]{2,1,0:T(8,128)} fusion(f32[16,768,128]{2,1,0:T(8,128)} %fusion, bf16[16,128,128]{2,1,0:T(8,128)(2,1)S(1)} %bitcast.165, s32[16,768]{1,0:T(8,128)S(1)} %get-tuple-element.21, bf16[4,6,128,128]{3,2,1,0:T(8,128)(2,1)} %param.13), kind=kOutput, calls=%fused_computation.34 | convolution fusion | flops 816316416 | bytes 13189120 | tf_op jit(solution)/shard_map/beh,hk->bek/dot_general | solution.py:47
  233.1 4.2 %fusion.45 = bf16[16,128,128]{2,1,0:T(8,128)(2,1)S(1)} fusion(f32[16,768,128]{2,1,0:T(8,128)} %fusion.23, f32[16,768]{1,0:T(8,128)S(1)} %convert_element_type.218, s32[16,768]{1,0:T(8,128)S(1)} %get-tuple-element.21), kind=kOutput, calls=%fused_computation.64 | convolution fusion | flops 407633920 | bytes 6914048 | tf_op jit(solution)/shard_map/ber,beh->brh/dot_general | solution.py:51
  (108 shorter events, 44.5 us)
Async XLA Ops:
  0.6 61.9 %copy-start = (bf16[2048,128]{1,0:T(8,128)(2,1)S(1)}, bf16[2048,128]{1,0:T(8,128)(2,1)}, u32[]{:S(2)}) copy-start(bf16[2048,128]{1,0:T(8,128)(2,1)} %param.12) | copy-start | bytes 1572868
  0.6 35.8 %copy-start.6 = (s32[1,128]{1,0:T(1,128)S(1)}, s32[1,128]{1,0:T(1,128)}, u32[]{:S(2)}) copy-start(s32[1,128]{1,0:T(1,128)} %param.20) | copy-start | bytes 1540
  0.7 49.4 %copy-start.2 = (s32[1,12288]{1,0:T(1,128)S(1)}, s32[1,12288]{1,0:T(1,128)}, u32[]{:S(2)}) copy-start(s32[1,12288]{1,0:T(1,128)} %param.16) | copy-start | bytes 147460
  0.7 49.5 %copy-start.7 = (s32[1,2,16]{2,1,0:T(2,128)S(1)}, s32[1,2,16]{2,1,0:T(2,128)}, u32[]{:S(2)}) copy-start(s32[1,2,16]{2,1,0:T(2,128)} %param.23) | copy-start | bytes 388
  0.7 49.6 %copy-start.4 = (s32[1,768]{1,0:T(1,128)S(1)}, s32[1,768]{1,0:T(1,128)}, u32[]{:S(2)}) copy-start(s32[1,768]{1,0:T(1,128)} %param.21) | copy-start | bytes 9220
  0.7 49.6 %copy-start.5 = (s32[1,768]{1,0:T(1,128)S(1)}, s32[1,768]{1,0:T(1,128)}, u32[]{:S(2)}) copy-start(s32[1,768]{1,0:T(1,128)} %param.22) | copy-start | bytes 9220
  2.3 60.2 %collective-permute-start = (bf16[128,128]{1,0:T(8,128)(2,1)S(1)}, bf16[128,128]{1,0:T(8,128)(2,1)S(1)}, u32[]{:S(2)}, u32[]{:S(2)}) collective-permute-start(bf16[128,128]{1,0:T(8,128)(2,1)S(1)} %get-tuple-element.17), channel_id=1, source_target_pairs={{0,1},{1,2},{2,3},{3,4},{4,5},{5,6},{6,7},{7,8},{8,9},{9,10},{10,1... | collective-permute-start | bytes 98312 | tf_op jit(solution)/shard_map/ppermute | solution.py:14
  6.7 55.9 %collective-permute-start.1 = (bf16[128,128]{1,0:T(8,128)(2,1)S(1)}, bf16[128,128]{1,0:T(8,128)(2,1)S(1)}, u32[]{:S(2)}, u32[]{:S(2)}) collective-permute-start(bf16[128,128]{1,0:T(8,128)(2,1)S(1)} %get-tuple-element.18), channel_id=1, source_target_pairs={{1,0},{2,1},{3,2},{4,3},{5,4},{6,5},{7,6},{8,7},{9,8},{10,9},{11,1... | collective-permute-start | bytes 98312 | tf_op jit(solution)/shard_map/ppermute | solution.py:15
  15.5 25.9 %all-to-all-start.2 = ((bf16[64,1,4]{2,1,0:T(2,128)(2,1)}), bf16[64,1,4]{2,1,0:T(2,128)(2,1)S(1)}, u32[]{:S(2)}, u32[]{:S(2)}) async-start(bf16[64,1,4]{2,1,0:T(2,128)(2,1)} %copy.45), calls=%async_computation.2 | async-start | bytes 65536 | tf_op jit(solution)/shard_map/all_to_all | solution.py:162
  41.4 20.2 %all-to-all-start = ((s32[64,1,4]{2,1,0:T(1,128)}), s32[64,1,4]{2,1,0:T(1,128)S(1)}, u32[]{:S(2)}, u32[]{:S(2)}) async-start(s32[64,1,4]{2,1,0:T(1,128)} %bitcast.28), calls=%async_computation | async-start | bytes 65536 | tf_op jit(solution)/shard_map/all_to_all | solution.py:165
  83.0 2.7 %copy-start.8 = (s32[1,2,128]{2,1,0:T(2,128)S(1)}, s32[1,2,128]{2,1,0:T(2,128)}, u32[]{:S(2)}) copy-start(s32[1,2,128]{2,1,0:T(2,128)} %param.17) | copy-start | bytes 3076
  87.3 8.6 %collective-permute-start.2 = (bf16[128,128]{1,0:T(8,128)(2,1)S(1)}, bf16[128,128]{1,0:T(8,128)(2,1)S(1)}, u32[]{:S(2)}, u32[]{:S(2)}) collective-permute-start(bf16[128,128]{1,0:T(8,128)(2,1)S(1)} %get-tuple-element.15), channel_id=1, source_target_pairs={{0,1},{1,2},{2,3},{3,4},{4,5},{5,6},{6,7},{7,8},{8,9},{9,10},{10,1... | collective-permute-start | bytes 98312 | tf_op jit(solution)/shard_map/ppermute | solution.py:14
  89.2 6.7 %collective-permute-start.3 = (bf16[128,128]{1,0:T(8,128)(2,1)S(1)}, bf16[128,128]{1,0:T(8,128)(2,1)S(1)}, u32[]{:S(2)}, u32[]{:S(2)}) collective-permute-start(bf16[128,128]{1,0:T(8,128)(2,1)S(1)} %get-tuple-element.16), channel_id=1, source_target_pairs={{1,0},{2,1},{3,2},{4,3},{5,4},{6,5},{7,6},{8,7},{9,8},{10,9},{11,1... | collective-permute-start | bytes 98312 | tf_op jit(solution)/shard_map/ppermute | solution.py:15
  116.4 3.0 %copy-start.3 = (s32[1,2048]{1,0:T(1,128)S(1)}, s32[1,2048]{1,0:T(1,128)}, u32[]{:S(2)}) copy-start(s32[1,2048]{1,0:T(1,128)} %param.18) | copy-start | bytes 24580
  120.5 18.9 %all-to-all-start.1 = ((bf16[64,4,128]{2,1,0:T(4,128)(2,1)}), bf16[64,4,128]{2,1,0:T(4,128)(2,1)S(1)}, u32[]{:S(2)}, u32[]{:S(2)}) async-start(bf16[64,4,128]{2,1,0:T(4,128)(2,1)} %bitcast.29), calls=%async_computation.1 | async-start | bytes 131072 | tf_op jit(solution)/shard_map/all_to_all | solution.py:159
  160.1 9.1 %collective-permute-start.4 = (bf16[16,128]{1,0:T(8,128)(2,1)S(1)}, bf16[16,128]{1,0:T(8,128)(2,1)S(1)}, u32[]{:S(2)}, u32[]{:S(2)}) collective-permute-start(bf16[16,128]{1,0:T(8,128)(2,1)S(1)} %get-tuple-element.19), channel_id=1, source_target_pairs={{0,4},{4,8},{8,12},{12,16},{16,20},{20,24},{24,28},{28,32},{32,36}... | collective-permute-start | bytes 12296 | tf_op jit(solution)/shard_map/ppermute | solution.py:14
  166.5 4.9 %collective-permute-start.5 = (bf16[16,128]{1,0:T(8,128)(2,1)S(1)}, bf16[16,128]{1,0:T(8,128)(2,1)S(1)}, u32[]{:S(2)}, u32[]{:S(2)}) collective-permute-start(bf16[16,128]{1,0:T(8,128)(2,1)S(1)} %get-tuple-element.20), channel_id=1, source_target_pairs={{4,0},{8,4},{12,8},{16,12},{20,16},{24,20},{28,24},{32,28},{36,32}... | collective-permute-start | bytes 12296 | tf_op jit(solution)/shard_map/ppermute | solution.py:15
  176.5 41.6 %copy-start.1 = (bf16[128,128]{1,0:T(8,128)(2,1)}, bf16[128,128]{1,0:T(8,128)(2,1)S(1)}, u32[]{:S(2)}) copy-start(bf16[128,128]{1,0:T(8,128)(2,1)S(1)} %add_convert_fusion.3) | copy-start | bytes 98308
  208.3 8.4 %collective-permute-start.6 = (bf16[128,128]{1,0:T(8,128)(2,1)S(1)}, bf16[128,128]{1,0:T(8,128)(2,1)S(1)}, u32[]{:S(2)}, u32[]{:S(2)}) collective-permute-start(bf16[128,128]{1,0:T(8,128)(2,1)S(1)} %get-tuple-element.13), channel_id=1, source_target_pairs={{0,1},{1,2},{2,3},{3,4},{4,5},{5,6},{6,7},{7,8},{8,9},{9,10},{10,1... | collective-permute-start | bytes 98312 | tf_op jit(solution)/shard_map/ppermute | solution.py:14
  210.3 6.5 %collective-permute-start.7 = (bf16[128,128]{1,0:T(8,128)(2,1)S(1)}, bf16[128,128]{1,0:T(8,128)(2,1)S(1)}, u32[]{:S(2)}, u32[]{:S(2)}) collective-permute-start(bf16[128,128]{1,0:T(8,128)(2,1)S(1)} %get-tuple-element.14), channel_id=1, source_target_pairs={{1,0},{2,1},{3,2},{4,3},{5,4},{6,5},{7,6},{8,7},{9,8},{10,9},{11,1... | collective-permute-start | bytes 98312 | tf_op jit(solution)/shard_map/ppermute | solution.py:15
where the time goes:
time: 244 us; the launch traced here: 241 us
  matrix products  83.3 us (34%)
  starting transfers between devices  62.1 us (25%)
  blocking collectives  49.8 us (20%)
  waiting for transfers between devices  29.7 us (12%)
  other arithmetic  11.1 us (5%)
  local copies, waits for them, and re-layouts  3.82 us (2%)
    all_to_all x1, blocking collectives, on_device(): lax.all_to_all(returned_rows.reshape(dom_count, capacity, width_now), 'do...  29.6 us
    dot_general x3, matrix products, node_update(): jnp.einsum('beh,hk->bek', activated, layer_weights[2], preferred_element_...  25.4 us
    dot_general x4, matrix products, node_update(): jnp.einsum('bes,bsh->beh', from_table, windows, preferred_element_type=jn...  20.8 us
    psum x1, blocking collectives, on_device(): lax.psum(local_sums.astype(jnp.bfloat16), 'sub').astype(jnp.float32)  20.2 us
    ppermute x4, starting transfers between devices, with_halo(): after = lax.ppermute(first, axis, down)  18.2 us
    ppermute x4, starting transfers between devices, with_halo(): before = lax.ppermute(last, axis, up)  14.5 us
    all_to_all x1, starting transfers between devices, on_device(): lax.all_to_all(send_counts.astype(jnp.bfloat16), 'dom', split_axis=0, con...  14.3 us
    dot_general x4, matrix products, node_update(): jnp.einsum('ber,beh->brh', to_table, message, preferred_element_type=jnp....  13.8 us
  transfers between devices with their start and end apart: 11, of which 4 were waited for; matrix products, arithmetic and copies ran while one was open for 6% of the time, Pallas kernels for 0%

commit v1 on v0

v1 whole, which is shorter than its diff:
```python
import functools

import jax
import jax.numpy as jnp
from jax import lax
from jax.experimental import pallas as pl
from jax.experimental.pallas import tpu as pltpu
from jax.sharding import PartitionSpec as P

BF = jnp.bfloat16
F32 = jnp.float32
I32 = jnp.int32
I16 = jnp.int16
NN = (((1,), (0,)), ((), ()))
NT = (((1,), (1,)), ((), ()))
TN = (((0,), (0,)), ((), ()))

GH = 128
CAP = 4
SLOTS = 16
VMEM_LIMIT = 28 << 20


def dot(left, right, dims=NN):
    return lax.dot_general(left, right, dims, preferred_element_type=F32)


def iota(shape, dim, dtype=I32):
    return lax.broadcasted_iota(I32, shape, dim).astype(dtype)


def hot(mask):
    return jnp.where(mask, 1.0, 0.0).astype(BF)


def column(row):
    return jnp.broadcast_to(row.astype(F32), (128, 128)).T


def half_silu(half):
    return half * (1.0 + jnp.tanh(half))


def rows_hot(index_row, count):
    table = lax.broadcasted_iota(I16, (count, index_row.shape[1]), 0)
    return jnp.where(table == index_row.astype(I16), BF(1), BF(0))


def edge_sum(source_t, target_t, from_row, to_row):
    from_hot = rows_hot(from_row, source_t.shape[1])
    to_hot = rows_hot(to_row, target_t.shape[1])
    table = jnp.concatenate([source_t, target_t], axis=1)
    half = dot(table, jnp.concatenate([from_hot, to_hot], axis=0))
    return dot(to_hot, half_silu(half).astype(BF), NT).astype(BF)


def node_weights(w):
    both = jnp.concatenate([w[3] * BF(0.5), (dot(w[2], w[4]) * 0.5).astype(BF)], axis=0)
    last = w[5].astype(F32)
    return both, (last - jnp.mean(last, axis=1, keepdims=True)).astype(BF)


def node_update(rows, sums, both, last):
    half = dot(jnp.concatenate([rows, sums], axis=1), both)
    centred = dot(half_silu(half).astype(BF), last)
    spread = jnp.mean(centred * centred, axis=1, keepdims=True)
    return (rows.astype(F32) + centred * lax.rsqrt(spread + 1e-5)).astype(BF)


def local_edges(b, row_count, src, dst, valid, width):
    at = pl.ds(b * width, width)
    edge = src[:, at]
    line = jnp.where(
        edge < row_count, edge + GH, jnp.where(edge < row_count + GH, edge - row_count, edge)
    )
    return line - b * GH, jnp.where(valid[:, at] != 0, dst[:, at] - b * GH, -1)


def pick_rows(rows_ref, list_row):
    count = rows_ref.shape[0]
    wanted = column(list_row)
    lanes = iota((128, 128), 1, F32)
    table = jnp.concatenate(
        [hot(wanted == lanes + float(128 * k)) for k in range(count // 128)], axis=1
    )
    return dot(table, rows_ref[...]).astype(BF)


def pick_both(rows_ref, lists, odd, near, far):
    to_lower, to_upper = lists[0:1, :], lists[1:2, :]
    near[...] = pick_rows(rows_ref, jnp.where(odd, to_lower, to_upper))
    far[...] = pick_rows(rows_ref, jnp.where(odd, to_upper, to_lower))


def pick_kernel(place, rows_ref, lists, near, far):
    pick_both(rows_ref, lists, place[1] % 2 == 1, near, far)


def inner_kernel(layer, rows_ref, weights, src, dst, valid, out, source, target, sums):
    w = [weights[layer, i] for i in range(6)]
    row_count = rows_ref.shape[0]
    blocks = row_count // GH
    width = src.shape[1] // blocks
    source[...] = dot(w[0] * BF(0.5), rows_ref[...], (((0,), (1,)), ((), ()))).astype(BF)
    target[...] = dot(w[1] * BF(0.5), rows_ref[...], (((0,), (1,)), ((), ()))).astype(BF)
    for b in range(1, blocks - 1):
        from_row, to_row = local_edges(b, row_count, src, dst, valid, width)
        sums[b * GH : (b + 1) * GH, :] = edge_sum(
            source[:, (b - 1) * GH : (b + 2) * GH],
            target[:, b * GH : (b + 1) * GH],
            from_row,
            to_row,
        )
    both, last = node_weights(w)
    step = 2 * GH
    for first in range(GH, row_count - GH, step):
        at = pl.ds(first, step)
        out[at, :] = node_update(rows_ref[at, :], sums[at, :], both, last)


def end_rows(layer, place, rows_ref, inner, from_near, from_far, weights, src, dst, valid, out):
    w = [weights[layer, i] for i in range(6)]
    odd = place[1] % 2 == 1
    row_count = rows_ref.shape[0]
    blocks = row_count // GH
    width = src.shape[1] // blocks
    near, far = from_near[...], from_far[...]
    before = jnp.where(odd, near, far)
    after = jnp.where(odd, far, near)
    ends = [
        (0, before, rows_ref[0 : 2 * GH, :], rows_ref[0:GH, :]),
        (
            blocks - 1,
            rows_ref[row_count - 2 * GH :, :],
            after,
            rows_ref[row_count - GH :, :],
        ),
    ]
    out[GH : row_count - GH, :] = inner[GH : row_count - GH, :]
    sums, own = [], []
    for b, lower, upper, rows in ends:
        line = jnp.concatenate([lower, upper], axis=0)
        source = dot(w[0] * BF(0.5), line, (((0,), (1,)), ((), ()))).astype(BF)
        target = dot(w[1] * BF(0.5), rows, (((0,), (1,)), ((), ()))).astype(BF)
        from_row, to_row = local_edges(b, row_count, src, dst, valid, width)
        sums.append(edge_sum(source, target, from_row, to_row))
        own.append(rows)
    both, last = node_weights(w)
    new = node_update(
        jnp.concatenate(own, axis=0), jnp.concatenate(sums, axis=0), both, last
    )
    out[0:GH, :] = new[:GH]
    out[row_count - GH :, :] = new[GH:]


def ends_kernel(layer, place, rows_ref, inner, from_near, from_far, weights, src, dst, valid, out):
    end_rows(layer, place, rows_ref, inner, from_near, from_far, weights, src, dst, valid, out)


def ends_pick_kernel(
    layer, place, rows_ref, inner, from_near, from_far, weights, src, dst, valid, lists, out, near, far
):
    end_rows(layer, place, rows_ref, inner, from_near, from_far, weights, src, dst, valid, out)
    pick_both(out, lists, place[1] % 2 == 1, near, far)


def ends_pool_kernel(
    layer,
    place,
    rows_ref,
    inner,
    from_near,
    from_far,
    weights,
    src,
    dst,
    valid,
    cluster,
    slot_pick,
    facts,
    out,
    parcel,
):
    end_rows(layer, place, rows_ref, inner, from_near, from_far, weights, src, dst, valid, out)
    member = rows_hot(cluster[...], 128)
    partial = dot(member, out[...]).astype(BF)
    parcel[...] = dot(slot_pick[...], jnp.concatenate([partial, facts[...]], axis=0)).astype(BF)


def prepare_kernel(cluster, owner, coarse_row, ghosts, slot_pick, facts, slot_of):
    member = rows_hot(cluster[...], 128)
    counts = jnp.sum(member.astype(F32), axis=1, keepdims=True)
    owner_row = owner[...].astype(F32)
    by_row, by_lane = column(owner_row), jnp.broadcast_to(owner_row, (128, 128))
    sub, lane = iota((128, 128), 0), iota((128, 128), 1)
    same = by_row == by_lane
    place_col = jnp.sum(jnp.where(same & (lane < sub), 1.0, 0.0), axis=1, keepdims=True)
    place_row = jnp.sum(jnp.where(same & (sub < lane), 1.0, 0.0), axis=0, keepdims=True)
    slot_row = owner_row * CAP + place_row
    slot_col = by_row * CAP + place_col
    owners = slot_pick.shape[0] // SLOTS
    slot_of[...] = hot(
        jnp.concatenate([slot_col] * (CAP * owners // 128), axis=1)
        == iota((128, CAP * owners), 1, F32)
    )
    row = iota((owners * SLOTS, 128), 0)
    to, at = row // SLOTS, row % SLOTS
    label = jnp.where(
        at < CAP,
        CAP * to + at,
        jnp.where(
            at < 2 * CAP,
            CAP * (to - 1) + at - CAP,
            jnp.where(at < 3 * CAP, CAP * (to + 1) + at - 2 * CAP, -1),
        ),
    )
    slot_pick[:, 0:128] = hot(label.astype(F32) == slot_row)
    fact = jnp.where(
        at == 3 * CAP,
        to,
        jnp.where(
            at == 3 * CAP + 1,
            to - 1,
            jnp.where(at == 3 * CAP + 2, to + 1, jnp.where(at == 3 * CAP + 3, 127, -1)),
        ),
    )
    slot_pick[:, 128:256] = hot(fact == iota(fact.shape, 1))
    high = jnp.floor(counts / 16.0)
    low = counts - 16.0 * high
    lanes = lane.astype(F32)
    values = (
        jnp.where(lanes == place_col, column(coarse_row[...]), 0.0)
        + jnp.where(lanes == place_col + CAP, high, 0.0)
        + jnp.where(lanes == place_col + 2 * CAP, low, 0.0)
    ).astype(BF)
    meta = dot(hot(by_lane == sub.astype(F32)), values)
    listed = jnp.concatenate(
        [ghosts[...].astype(F32), jnp.zeros((1, 128 - ghosts.shape[1]), F32)], axis=1
    )
    facts[...] = jnp.where(sub == 127, listed, meta).astype(BF)


def received_kernel(place, got, part, back):
    total = got.shape[0]
    owners = total // SLOTS
    here = place[0]
    wide = iota((3 * owners, total), 1)
    pick = iota((3 * owners, total), 0)
    metas = dot(
        hot(wide == SLOTS * (pick % owners) + 3 * CAP + pick // owners), got[...]
    ).astype(BF)
    spread = hot((wide // SLOTS == pick % owners) & (wide % SLOTS // CAP == pick // owners))
    facts = dot(metas, spread, TN)[0:16]
    lane = iota((1, total), 1)
    turn = iota((16, total), 0) - iota((16, total), 1) % CAP

    def fact(number):
        return jnp.sum(jnp.where(turn == CAP * number, facts, 0.0), axis=0, keepdims=True)

    group = lane % SLOTS // CAP
    key = jnp.where(group < 3, fact(0) + (128 * group).astype(F32), -1.0)
    below = got[pl.ds(pl.multiple_of(jnp.maximum(here - 1, 0) * SLOTS, SLOTS), SLOTS), :]
    above = got[pl.ds(pl.multiple_of(jnp.minimum(here + 1, owners - 1) * SLOTS, SLOTS), SLOTS), :]
    below = column(below.astype(F32)[SLOTS - 1 : SLOTS, :])[16:32]
    above = column(above.astype(F32)[SLOTS - 1 : SLOTS, :])[0:16]
    label = jnp.concatenate(
        [
            iota((128, 128), 0, F32),
            jnp.where(here > 0, below + 128.0, -7.0),
            jnp.where(here < owners - 1, above + 256.0, -7.0),
            jnp.full((96, 128), -7.0, F32),
        ],
        axis=0,
    )
    label = jnp.concatenate([label] * (total // 128), axis=1)
    table = hot(label == key)
    part[0:160, :] = dot(table[0:160], got[...]).astype(BF)
    counted = dot(
        jnp.concatenate([fact(1), fact(2), jnp.zeros((6, total), F32)], axis=0).astype(BF),
        table,
        NT,
    )
    count = counted[0:1] * 16.0 + counted[1:2]
    third = jnp.floor(count / 65536.0)
    second = jnp.floor((count - 65536.0 * third) / 256.0)
    first = count - 65536.0 * third - 256.0 * second
    digits = [first, second, third]
    part[160:176, :] = jnp.concatenate(
        [d[:, 0:128] for d in digits]
        + [d[:, 128:256] for d in digits]
        + [jnp.zeros((10, 128), F32)],
        axis=0,
    ).astype(BF)
    slot = iota((CAP * owners, owners), 0)
    ids = dot(hot(slot // CAP == iota((CAP * owners, owners), 1)), metas[0:owners])
    lanes = iota((CAP * owners, 128), 1)
    turns = iota((CAP * owners, 128), 0) % CAP
    named = jnp.sum(jnp.where(lanes == turns, ids, 0.0), axis=1, keepdims=True)
    back[...] = hot(lanes.astype(F32) == named)


def coarse_kernel(layer, own, other1, other2, other3, back, weights, src, dst, out, reply):
    w = [weights[layer, i] for i in range(6)]
    whole = (own[...].astype(F32) + other1[...].astype(F32)) + (
        other2[...].astype(F32) + other3[...].astype(F32)
    )

    def counts(first):
        row = (
            whole[first : first + 1]
            + 256.0 * whole[first + 1 : first + 2]
            + 65536.0 * whole[first + 2 : first + 3]
        )
        return jnp.maximum(column(row), 1.0)

    rows = (whole[0:128] / counts(160)).astype(BF)
    ghosts = (whole[128:160] / counts(163)[0:32]).astype(BF)
    table = jnp.concatenate([rows, ghosts], axis=0)
    source = dot(w[0] * BF(0.5), table, (((0,), (1,)), ((), ()))).astype(BF)
    target = dot(w[1] * BF(0.5), rows, (((0,), (1,)), ((), ()))).astype(BF)
    from_hot = rows_hot(src[...], 160)
    to_hot = rows_hot(dst[...], 128)
    half = dot(source, from_hot) + dot(target, to_hot)
    sums = dot(to_hot, half_silu(half).astype(BF), NT).astype(BF)
    new = node_update(rows, sums, *node_weights(w))
    out[...] = new
    reply[...] = dot(back[...], new).astype(BF)


def lift_kernel(place, rows_ref, cluster, slot_of, reply, lists, out, near, far):
    row_count = rows_ref.shape[0]
    by_cluster = dot(slot_of[...], reply[...]).astype(BF)
    lanes = iota((128, 128), 1, F32)
    for first in range(0, row_count, 128):
        member = hot(column(cluster[:, first : first + 128]) == lanes)
        at = pl.ds(first, 128)
        out[at, :] = (rows_ref[at, :].astype(F32) + dot(member, by_cluster)).astype(BF)
    pick_both(out, lists, place[1] % 2 == 1, near, far)


def run(kernel, outs, args, scalars=0, layer=None, scratch=(), flops=0, name=None):
    specs = []
    for i, arg in enumerate(args):
        if i < scalars:
            specs.append(pl.BlockSpec(memory_space=pltpu.SMEM))
        else:
            specs.append(pl.BlockSpec(memory_space=pltpu.VMEM))
    return pl.pallas_call(
        kernel if layer is None else functools.partial(kernel, layer),
        out_shape=[jax.ShapeDtypeStruct(shape, BF) for shape in outs],
        in_specs=specs,
        out_specs=[pl.BlockSpec(memory_space=pltpu.VMEM) for _ in outs],
        scratch_shapes=[pltpu.VMEM(shape, BF) for shape in scratch],
        compiler_params=pltpu.CompilerParams(vmem_limit_bytes=VMEM_LIMIT),
        cost_estimate=pl.CostEstimate(flops=flops, bytes_accessed=1 << 20, transcendentals=0),
        name=name,
    )(*args)


def on_device(
    nodes,
    weights,
    edge_src,
    edge_dst,
    edge_valid,
    ghost_list,
    cluster_of,
    owner,
    coarse_row,
    coarse_src,
    coarse_dst,
    coarse_ghosts,
):
    count, width = nodes.shape
    doms, subs = lax.axis_size("dom"), lax.axis_size("sub")
    place = jnp.stack([lax.axis_index("dom"), lax.axis_index("sub")]).astype(I32)
    lists = ghost_list[0]
    owner = owner.reshape(1, -1)
    coarse_lists = coarse_ghosts.reshape(1, -1)
    edges = (edge_src, edge_dst, edge_valid)
    ghost = (GH, width)
    chain = doms * subs
    near_pairs = [(i, i ^ 1) for i in range(chain)]
    far_pairs = [(i, i + 1 if i % 2 else i - 1) for i in range(1, chain - 1)]

    def swap(near, far):
        from_far = lax.ppermute(far, ("dom", "sub"), far_pairs)
        from_near = lax.ppermute(near, ("dom", "sub"), near_pairs)
        return from_near, from_far

    def inner(states, layer):
        return run(
            inner_kernel,
            [states.shape],
            (states, weights) + edges,
            layer=layer,
            scratch=[(width, count), (width, count), (count, width)],
            flops=5 * 10**9,
            name="inner",
        )[0]

    near, far = run(pick_kernel, [ghost, ghost], (place, nodes, lists), scalars=1, name="pick")
    ghosts = swap(near, far)
    slot_pick, facts, slot_of = run(
        prepare_kernel,
        [(doms * SLOTS, 256), (128, 128), (128, CAP * doms)],
        (cluster_of, owner, coarse_row, coarse_lists),
        flops=10**8,
        name="prepare",
    )
    middle = inner(nodes, 0)
    first, near, far = run(
        ends_pick_kernel,
        [nodes.shape, ghost, ghost],
        (place, nodes, middle) + ghosts + (weights,) + edges + (lists,),
        scalars=1,
        layer=0,
        flops=10**9,
        name="ends_pick",
    )
    ghosts = swap(near, far)
    middle = inner(first, 1)
    second, parcel = run(
        ends_pool_kernel,
        [nodes.shape, (doms * SLOTS, width)],
        (place, first, middle) + ghosts + (weights,) + edges + (cluster_of, slot_pick, facts),
        scalars=1,
        layer=1,
        flops=10**9,
        name="ends_pool",
    )
    got = lax.all_to_all(
        parcel.reshape(doms, SLOTS, width), "dom", split_axis=0, concat_axis=0, tiled=True
    ).reshape(doms * SLOTS, width)
    part, back = run(
        received_kernel,
        [(176, width), (doms * CAP, width)],
        (place, got),
        scalars=1,
        flops=10**8,
        name="received",
    )
    others = [lax.ppermute(part, "sub", [(i, i ^ k) for i in range(subs)]) for k in (1, 2, 3)]
    coarse, reply = run(
        coarse_kernel,
        [(128, width), (doms * CAP, width)],
        (part, *others, back, weights, coarse_src, coarse_dst),
        layer=2,
        flops=10**9,
        name="coarse",
    )
    reply = lax.all_to_all(
        reply.reshape(doms, CAP, width), "dom", split_axis=0, concat_axis=0, tiled=True
    ).reshape(doms * CAP, width)
    lifted, near, far = run(
        lift_kernel,
        [nodes.shape, ghost, ghost],
        (place, second, cluster_of, slot_of, reply, lists),
        scalars=1,
        flops=10**9,
        name="lift",
    )
    ghosts = swap(near, far)
    middle = inner(lifted, 3)
    (last,) = run(
        ends_kernel,
        [nodes.shape],
        (place, lifted, middle) + ghosts + (weights,) + edges,
        scalars=1,
        layer=3,
        flops=10**9,
        name="ends",
    )
    return (last, coarse)


def solution(mesh):
    placed = (
        P(("dom", "sub"), None),
        P(),
        P(("dom", "sub"), None),
        P(("dom", "sub"), None),
        P(("dom", "sub"), None),
        P(("dom", "sub"), None, None),
        P(("dom", "sub"), None),
        P(("dom", "sub"), None, None),
        P(("dom", "sub"), None),
        P("dom", None),
        P("dom", None),
        P("dom", None, None),
    )
    return jax.shard_map(
        on_device,
        mesh=mesh,
        in_specs=placed,
        out_specs=(P(("dom", "sub"), None), P("dom", None)),
        check_vma=False,
    )
```

time: 244 us -> 103 us (0.42)
  matrix products: 83.3 us -> 0 us
  starting transfers between devices: 62.1 us -> 20.7 us
  Pallas kernels: 0 us -> 29.1 us
  waiting for transfers between devices: 29.7 us -> 4.2 us
  other arithmetic: 11.1 us -> 0.08 us
  blocking collectives: 49.8 us -> 43.9 us
    dot_general x38 -> x0, matrix products: 83.3 us -> none  [the longest x3 25.4 us: node_update(): jnp.einsum('beh,hk->bek', activated, layer_weights[2], preferred_element_...]
    all_to_all x3 -> x0, starting transfers between devices: 29.4 us -> none  [the longest x1 14.3 us: on_device(): lax.all_to_all(send_counts.astype(jnp.bfloat16), 'dom', split_axis=0, con...]
    pallas_call x0 -> x11, Pallas kernels: none -> 29.1 us  [run(): pl.pallas_call(kernel if layer is None else functools.partial(kernel, lay...]
    all_to_all x3 -> x0, waiting for transfers between devices: 27.6 us -> none  [the longest x1 12.3 us: on_device(): lax.all_to_all(send_rows.astype(jnp.bfloat16), 'dom', split_axis=0, conca...]
    psum x1 -> x0, blocking collectives: 20.2 us -> none  [on_device(): lax.psum(local_sums.astype(jnp.bfloat16), 'sub').astype(jnp.float32)]
    all_to_all x1 -> x2, blocking collectives: 29.6 us -> 43.9 us  [the longest x1 26.9 us: on_device(): lax.all_to_all(parcel.reshape(doms, SLOTS, width), 'dom', split_axis=0, c...]
    ppermute x8 -> x9, starting transfers between devices: 32.7 us -> 20.7 us  [the longest x3 11.9 us: swap(): from_far = lax.ppermute(far, ('dom', 'sub'), far_pairs)]
    unnamed x4 -> x0, other arithmetic: 3.24 us -> none
  transfers between devices with their start and end apart: 11 -> 9, of which waited for: 4 -> 2; matrix products, arithmetic and copies ran while one was open for 6% -> 0% of each run, Pallas kernels for 0% -> 16%
where the time goes in v1:
time: 103 us; the launch traced here: 102 us
  blocking collectives  43.9 us (43%)
  Pallas kernels  29.1 us (28%)
  starting transfers between devices  20.7 us (20%)
  waiting for transfers between devices  4.2 us (4%)
  local copies, waits for them, and re-layouts  3.64 us (4%)
    pallas_call x11, Pallas kernels, run(): pl.pallas_call(kernel if layer is None else functools.partial(kernel, lay...  29.1 us
    all_to_all x1, blocking collectives, on_device(): lax.all_to_all(parcel.reshape(doms, SLOTS, width), 'dom', split_axis=0, c...  26.9 us
    all_to_all x1, blocking collectives, on_device(): lax.all_to_all(reply.reshape(doms, CAP, width), 'dom', split_axis=0, conc...  17 us
    ppermute x3, starting transfers between devices, swap(): from_far = lax.ppermute(far, ('dom', 'sub'), far_pairs)  11.9 us
    ppermute x3, starting transfers between devices, swap(): from_near = lax.ppermute(near, ('dom', 'sub'), near_pairs)  4.72 us
    ppermute x3, waiting for transfers between devices, on_device(): lax.ppermute(part, 'sub', [(i, i ^ k) for i in range(subs)])  4.19 us
    ppermute x3, starting transfers between devices, on_device(): lax.ppermute(part, 'sub', [(i, i ^ k) for i in range(subs)])  4.01 us
    unnamed x28, local copies, waits for them, and re-layouts  3.55 us
  transfers between devices with their start and end apart: 9, of which 2 were waited for; matrix products, arithmetic and copies ran while one was open for 0% of the time, Pallas kernels for 16%

profile of v1, /device:TPU:1, one launch (start us, length us, event | category | flops | bytes accessed | tf_op | source)
XLA Modules:
  0.0 102.4 jit_solution(6197207877148087328)
XLA Ops:
  1.4 1.0 %copy-done = bf16[2048,128]{1,0:T(8,128)(2,1)S(1)} copy-done((bf16[2048,128]{1,0:T(8,128)(2,1)S(1)}, bf16[2048,128]{1,0:T(8,128)(2,1)}, u32[]{:S(2)}) %copy-start) | copy-done | bytes 524312
  2.4 1.1 %pick.1 = (bf16[128,128]{1,0:T(8,128)(2,1)S(1)}, bf16[128,128]{1,0:T(8,128)(2,1)S(1)}) custom-call(s32[2]{0:T(128)S(1)} %pad_add_fusion.place, bf16[2048,128]{1,0:T(8,128)(2,1)S(1)} %copy-done, s32[2,128]{1,0:T(2,128)S(1)} %bitcast.12), custom_call_target="tpu_custom_call" | custom-call | bytes 1048576 | tf_op jit(solution)/shard_map/pick/pallas_call | solution.py:348
  3.5 2.6 %collective-permute-start = (bf16[128,128]{1,0:T(8,128)(2,1)S(1)}, bf16[128,128]{1,0:T(8,128)(2,1)S(1)}, u32[]{:S(2)}, u32[]{:S(2)}) collective-permute-start(bf16[128,128]{1,0:T(8,128)(2,1)S(1)} %get-tuple-element.19), channel_id=1, source_target_pairs={{0,1},{1,0},{2,3},{3,2},{4,5},{5,4},{6,7},{7,6},{8,9},{9,8},{10,11... | collective-permute-start | bytes 98312 | tf_op jit(solution)/shard_map/ppermute | solution.py:388
  6.1 5.4 %collective-permute-start.1 = (bf16[128,128]{1,0:T(8,128)(2,1)S(1)}, bf16[128,128]{1,0:T(8,128)(2,1)S(1)}, u32[]{:S(2)}, u32[]{:S(2)}) collective-permute-start(bf16[128,128]{1,0:T(8,128)(2,1)S(1)} %get-tuple-element.20), channel_id=1, source_target_pairs={{1,2},{2,1},{3,4},{4,3},{5,6},{6,5},{7,8},{8,7},{9,10},{10,9},{11,... | collective-permute-start | bytes 98312 | tf_op jit(solution)/shard_map/ppermute | solution.py:387
  11.5 1.1 %copy-done.3 = bf16[4,6,128,128]{3,2,1,0:T(8,128)(2,1)S(1)} copy-done((bf16[4,6,128,128]{3,2,1,0:T(8,128)(2,1)S(1)}, bf16[4,6,128,128]{3,2,1,0:T(8,128)(2,1)}, u32[]{:S(2)}) %copy-start.3) | copy-done | bytes 786456
  12.7 5.1 %inner.3 = bf16[2048,128]{1,0:T(8,128)(2,1)S(1)} custom-call(bf16[2048,128]{1,0:T(8,128)(2,1)S(1)} %copy-done, bf16[4,6,128,128]{3,2,1,0:T(8,128)(2,1)S(1)} %copy-done.3, s32[1,12288]{1,0:T(1,128)S(1)} %copy-done.5, s32[1,12288]{1,0:T(1,128)S(1)} %copy-done.6, s32[1,12288]{1,0:T(1,128)S(1)} %copy-done.7), custom_call_target="tpu_custom_call" | custom-call | flops 5000000000 | bytes 1048576 | tf_op jit(solution)/shard_map/inner/pallas_call | solution.py:348
  18.5 0.8 prepare.1
  19.4 2.3 %ends_pick.1 = (bf16[2048,128]{1,0:T(8,128)(2,1)S(1)}, bf16[128,128]{1,0:T(8,128)(2,1)S(1)}, bf16[128,128]{1,0:T(8,128)(2,1)S(1)}) custom-call(s32[2]{0:T(128)S(1)} %pad_add_fusion.place, bf16[2048,128]{1,0:T(8,128)(2,1)S(1)} %copy-done.1, bf16[2048,128]{1,0:T(8,128)(2,1)S(1)} %inner.3, bf16[128,128]{1,0:T(8,128)(2,1)S(1)} %collective-permute-done.from_near, ...), custom_call_target="tpu_custom_call" | custom-call | flops 1000000000 | bytes 1048576 | tf_op jit(solution)/shard_map/ends_pick/pallas_call | solution.py:348
  21.8 4.0 %collective-permute-start.3 = (bf16[128,128]{1,0:T(8,128)(2,1)S(1)}, bf16[128,128]{1,0:T(8,128)(2,1)S(1)}, u32[]{:S(2)}, u32[]{:S(2)}) collective-permute-start(bf16[128,128]{1,0:T(8,128)(2,1)S(1)} %get-tuple-element.23), channel_id=1, source_target_pairs={{1,2},{2,1},{3,4},{4,3},{5,6},{6,5},{7,8},{8,7},{9,10},{10,9},{11,... | collective-permute-start | bytes 98312 | tf_op jit(solution)/shard_map/ppermute | solution.py:387
  25.9 5.1 %inner.4 = bf16[2048,128]{1,0:T(8,128)(2,1)S(1)} custom-call(bf16[2048,128]{1,0:T(8,128)(2,1)S(1)} %get-tuple-element.21.rows_ref, bf16[4,6,128,128]{3,2,1,0:T(8,128)(2,1)S(1)} %copy-done.4, s32[1,12288]{1,0:T(1,128)S(1)} %copy-done.5, s32[1,12288]{1,0:T(1,128)S(1)} %copy-done.6, s32[1,12288]{1,0:T(1,128)S(1)} %copy-done.7), custom_call_target="tpu_custom_call" | custom-call | flops 5000000000 | bytes 1048576 | tf_op jit(solution)/shard_map/inner/pallas_call | solution.py:348
  31.0 2.4 %ends_pool.1 = (bf16[2048,128]{1,0:T(8,128)(2,1)S(1)}, bf16[1024,128]{1,0:T(8,128)(2,1)S(1)}) custom-call(s32[2]{0:T(128)S(1)} %pad_add_fusion.place, bf16[2048,128]{1,0:T(8,128)(2,1)S(1)} %get-tuple-element.21.rows_ref, bf16[2048,128]{1,0:T(8,128)(2,1)S(1)} %inner.4, bf16[128,128]{1,0:T(8,128)(2,1)S(1)} %collective-permute-done.2.from_near, ...), custom_call_target="tpu_custom_call" | custom-call | flops 1000000000 | bytes 1048576 | tf_op jit(solution)/shard_map/ends_pool/pallas_call | solution.py:348
  33.4 26.9 %all_to_all.10 = bf16[64,16,128]{2,1,0:T(8,128)(2,1)S(1)} all-to-all(bf16[64,16,128]{2,1,0:T(8,128)(2,1)S(1)} %bitcast.8), channel_id=1, replica_groups=mesh['dom'=64,'sub'=4] {'dom'}, dimensions={0} | all-to-all | bytes 524288 | tf_op jit(solution)/shard_map/all_to_all | solution.py:432
  60.3 1.4 %received.1 = (bf16[176,128]{1,0:T(8,128)(2,1)S(1)}, bf16[256,128]{1,0:T(8,128)(2,1)S(1)}) custom-call(s32[2]{0:T(128)S(1)} %pad_add_fusion.place, bf16[1024,128]{1,0:T(8,128)(2,1)S(1)} %bitcast.9), custom_call_target="tpu_custom_call" | custom-call | flops 100000000 | bytes 1048576 | tf_op jit(solution)/shard_map/received/pallas_call | solution.py:348
  61.7 2.1 %collective-permute-start.6 = (bf16[176,128]{1,0:T(8,128)(2,1)S(1)}, bf16[176,128]{1,0:T(8,128)(2,1)S(1)}, u32[]{:S(2)}, u32[]{:S(2)}) collective-permute-start(bf16[176,128]{1,0:T(8,128)(2,1)S(1)} %get-tuple-element.29.own), channel_id=1, source_target_pairs={{0,3},{1,2},{2,1},{3,0},{4,7},{5,6},{6,5},{7,4},{8,11},{9,10},{10,... | collective-permute-start | bytes 135176 | tf_op jit(solution)/shard_map/ppermute | solution.py:443
  63.9 1.9 %collective-permute-start.5 = (bf16[176,128]{1,0:T(8,128)(2,1)S(1)}, bf16[176,128]{1,0:T(8,128)(2,1)S(1)}, u32[]{:S(2)}, u32[]{:S(2)}) collective-permute-start(bf16[176,128]{1,0:T(8,128)(2,1)S(1)} %get-tuple-element.29.own), channel_id=1, source_target_pairs={{0,2},{1,3},{2,0},{3,1},{4,6},{5,7},{6,4},{7,5},{8,10},{9,11},{10,... | collective-permute-start | bytes 135176 | tf_op jit(solution)/shard_map/ppermute | solution.py:443
  65.7 0.8 collective-permute-done.6.other3
  66.5 3.4 %collective-permute-done.5.other2 = bf16[176,128]{1,0:T(8,128)(2,1)S(1)} collective-permute-done((bf16[176,128]{1,0:T(8,128)(2,1)S(1)}, bf16[176,128]{1,0:T(8,128)(2,1)S(1)}, u32[]{:S(2)}, u32[]{:S(2)}) %collective-permute-start.5) | collective-permute-done | bytes 45088 | tf_op jit(solution)/shard_map/ppermute | solution.py:443
  69.9 1.7 %coarse.1 = (bf16[128,128]{1,0:T(8,128)(2,1)}, bf16[256,128]{1,0:T(8,128)(2,1)S(1)}) custom-call(bf16[176,128]{1,0:T(8,128)(2,1)S(1)} %get-tuple-element.29.own, bf16[176,128]{1,0:T(8,128)(2,1)S(1)} %collective-permute-done.4.other1, bf16[176,128]{1,0:T(8,128)(2,1)S(1)} %collective-permute-done.5.other2, bf16[176,128]{1,0:T(8,128)(2,1)S(1)} %collective-permute-done.6.other3, ...), custom_call_target="tpu_custom_call" | custom-call | flops 1000000000 | bytes 1048576 | tf_op jit(solution)/shard_map/coarse/pallas_call | solution.py:348
  71.6 17.0 %all_to_all.11 = bf16[64,4,128]{2,1,0:T(4,128)(2,1)S(1)} all-to-all(bf16[64,4,128]{2,1,0:T(4,128)(2,1)S(1)} %bitcast.11), channel_id=1, replica_groups=mesh['dom'=64,'sub'=4] {'dom'}, dimensions={0} | all-to-all | bytes 131072 | tf_op jit(solution)/shard_map/all_to_all | solution.py:452
  88.6 1.4 %lift.1 = (bf16[2048,128]{1,0:T(8,128)(2,1)S(1)}, bf16[128,128]{1,0:T(8,128)(2,1)S(1)}, bf16[128,128]{1,0:T(8,128)(2,1)S(1)}) custom-call(s32[2]{0:T(128)S(1)} %pad_add_fusion.place, bf16[2048,128]{1,0:T(8,128)(2,1)S(1)} %get-tuple-element.26.rows_ref, s32[1,2048]{1,0:T(1,128)S(1)} %copy-done.8, bf16[128,256]{1,0:T(8,128)(2,1)S(1)} %get-tuple-element.27.slot_of, ...), custom_call_target="tpu_custom_call" | custom-call | flops 1000000000 | bytes 1048576 | tf_op jit(solution)/shard_map/lift/pallas_call | solution.py:348
  90.0 2.1 %collective-permute-start.7 = (bf16[128,128]{1,0:T(8,128)(2,1)S(1)}, bf16[128,128]{1,0:T(8,128)(2,1)S(1)}, u32[]{:S(2)}, u32[]{:S(2)}) collective-permute-start(bf16[128,128]{1,0:T(8,128)(2,1)S(1)} %get-tuple-element.33), channel_id=1, source_target_pairs={{0,1},{1,0},{2,3},{3,2},{4,5},{5,4},{6,7},{7,6},{8,9},{9,8},{10,11... | collective-permute-start | bytes 98312 | tf_op jit(solution)/shard_map/ppermute | solution.py:388
  92.0 2.5 %collective-permute-start.8 = (bf16[128,128]{1,0:T(8,128)(2,1)S(1)}, bf16[128,128]{1,0:T(8,128)(2,1)S(1)}, u32[]{:S(2)}, u32[]{:S(2)}) collective-permute-start(bf16[128,128]{1,0:T(8,128)(2,1)S(1)} %get-tuple-element.34), channel_id=1, source_target_pairs={{1,2},{2,1},{3,4},{4,3},{5,6},{6,5},{7,8},{8,7},{9,10},{10,9},{11,... | collective-permute-start | bytes 98312 | tf_op jit(solution)/shard_map/ppermute | solution.py:387
  94.6 5.1 %inner.5 = bf16[2048,128]{1,0:T(8,128)(2,1)S(1)} custom-call(bf16[2048,128]{1,0:T(8,128)(2,1)S(1)} %get-tuple-element.32.rows_ref, bf16[4,6,128,128]{3,2,1,0:T(8,128)(2,1)S(1)} %copy-done.4, s32[1,12288]{1,0:T(1,128)S(1)} %copy-done.5, s32[1,12288]{1,0:T(1,128)S(1)} %copy-done.6, s32[1,12288]{1,0:T(1,128)S(1)} %copy-done.7), custom_call_target="tpu_custom_call" | custom-call | flops 5000000000 | bytes 1048576 | tf_op jit(solution)/shard_map/inner/pallas_call | solution.py:348
  99.7 2.7 %ends.1 = bf16[2048,128]{1,0:T(8,128)(2,1)} custom-call(s32[2]{0:T(128)S(1)} %pad_add_fusion.place, bf16[2048,128]{1,0:T(8,128)(2,1)S(1)} %get-tuple-element.32.rows_ref, bf16[2048,128]{1,0:T(8,128)(2,1)S(1)} %inner.5, bf16[128,128]{1,0:T(8,128)(2,1)S(1)} %collective-permute-done.7.from_near, bf16[128,128]{1,0:T(8,128)(2,1)S(1)} %collective-permute-done.8.from_far, ...), custom_call_target="tpu_custom_call" | custom-call | flops 1000000000 | bytes 1048576 | tf_op jit(solution)/shard_map/ends/pallas_call | solution.py:348
  (37 shorter events, 1.7 us)
Async XLA Ops:
  0.7 0.7 copy-start.2
  1.4 1.0 %copy-start = (bf16[2048,128]{1,0:T(8,128)(2,1)S(1)}, bf16[2048,128]{1,0:T(8,128)(2,1)}, u32[]{:S(2)}) copy-start(bf16[2048,128]{1,0:T(8,128)(2,1)} %rows_ref.5) | copy-start | bytes 1572868
  2.4 9.1 %copy-start.5 = (s32[1,12288]{1,0:T(1,128)S(1)}, s32[1,12288]{1,0:T(1,128)}, u32[]{:S(2)}) copy-start(s32[1,12288]{1,0:T(1,128)} %src.13) | copy-start | bytes 147460
  2.4 9.1 %copy-start.6 = (s32[1,12288]{1,0:T(1,128)S(1)}, s32[1,12288]{1,0:T(1,128)}, u32[]{:S(2)}) copy-start(s32[1,12288]{1,0:T(1,128)} %dst.13) | copy-start | bytes 147460
  2.4 9.1 %copy-start.7 = (s32[1,12288]{1,0:T(1,128)S(1)}, s32[1,12288]{1,0:T(1,128)}, u32[]{:S(2)}) copy-start(s32[1,12288]{1,0:T(1,128)} %valid.11) | copy-start | bytes 147460
  3.5 15.8 %collective-permute-start = (bf16[128,128]{1,0:T(8,128)(2,1)S(1)}, bf16[128,128]{1,0:T(8,128)(2,1)S(1)}, u32[]{:S(2)}, u32[]{:S(2)}) collective-permute-start(bf16[128,128]{1,0:T(8,128)(2,1)S(1)} %get-tuple-element.19), channel_id=1, source_target_pairs={{0,1},{1,0},{2,3},{3,2},{4,5},{5,4},{6,7},{7,6},{8,9},{9,8},{10,11... | collective-permute-start | bytes 98312 | tf_op jit(solution)/shard_map/ppermute | solution.py:388
  6.1 13.3 %copy-start.1 = (bf16[2048,128]{1,0:T(8,128)(2,1)S(1)}, bf16[2048,128]{1,0:T(8,128)(2,1)}, u32[]{:S(2)}) copy-start(bf16[2048,128]{1,0:T(8,128)(2,1)} %rows_ref.5) | copy-start | bytes 1572868
  6.1 13.3 %collective-permute-start.1 = (bf16[128,128]{1,0:T(8,128)(2,1)S(1)}, bf16[128,128]{1,0:T(8,128)(2,1)S(1)}, u32[]{:S(2)}, u32[]{:S(2)}) collective-permute-start(bf16[128,128]{1,0:T(8,128)(2,1)S(1)} %get-tuple-element.20), channel_id=1, source_target_pairs={{1,2},{2,1},{3,4},{4,3},{5,6},{6,5},{7,8},{8,7},{9,10},{10,9},{11,... | collective-permute-start | bytes 98312 | tf_op jit(solution)/shard_map/ppermute | solution.py:387
  11.5 1.1 %copy-start.3 = (bf16[4,6,128,128]{3,2,1,0:T(8,128)(2,1)S(1)}, bf16[4,6,128,128]{3,2,1,0:T(8,128)(2,1)}, u32[]{:S(2)}) copy-start(bf16[4,6,128,128]{3,2,1,0:T(8,128)(2,1)} %weights.13) | copy-start | bytes 2359300
  12.7 5.1 %copy-start.13 = (s32[1,2,16]{2,1,0:T(2,128)S(1)}, s32[1,2,16]{2,1,0:T(2,128)}, u32[]{:S(2)}) copy-start(s32[1,2,16]{2,1,0:T(2,128)} %param.23) | copy-start | bytes 388
  12.7 5.2 %copy-start.8 = (s32[1,2048]{1,0:T(1,128)S(1)}, s32[1,2048]{1,0:T(1,128)}, u32[]{:S(2)}) copy-start(s32[1,2048]{1,0:T(1,128)} %cluster.5) | copy-start | bytes 24580
  12.7 6.7 %copy-start.4 = (bf16[4,6,128,128]{3,2,1,0:T(8,128)(2,1)S(1)}, bf16[4,6,128,128]{3,2,1,0:T(8,128)(2,1)}, u32[]{:S(2)}) copy-start(bf16[4,6,128,128]{3,2,1,0:T(8,128)(2,1)} %weights.13) | copy-start | bytes 2359300
  17.9 0.7 copy-start.11
  17.9 0.7 copy-start.12
  21.7 9.3 %collective-permute-start.2 = (bf16[128,128]{1,0:T(8,128)(2,1)S(1)}, bf16[128,128]{1,0:T(8,128)(2,1)S(1)}, u32[]{:S(2)}, u32[]{:S(2)}) collective-permute-start(bf16[128,128]{1,0:T(8,128)(2,1)S(1)} %get-tuple-element.22), channel_id=1, source_target_pairs={{0,1},{1,0},{2,3},{3,2},{4,5},{5,4},{6,7},{7,6},{8,9},{9,8},{10,11... | collective-permute-start | bytes 98312 | tf_op jit(solution)/shard_map/ppermute | solution.py:388
  21.8 9.2 %collective-permute-start.3 = (bf16[128,128]{1,0:T(8,128)(2,1)S(1)}, bf16[128,128]{1,0:T(8,128)(2,1)S(1)}, u32[]{:S(2)}, u32[]{:S(2)}) collective-permute-start(bf16[128,128]{1,0:T(8,128)(2,1)S(1)} %get-tuple-element.23), channel_id=1, source_target_pairs={{1,2},{2,1},{3,4},{4,3},{5,6},{6,5},{7,8},{8,7},{9,10},{10,9},{11,... | collective-permute-start | bytes 98312 | tf_op jit(solution)/shard_map/ppermute | solution.py:387
  33.4 36.5 %copy-start.10 = (s32[1,768]{1,0:T(1,128)S(1)}, s32[1,768]{1,0:T(1,128)}, u32[]{:S(2)}) copy-start(s32[1,768]{1,0:T(1,128)} %dst.11) | copy-start | bytes 9220
  61.7 8.2 %copy-start.9 = (s32[1,768]{1,0:T(1,128)S(1)}, s32[1,768]{1,0:T(1,128)}, u32[]{:S(2)}) copy-start(s32[1,768]{1,0:T(1,128)} %src.11) | copy-start | bytes 9220
  61.7 4.8 %collective-permute-start.6 = (bf16[176,128]{1,0:T(8,128)(2,1)S(1)}, bf16[176,128]{1,0:T(8,128)(2,1)S(1)}, u32[]{:S(2)}, u32[]{:S(2)}) collective-permute-start(bf16[176,128]{1,0:T(8,128)(2,1)S(1)} %get-tuple-element.29.own), channel_id=1, source_target_pairs={{0,3},{1,2},{2,1},{3,0},{4,7},{5,6},{6,5},{7,4},{8,11},{9,10},{10,... | collective-permute-start | bytes 135176 | tf_op jit(solution)/shard_map/ppermute | solution.py:443
  63.9 6.1 %collective-permute-start.5 = (bf16[176,128]{1,0:T(8,128)(2,1)S(1)}, bf16[176,128]{1,0:T(8,128)(2,1)S(1)}, u32[]{:S(2)}, u32[]{:S(2)}) collective-permute-start(bf16[176,128]{1,0:T(8,128)(2,1)S(1)} %get-tuple-element.29.own), channel_id=1, source_target_pairs={{0,2},{1,3},{2,0},{3,1},{4,6},{5,7},{6,4},{7,5},{8,10},{9,11},{10,... | collective-permute-start | bytes 135176 | tf_op jit(solution)/shard_map/ppermute | solution.py:443
  65.7 4.2 %collective-permute-start.4 = (bf16[176,128]{1,0:T(8,128)(2,1)S(1)}, bf16[176,128]{1,0:T(8,128)(2,1)S(1)}, u32[]{:S(2)}, u32[]{:S(2)}) collective-permute-start(bf16[176,128]{1,0:T(8,128)(2,1)S(1)} %get-tuple-element.29.own), channel_id=1, source_target_pairs={{0,1},{1,0},{2,3},{3,2},{4,5},{5,4},{6,7},{7,6},{8,9},{9,8},{10,11... | collective-permute-start | bytes 135176 | tf_op jit(solution)/shard_map/ppermute | solution.py:443
  90.0 9.7 %collective-permute-start.7 = (bf16[128,128]{1,0:T(8,128)(2,1)S(1)}, bf16[128,128]{1,0:T(8,128)(2,1)S(1)}, u32[]{:S(2)}, u32[]{:S(2)}) collective-permute-start(bf16[128,128]{1,0:T(8,128)(2,1)S(1)} %get-tuple-element.33), channel_id=1, source_target_pairs={{0,1},{1,0},{2,3},{3,2},{4,5},{5,4},{6,7},{7,6},{8,9},{9,8},{10,11... | collective-permute-start | bytes 98312 | tf_op jit(solution)/shard_map/ppermute | solution.py:388
  92.0 7.7 %collective-permute-start.8 = (bf16[128,128]{1,0:T(8,128)(2,1)S(1)}, bf16[128,128]{1,0:T(8,128)(2,1)S(1)}, u32[]{:S(2)}, u32[]{:S(2)}) collective-permute-start(bf16[128,128]{1,0:T(8,128)(2,1)S(1)} %get-tuple-element.34), channel_id=1, source_target_pairs={{1,2},{2,1},{3,4},{4,3},{5,6},{6,5},{7,8},{8,7},{9,10},{10,9},{11,... | collective-permute-start | bytes 98312 | tf_op jit(solution)/shard_map/ppermute | solution.py:387

commit v2 on v1

v2 whole, which is shorter than its diff:
```python
import functools

import jax
import jax.numpy as jnp
from jax import lax
from jax.experimental import pallas as pl
from jax.experimental.pallas import tpu as pltpu
from jax.sharding import PartitionSpec as P

BF = jnp.bfloat16
F32 = jnp.float32
I32 = jnp.int32
I16 = jnp.int16
NN = (((1,), (0,)), ((), ()))
NT = (((1,), (1,)), ((), ()))
TN = (((0,), (0,)), ((), ()))

GH = 128
CAP = 4
SLOTS = 16
VMEM_LIMIT = 28 << 20


def dot(left, right, dims=NN):
    return lax.dot_general(left, right, dims, preferred_element_type=F32)


def iota(shape, dim, dtype=I32):
    return lax.broadcasted_iota(I32, shape, dim).astype(dtype)


def hot(mask):
    return jnp.where(mask, 1.0, 0.0).astype(BF)


def column(row):
    return jnp.broadcast_to(row.astype(F32), (128, 128)).T


def half_silu(half):
    return half * (1.0 + jnp.tanh(half))


def rows_hot(index_row, count):
    table = lax.broadcasted_iota(I16, (count, index_row.shape[1]), 0)
    return jnp.where(table == index_row.astype(I16), BF(1), BF(0))


def edge_sum(source_t, target_t, from_hot, to_hot):
    table = jnp.concatenate([source_t, target_t], axis=1)
    half = dot(table, jnp.concatenate([from_hot, to_hot], axis=0))
    return dot(half_silu(half).astype(BF), to_hot, NT).astype(BF)


def layer_weights(w):
    first = jnp.concatenate([w[0].astype(F32).T, w[1].astype(F32).T], axis=0) * 0.5
    both = jnp.concatenate([w[3].astype(F32).T, dot(w[2], w[4]).T], axis=1) * 0.5
    last = w[5].astype(F32)
    last = last - jnp.mean(last, axis=1, keepdims=True)
    return first.astype(BF), both.astype(BF), last.T.astype(BF)


def node_update(rows_t, sums_t, both, last):
    half = dot(both, jnp.concatenate([rows_t, sums_t], axis=0))
    centred = dot(last, half_silu(half).astype(BF))
    spread = jnp.mean(centred * centred, axis=0, keepdims=True)
    return (rows_t.astype(F32) + centred * lax.rsqrt(spread + 1e-5)).astype(BF)


def local_edges(b, row_count, src, dst, valid, width):
    at = pl.ds(b * width, width)
    edge = src[:, at]
    line = jnp.where(
        edge < row_count, edge + GH, jnp.where(edge < row_count + GH, edge - row_count, edge)
    )
    to_row = jnp.where(valid[:, at] != 0, dst[:, at] - b * GH, -1)
    return rows_hot(line - b * GH, 3 * GH), rows_hot(to_row, GH)


def pick_both(rows_t, lists, odd, near, far):
    to_lower, to_upper = lists[0:1, :], lists[1:2, :]
    wanted = jnp.concatenate(
        [jnp.where(odd, to_lower, to_upper), jnp.where(odd, to_upper, to_lower)], axis=1
    )
    picked = dot(rows_t[...], rows_hot(wanted, rows_t.shape[1])).astype(BF)
    near[...] = picked[:, :GH]
    far[...] = picked[:, GH:]


def inner_kernel(layer, rows_t, weights, src, dst, valid, out, first, both, last, ends, sums):
    row_count = rows_t.shape[1]
    blocks = row_count // GH
    width = src.shape[1] // blocks
    first[...], both[...], last[...] = layer_weights([weights[layer, i] for i in range(6)])
    ends[...] = dot(first[...], rows_t[...]).astype(BF)
    for b in range(1, blocks - 1):
        at = slice(b * GH, (b + 1) * GH)
        sums[:, at] = edge_sum(
            ends[0:128, (b - 1) * GH : (b + 2) * GH],
            ends[128:256, at],
            *local_edges(b, row_count, src, dst, valid, width),
        )
    step = (row_count - 2 * GH) // 2
    for start in range(GH, row_count - GH, step):
        at = slice(start, start + step)
        out[:, at] = node_update(rows_t[:, at], sums[:, at], both[...], last[...])


def end_blocks(place, rows_t, from_near, from_far, first, both, last, src, dst, valid):
    odd = place[1] % 2 == 1
    row_count = rows_t.shape[1]
    blocks = row_count // GH
    width = src.shape[1] // blocks
    near, far = from_near[...], from_far[...]
    nothing = jnp.zeros_like(near)
    before = jnp.where(place[2] == 0, nothing, jnp.where(odd, near, far))
    after = jnp.where(place[3] == 0, nothing, jnp.where(odd, far, near))
    head, tail = rows_t[:, 0 : 2 * GH], rows_t[:, row_count - 2 * GH :]
    line = jnp.concatenate([before, head, tail, after], axis=1)
    ends = dot(first[...], line).astype(BF)
    sums = [
        edge_sum(
            ends[0:128, at : at + 3 * GH],
            ends[128:256, at + own : at + own + GH],
            *local_edges(b, row_count, src, dst, valid, width),
        )
        for b, at, own in ((0, 0, GH), (blocks - 1, 3 * GH, GH))
    ]
    own = jnp.concatenate([head[:, :GH], tail[:, GH:]], axis=1)
    return node_update(own, jnp.concatenate(sums, axis=1), both[...], last[...])


def whole_layer(inner, new, out):
    count = out.shape[1]
    out[:, GH : count - GH] = inner[:, GH : count - GH]
    out[:, 0:GH] = new[:, :GH]
    out[:, count - GH :] = new[:, GH:]


def ends_kernel(place, inner, *refs):
    out = refs[-1]
    new = end_blocks(place, *refs[:-1])
    count = out.shape[0]
    out[GH : count - GH, :] = inner[:, GH : count - GH].T
    out[0:GH, :] = new[:, :GH].T
    out[count - GH :, :] = new[:, GH:].T


def ends_pick_kernel(place, inner, *refs):
    lists, out, near, far = refs[-4:]
    whole_layer(inner, end_blocks(place, *refs[:-4]), out)
    pick_both(out, lists, place[1] % 2 == 1, near, far)


def ends_pool_kernel(place, inner, *refs):
    cluster, slot_pick, facts, out, parcel = refs[-5:]
    whole_layer(inner, end_blocks(place, *refs[:-5]), out)
    member = rows_hot(cluster[...], 128)
    partial = dot(out[...], member, NT).T.astype(BF)
    parcel[...] = dot(slot_pick[...], jnp.concatenate([partial, facts[...]], axis=0)).astype(BF)


def start_kernel(place, nodes, lists, facts, rows_t, near, far):
    rows_t[...] = nodes[...].T
    pick_both(rows_t, lists, place[1] % 2 == 1, near, far)


def prepare_kernel(cluster, owner, coarse_row, ghosts, slot_pick, facts, slot_of):
    member = rows_hot(cluster[...], 128)
    counts = jnp.sum(member.astype(F32), axis=1, keepdims=True)
    owner_row = owner[...].astype(F32)
    by_row, by_lane = column(owner_row), jnp.broadcast_to(owner_row, (128, 128))
    sub, lane = iota((128, 128), 0), iota((128, 128), 1)
    same = by_row == by_lane
    place_col = jnp.sum(jnp.where(same & (lane < sub), 1.0, 0.0), axis=1, keepdims=True)
    place_row = jnp.sum(jnp.where(same & (sub < lane), 1.0, 0.0), axis=0, keepdims=True)
    slot_row = owner_row * CAP + place_row
    owners = slot_pick.shape[0] // SLOTS
    slot_of[...] = hot(slot_row == iota((CAP * owners, 128), 0, F32))
    row = iota((owners * SLOTS, 128), 0)
    to, at = row // SLOTS, row % SLOTS
    label = jnp.where(
        at < CAP,
        CAP * to + at,
        jnp.where(
            at < 2 * CAP,
            CAP * (to - 1) + at - CAP,
            jnp.where(at < 3 * CAP, CAP * (to + 1) + at - 2 * CAP, -1),
        ),
    )
    slot_pick[:, 0:128] = hot(label.astype(F32) == slot_row)
    fact = jnp.where(
        at == 3 * CAP,
        to,
        jnp.where(
            at == 3 * CAP + 1,
            to - 1,
            jnp.where(at == 3 * CAP + 2, to + 1, jnp.where(at == 3 * CAP + 3, 127, -1)),
        ),
    )
    slot_pick[:, 128:256] = hot(fact == iota(fact.shape, 1))
    high = jnp.floor(counts / 16.0)
    low = counts - 16.0 * high
    lanes = lane.astype(F32)
    values = (
        jnp.where(lanes == place_col, column(coarse_row[...]), 0.0)
        + jnp.where(lanes == place_col + CAP, high, 0.0)
        + jnp.where(lanes == place_col + 2 * CAP, low, 0.0)
    ).astype(BF)
    meta = dot(hot(by_lane == sub.astype(F32)), values)
    each = ghosts.shape[2]
    listed = jnp.concatenate(
        [ghosts[0, 0:1], ghosts[0, 1:2], jnp.zeros((1, 128 - 2 * each), I32)], axis=1
    ).astype(F32)
    facts[...] = jnp.where(sub == 127, listed, meta).astype(BF)


def received_kernel(place, got, part, own_metas):
    total = got.shape[0]
    owners = total // SLOTS
    here = place[0]
    wide = iota((3 * owners, total), 1)
    pick = iota((3 * owners, total), 0)
    metas = dot(
        hot(wide == SLOTS * (pick % owners) + 3 * CAP + pick // owners), got[...]
    ).astype(BF)
    own_metas[...] = metas[0:owners]
    spread = hot((wide // SLOTS == pick % owners) & (wide % SLOTS // CAP == pick // owners))
    facts = dot(metas, spread, TN)[0:16]
    lane = iota((1, total), 1)
    turn = iota((16, total), 0) - iota((16, total), 1) % CAP

    def fact(number):
        return jnp.sum(jnp.where(turn == CAP * number, facts, 0.0), axis=0, keepdims=True)

    group = lane % SLOTS // CAP
    key = jnp.where(group < 3, fact(0) + (128 * group).astype(F32), -1.0)
    below = got[pl.ds(pl.multiple_of(jnp.maximum(here - 1, 0) * SLOTS, SLOTS), SLOTS), :]
    above = got[pl.ds(pl.multiple_of(jnp.minimum(here + 1, owners - 1) * SLOTS, SLOTS), SLOTS), :]
    below = column(below.astype(F32)[SLOTS - 1 : SLOTS, :])[16:32]
    above = column(above.astype(F32)[SLOTS - 1 : SLOTS, :])[0:16]
    label = jnp.concatenate(
        [
            iota((128, 128), 0, F32),
            jnp.where(here > 0, below + 128.0, -7.0),
            jnp.where(here < owners - 1, above + 256.0, -7.0),
            jnp.full((96, 128), -7.0, F32),
        ],
        axis=0,
    )
    label = jnp.concatenate([label] * (total // 128), axis=1)
    table = hot(label == key)
    part[0:160, :] = dot(table[0:160], got[...]).astype(BF)
    counted = dot(
        jnp.concatenate([fact(1), fact(2), jnp.zeros((6, total), F32)], axis=0).astype(BF),
        table,
        NT,
    )
    count = counted[0:1] * 16.0 + counted[1:2]
    third = jnp.floor(count / 65536.0)
    second = jnp.floor((count - 65536.0 * third) / 256.0)
    first = count - 65536.0 * third - 256.0 * second
    digits = [first, second, third]
    part[160:176, :] = jnp.concatenate(
        [d[:, 0:128] for d in digits]
        + [d[:, 128:256] for d in digits]
        + [jnp.zeros((10, 128), F32)],
        axis=0,
    ).astype(BF)


def ready_kernel(layer, own_metas, weights, src, dst, back, first, both, last, from_hot, to_hot):
    owners = own_metas.shape[0]
    slots = CAP * owners
    turn = iota((slots, owners), 0)
    ids = dot(hot(turn // CAP == iota((slots, owners), 1)), own_metas[...])
    lanes = iota((slots, 128), 1)
    turns = iota((slots, 128), 0) % CAP
    named = jnp.sum(jnp.where(lanes == turns, ids, 0.0), axis=1, keepdims=True)
    back[...] = hot(lanes.astype(F32) == named)
    first[...], both[...], last[...] = layer_weights([weights[layer, i] for i in range(6)])
    from_hot[...] = rows_hot(src[...], 160)
    to_hot[...] = rows_hot(dst[...], 128)


def coarse_kernel(own, other1, other2, other3, back, first, both, last, from_hot, to_hot, out, reply):
    whole = (own[...].astype(F32) + other1[...].astype(F32)) + (
        other2[...].astype(F32) + other3[...].astype(F32)
    )

    def counts(at):
        row = whole[at : at + 1] + 256.0 * whole[at + 1 : at + 2] + 65536.0 * whole[at + 2 : at + 3]
        return jnp.maximum(row, 1.0)

    rows_t = (whole[0:128].T / counts(160)).astype(BF)
    ghosts = jnp.concatenate([whole[128:160], jnp.zeros((96, 128), F32)], axis=0)
    ghosts_t = (ghosts.T / counts(163)).astype(BF)
    ends = dot(first[...], jnp.concatenate([rows_t, ghosts_t], axis=1)).astype(BF)
    half = dot(ends[0:128, 0:160], from_hot[...]) + dot(ends[128:256, 0:128], to_hot[...])
    sums = dot(half_silu(half).astype(BF), to_hot[...], NT).astype(BF)
    new = node_update(rows_t, sums, both[...], last[...]).T
    out[...] = new
    reply[...] = dot(back[...], new).astype(BF)


def lift_kernel(place, rows_t, cluster, slot_of, reply, lists, out, near, far):
    by_cluster = dot(reply[...], slot_of[...], TN).astype(BF)
    member = rows_hot(cluster[...], 128)
    out[...] = (rows_t[...].astype(F32) + dot(by_cluster, member)).astype(BF)
    pick_both(out, lists, place[1] % 2 == 1, near, far)


def run(kernel, outs, args, scalars=0, layer=None, scratch=(), flops=0, name=None):
    specs = []
    for i in range(len(args)):
        specs.append(pl.BlockSpec(memory_space=pltpu.SMEM if i < scalars else pltpu.VMEM))
    return pl.pallas_call(
        kernel if layer is None else functools.partial(kernel, layer),
        out_shape=[jax.ShapeDtypeStruct(shape, BF) for shape in outs],
        in_specs=specs,
        out_specs=[pl.BlockSpec(memory_space=pltpu.VMEM) for _ in outs],
        scratch_shapes=scratch,
        compiler_params=pltpu.CompilerParams(vmem_limit_bytes=VMEM_LIMIT),
        cost_estimate=pl.CostEstimate(flops=flops, bytes_accessed=1 << 20, transcendentals=0),
        name=name,
    )(*args)


def on_device(
    nodes,
    weights,
    edge_src,
    edge_dst,
    edge_valid,
    ghost_list,
    cluster_of,
    owner,
    coarse_row,
    coarse_src,
    coarse_dst,
    coarse_ghosts,
):
    count, width = nodes.shape
    doms, subs = lax.axis_size("dom"), lax.axis_size("sub")
    dom, sub = lax.axis_index("dom"), lax.axis_index("sub")
    chain = doms * subs
    index = dom * subs + sub
    place = jnp.stack([dom, sub, index, chain - 1 - index]).astype(I32)
    lists = ghost_list[0]
    edges = (edge_src, edge_dst, edge_valid)
    ghost = (width, GH)
    rows_t = (width, count)
    forms = [(2 * width, width), (width, 2 * width), (width, width)]
    near_pairs = [(i, i ^ 1) for i in range(chain)]
    far_pairs = [(i, (i + 1 if i % 2 else i - 1) % chain) for i in range(chain)]

    def swap(near, far):
        from_near = lax.ppermute(near, ("dom", "sub"), near_pairs)
        from_far = lax.ppermute(far, ("dom", "sub"), far_pairs)
        return from_near, from_far

    def inner(states, layer):
        out, *weights_now = run(
            inner_kernel,
            [rows_t] + forms,
            (states, weights) + edges,
            layer=layer,
            scratch=[pltpu.VMEM((2 * width, count), BF), pltpu.VMEM(rows_t, BF)],
            flops=4 * 10**9,
            name="inner",
        )
        return out, tuple(weights_now)

    slot_pick, facts, slot_of = run(
        prepare_kernel,
        [(doms * SLOTS, 256), (128, 128), (CAP * doms, 128)],
        (cluster_of, owner.reshape(1, -1), coarse_row, coarse_ghosts),
        flops=3 * 10**9,
        name="prepare",
    )
    states, near, far = run(
        start_kernel,
        [rows_t, ghost, ghost],
        (place, nodes, lists, facts),
        scalars=1,
        flops=10**9,
        name="start",
    )
    ghosts = swap(near, far)
    middle, now = inner(states, 0)
    states, near, far = run(
        ends_pick_kernel,
        [rows_t, ghost, ghost],
        (place, middle, states) + ghosts + now + edges + (lists,),
        scalars=1,
        flops=10**9,
        name="ends_pick",
    )
    ghosts = swap(near, far)
    middle, now = inner(states, 1)
    states, parcel = run(
        ends_pool_kernel,
        [rows_t, (doms * SLOTS, width)],
        (place, middle, states) + ghosts + now + edges + (cluster_of, slot_pick, facts),
        scalars=1,
        flops=10**9,
        name="ends_pool",
    )
    got = lax.all_to_all(
        parcel.reshape(doms, SLOTS, width), "dom", split_axis=0, concat_axis=0, tiled=True
    ).reshape(doms * SLOTS, width)
    part, own_metas = run(
        received_kernel,
        [(176, width), (doms, width)],
        (place, got),
        scalars=1,
        flops=10**9,
        name="received",
    )
    others = [lax.ppermute(part, "sub", [(i, i ^ k) for i in range(subs)]) for k in (1, 2, 3)]
    ready = run(
        ready_kernel,
        [(doms * CAP, width)] + forms + [(160, coarse_src.shape[1]), (128, coarse_src.shape[1])],
        (own_metas, weights, coarse_src, coarse_dst),
        layer=2,
        flops=10**9,
        name="ready",
    )
    coarse, reply = run(
        coarse_kernel,
        [(128, width), (doms * CAP, width)],
        (part, *others, *ready),
        flops=10**9,
        name="coarse",
    )
    reply = lax.all_to_all(
        reply.reshape(doms, CAP, width), "dom", split_axis=0, concat_axis=0, tiled=True
    ).reshape(doms * CAP, width)
    states, near, far = run(
        lift_kernel,
        [rows_t, ghost, ghost],
        (place, states, cluster_of, slot_of, reply, lists),
        scalars=1,
        flops=10**9,
        name="lift",
    )
    ghosts = swap(near, far)
    middle, now = inner(states, 3)
    (last,) = run(
        ends_kernel,
        [nodes.shape],
        (place, middle, states) + ghosts + now + edges,
        scalars=1,
        flops=10**9,
        name="ends",
    )
    return (last, coarse)


def solution(mesh):
    placed = (
        P(("dom", "sub"), None),
        P(),
        P(("dom", "sub"), None),
        P(("dom", "sub"), None),
        P(("dom", "sub"), None),
        P(("dom", "sub"), None, None),
        P(("dom", "sub"), None),
        P(("dom", "sub"), None, None),
        P(("dom", "sub"), None),
        P("dom", None),
        P("dom", None),
        P("dom", None, None),
    )
    return jax.shard_map(
        on_device,
        mesh=mesh,
        in_specs=placed,
        out_specs=(P(("dom", "sub"), None), P("dom", None)),
        check_vma=False,
    )
```

time: 103 us -> 96.1 us (0.933)
  Pallas kernels: 29.1 us -> 25 us
  blocking collectives: 43.9 us -> 47.4 us
  starting transfers between devices: 20.7 us -> 18 us
  local copies, waits for them, and re-layouts: 3.64 us -> 1.43 us
  waiting for transfers between devices: 4.2 us -> 3.12 us
    pallas_call x11 -> x12, Pallas kernels: 29.1 us -> 25 us  [run(): pl.pallas_call(kernel if layer is None else functools.partial(kernel, lay...]
    all_to_all x1, blocking collectives: 17 us -> 20.4 us  [on_device(): lax.all_to_all(reply.reshape(doms, CAP, width), 'dom', split_axis=0, conc...]
    ppermute x3, starting transfers between devices: 11.9 us -> 9.07 us  [swap(): from_far = lax.ppermute(far, ('dom', 'sub'), far_pairs)]
    unnamed x28 -> x24, local copies, waits for them, and re-layouts: 3.55 us -> 1.43 us
    ppermute x3, starting transfers between devices: 4.01 us -> 5.95 us  [on_device(): lax.ppermute(part, 'sub', [(i, i ^ k) for i in range(subs)])]
    ppermute x3, starting transfers between devices: 4.72 us -> 2.95 us  [swap(): from_near = lax.ppermute(near, ('dom', 'sub'), near_pairs)]
    ppermute x3, waiting for transfers between devices: 4.19 us -> 3.11 us  [on_device(): lax.ppermute(part, 'sub', [(i, i ^ k) for i in range(subs)])]
  transfers between devices with their start and end apart: 9 -> 9, of which waited for: 2 -> 2; matrix products, arithmetic and copies ran while one was open for 0% -> 0% of each run, Pallas kernels for 16% -> 13%
where the time goes in v2:
time: 96.1 us; the launch traced here: 95.8 us
  blocking collectives  47.4 us (49%)
  Pallas kernels  25 us (26%)
  starting transfers between devices  18 us (19%)
  waiting for transfers between devices  3.12 us (3%)
  local copies, waits for them, and re-layouts  1.43 us (1%)
    all_to_all x1, blocking collectives, on_device(): lax.all_to_all(parcel.reshape(doms, SLOTS, width), 'dom', split_axis=0, c...  27 us
    pallas_call x12, Pallas kernels, run(): pl.pallas_call(kernel if layer is None else functools.partial(kernel, lay...  25 us
    all_to_all x1, blocking collectives, on_device(): lax.all_to_all(reply.reshape(doms, CAP, width), 'dom', split_axis=0, conc...  20.4 us
    ppermute x3, starting transfers between devices, swap(): from_far = lax.ppermute(far, ('dom', 'sub'), far_pairs)  9.07 us
    ppermute x3, starting transfers between devices, on_device(): lax.ppermute(part, 'sub', [(i, i ^ k) for i in range(subs)])  5.95 us
    ppermute x3, waiting for transfers between devices, on_device(): lax.ppermute(part, 'sub', [(i, i ^ k) for i in range(subs)])  3.11 us
    ppermute x3, starting transfers between devices, swap(): from_near = lax.ppermute(near, ('dom', 'sub'), near_pairs)  2.95 us
  transfers between devices with their start and end apart: 9, of which 2 were waited for; matrix products, arithmetic and copies ran while one was open for 0% of the time, Pallas kernels for 13%

profile of v2, /device:TPU:1, one launch (start us, length us, event | category | flops | bytes accessed | tf_op | source)
XLA Modules:
  0.0 95.8 jit_solution(244604209332967405)
XLA Ops:
  0.7 0.6 copy-done.5
  1.4 0.8 prepare.1
  2.5 0.4 copy-done.9
  2.9 0.9 start.1
  3.8 2.6 %collective-permute-start = (bf16[128,128]{1,0:T(8,128)(2,1)S(1)}, bf16[128,128]{1,0:T(8,128)(2,1)S(1)}, u32[]{:S(2)}, u32[]{:S(2)}) collective-permute-start(bf16[128,128]{1,0:T(8,128)(2,1)S(1)} %get-tuple-element.41), channel_id=1, source_target_pairs={{0,1},{1,0},{2,3},{3,2},{4,5},{5,4},{6,7},{7,6},{8,9},{9,8},{10,11... | collective-permute-start | bytes 98312 | tf_op jit(solution)/shard_map/ppermute | solution.py:358
  6.4 3.4 %collective-permute-start.1 = (bf16[128,128]{1,0:T(8,128)(2,1)S(1)}, bf16[128,128]{1,0:T(8,128)(2,1)S(1)}, u32[]{:S(2)}, u32[]{:S(2)}) collective-permute-start(bf16[128,128]{1,0:T(8,128)(2,1)S(1)} %get-tuple-element.42), channel_id=1, source_target_pairs={{0,255},{1,2},{2,1},{3,4},{4,3},{5,6},{6,5},{7,8},{8,7},{9,10},{10... | collective-permute-start | bytes 98312 | tf_op jit(solution)/shard_map/ppermute | solution.py:359
  9.7 3.9 %inner.3 = (bf16[128,2048]{1,0:T(8,128)(2,1)S(1)}, bf16[256,128]{1,0:T(8,128)(2,1)S(1)}, bf16[128,256]{1,0:T(8,128)(2,1)S(1)}, bf16[128,128]{1,0:T(8,128)(2,1)S(1)}) custom-call(bf16[128,2048]{1,0:T(8,128)(2,1)S(1)} %get-tuple-element.39.rows_t.refs_0_, bf16[4,6,128,128]{3,2,1,0:T(8,128)(2,1)S(1)} %copy-done, s32[1,12288]{1,0:T(1,128)S(1)} %copy-done.2, ...), custom_call_target="tpu_custom_call" | custom-call | flops 4000000000 | bytes 1048576 | tf_op jit(solution)/shard_map/inner/pallas_call | solution.py:317
  13.7 2.1 %ends_pick.1 = (bf16[128,2048]{1,0:T(8,128)(2,1)S(1)}, bf16[128,128]{1,0:T(8,128)(2,1)S(1)}, bf16[128,128]{1,0:T(8,128)(2,1)S(1)}) custom-call(s32[4]{0:T(128)S(1)} %pad_add_fusion.place, bf16[128,2048]{1,0:T(8,128)(2,1)S(1)} %get-tuple-element.40.inner, bf16[128,2048]{1,0:T(8,128)(2,1)S(1)} %get-tuple-element.39.rows_t.refs_0_, ...), custom_call_target="tpu_custom_call" | custom-call | flops 1000000000 | bytes 1048576 | tf_op jit(solution)/shard_map/ends_pick/pallas_call | solution.py:317
  15.9 2.1 %collective-permute-start.3 = (bf16[128,128]{1,0:T(8,128)(2,1)S(1)}, bf16[128,128]{1,0:T(8,128)(2,1)S(1)}, u32[]{:S(2)}, u32[]{:S(2)}) collective-permute-start(bf16[128,128]{1,0:T(8,128)(2,1)S(1)} %get-tuple-element.49), channel_id=1, source_target_pairs={{0,255},{1,2},{2,1},{3,4},{4,3},{5,6},{6,5},{7,8},{8,7},{9,10},{10... | collective-permute-start | bytes 98312 | tf_op jit(solution)/shard_map/ppermute | solution.py:359
  18.0 3.9 %inner.4 = (bf16[128,2048]{1,0:T(8,128)(2,1)S(1)}, bf16[256,128]{1,0:T(8,128)(2,1)S(1)}, bf16[128,256]{1,0:T(8,128)(2,1)S(1)}, bf16[128,128]{1,0:T(8,128)(2,1)S(1)}) custom-call(bf16[128,2048]{1,0:T(8,128)(2,1)S(1)} %get-tuple-element.46.rows_t.refs_0_, bf16[4,6,128,128]{3,2,1,0:T(8,128)(2,1)S(1)} %copy-done, s32[1,12288]{1,0:T(1,128)S(1)} %copy-done.2, ...), custom_call_target="tpu_custom_call" | custom-call | flops 4000000000 | bytes 1048576 | tf_op jit(solution)/shard_map/inner/pallas_call | solution.py:317
  21.9 2.5 %ends_pool.1 = (bf16[128,2048]{1,0:T(8,128)(2,1)S(1)}, bf16[1024,128]{1,0:T(8,128)(2,1)S(1)}) custom-call(s32[4]{0:T(128)S(1)} %pad_add_fusion.place, bf16[128,2048]{1,0:T(8,128)(2,1)S(1)} %get-tuple-element.47.inner, bf16[128,2048]{1,0:T(8,128)(2,1)S(1)} %get-tuple-element.46.rows_t.refs_0_, bf16[128,128]{1,0:T(8,128)(2,1)S(1)} %collective-permute-done.2.refs_1_, ...), custom_call_target="tpu_custom_call" | custom-call | flops 1000000000 | bytes 1048576 | tf_op jit(solution)/shard_map/ends_pool/pallas_call | solution.py:317
  24.4 27.0 %all_to_all.10 = bf16[64,16,128]{2,1,0:T(8,128)(2,1)S(1)} all-to-all(bf16[64,16,128]{2,1,0:T(8,128)(2,1)S(1)} %bitcast.10), channel_id=1, replica_groups=mesh['dom'=64,'sub'=4] {'dom'}, dimensions={0} | all-to-all | bytes 524288 | tf_op jit(solution)/shard_map/all_to_all | solution.py:409
  51.4 1.3 %received.1 = (bf16[176,128]{1,0:T(8,128)(2,1)S(1)}, bf16[64,128]{1,0:T(8,128)(2,1)S(1)}) custom-call(s32[4]{0:T(128)S(1)} %pad_add_fusion.place, bf16[1024,128]{1,0:T(8,128)(2,1)S(1)} %bitcast.11), custom_call_target="tpu_custom_call" | custom-call | flops 1000000000 | bytes 1048576 | tf_op jit(solution)/shard_map/received/pallas_call | solution.py:317
  52.8 5.6 %collective-permute-start.6 = (bf16[176,128]{1,0:T(8,128)(2,1)S(1)}, bf16[176,128]{1,0:T(8,128)(2,1)S(1)}, u32[]{:S(2)}, u32[]{:S(2)}) collective-permute-start(bf16[176,128]{1,0:T(8,128)(2,1)S(1)} %get-tuple-element.57.own), channel_id=1, source_target_pairs={{0,3},{1,2},{2,1},{3,0},{4,7},{5,6},{6,5},{7,4},{8,11},{9,10},{10,... | collective-permute-start | bytes 135176 | tf_op jit(solution)/shard_map/ppermute | solution.py:420
  58.3 0.4 collective-permute-start.4
  58.7 0.3 ready.1
  59.0 0.7 collective-permute-done.6.other3
  59.8 2.4 %collective-permute-done.5.other2 = bf16[176,128]{1,0:T(8,128)(2,1)S(1)} collective-permute-done((bf16[176,128]{1,0:T(8,128)(2,1)S(1)}, bf16[176,128]{1,0:T(8,128)(2,1)S(1)}, u32[]{:S(2)}, u32[]{:S(2)}) %collective-permute-start.5) | collective-permute-done | bytes 45088 | tf_op jit(solution)/shard_map/ppermute | solution.py:420
  62.2 1.7 %coarse.1 = (bf16[128,128]{1,0:T(8,128)(2,1)}, bf16[256,128]{1,0:T(8,128)(2,1)S(1)}) custom-call(bf16[176,128]{1,0:T(8,128)(2,1)S(1)} %get-tuple-element.57.own, bf16[176,128]{1,0:T(8,128)(2,1)S(1)} %collective-permute-done.4.other1, bf16[176,128]{1,0:T(8,128)(2,1)S(1)} %collective-permute-done.5.other2, bf16[176,128]{1,0:T(8,128)(2,1)S(1)} %collective-permute-done.6.other3, ...), custom_call_target="tpu_custom_call" | custom-call | flops 1000000000 | bytes 1048576 | tf_op jit(solution)/shard_map/coarse/pallas_call | solution.py:317
  63.8 20.4 %all_to_all.11 = bf16[64,4,128]{2,1,0:T(4,128)(2,1)S(1)} all-to-all(bf16[64,4,128]{2,1,0:T(4,128)(2,1)S(1)} %bitcast.12), channel_id=1, replica_groups=mesh['dom'=64,'sub'=4] {'dom'}, dimensions={0} | all-to-all | bytes 131072 | tf_op jit(solution)/shard_map/all_to_all | solution.py:436
  84.3 1.2 %lift.1 = (bf16[128,2048]{1,0:T(8,128)(2,1)S(1)}, bf16[128,128]{1,0:T(8,128)(2,1)S(1)}, bf16[128,128]{1,0:T(8,128)(2,1)S(1)}) custom-call(s32[4]{0:T(128)S(1)} %pad_add_fusion.place, bf16[128,2048]{1,0:T(8,128)(2,1)S(1)} %get-tuple-element.54.rows_t, s32[1,2048]{1,0:T(1,128)S(1)} %copy-done.5, bf16[256,128]{1,0:T(8,128)(2,1)S(1)} %get-tuple-element.55.slot_of, ...), custom_call_target="tpu_custom_call" | custom-call | flops 1000000000 | bytes 1048576 | tf_op jit(solution)/shard_map/lift/pallas_call | solution.py:317
  85.8 3.6 %collective-permute-start.8 = (bf16[128,128]{1,0:T(8,128)(2,1)S(1)}, bf16[128,128]{1,0:T(8,128)(2,1)S(1)}, u32[]{:S(2)}, u32[]{:S(2)}) collective-permute-start(bf16[128,128]{1,0:T(8,128)(2,1)S(1)} %get-tuple-element.69), channel_id=1, source_target_pairs={{0,255},{1,2},{2,1},{3,4},{4,3},{5,6},{6,5},{7,8},{8,7},{9,10},{10... | collective-permute-start | bytes 98312 | tf_op jit(solution)/shard_map/ppermute | solution.py:359
  89.4 3.9 %inner.5 = (bf16[128,2048]{1,0:T(8,128)(2,1)S(1)}, bf16[256,128]{1,0:T(8,128)(2,1)S(1)}, bf16[128,256]{1,0:T(8,128)(2,1)S(1)}, bf16[128,128]{1,0:T(8,128)(2,1)S(1)}) custom-call(bf16[128,2048]{1,0:T(8,128)(2,1)S(1)} %get-tuple-element.66.rows_t.refs_0_, bf16[4,6,128,128]{3,2,1,0:T(8,128)(2,1)S(1)} %copy-done, s32[1,12288]{1,0:T(1,128)S(1)} %copy-done.2, ...), custom_call_target="tpu_custom_call" | custom-call | flops 4000000000 | bytes 1048576 | tf_op jit(solution)/shard_map/inner/pallas_call | solution.py:317
  93.4 2.5 %ends.1 = bf16[2048,128]{1,0:T(8,128)(2,1)} custom-call(s32[4]{0:T(128)S(1)} %pad_add_fusion.place, bf16[128,2048]{1,0:T(8,128)(2,1)S(1)} %get-tuple-element.67.inner, bf16[128,2048]{1,0:T(8,128)(2,1)S(1)} %get-tuple-element.66.rows_t.refs_0_, bf16[128,128]{1,0:T(8,128)(2,1)S(1)} %collective-permute-done.7.refs_1_, ...), custom_call_target="tpu_custom_call" | custom-call | flops 1000000000 | bytes 1048576 | tf_op jit(solution)/shard_map/ends/pallas_call | solution.py:317
  (33 shorter events, 0.9 us)
Async XLA Ops:
  0.6 0.7 copy-start.5
  0.6 0.7 copy-start.11
  0.7 0.7 copy-start.8
  0.7 0.7 copy-start.10
  1.4 1.0 %copy-start.1 = (bf16[2048,128]{1,0:T(8,128)(2,1)S(1)}, bf16[2048,128]{1,0:T(8,128)(2,1)}, u32[]{:S(2)}) copy-start(bf16[2048,128]{1,0:T(8,128)(2,1)} %nodes.1) | copy-start | bytes 1572868
  2.2 0.7 copy-start.9
  2.9 6.8 %copy-start = (bf16[4,6,128,128]{3,2,1,0:T(8,128)(2,1)S(1)}, bf16[4,6,128,128]{3,2,1,0:T(8,128)(2,1)}, u32[]{:S(2)}) copy-start(bf16[4,6,128,128]{3,2,1,0:T(8,128)(2,1)} %weights.7) | copy-start | bytes 2359300
  2.9 6.8 %copy-start.2 = (s32[1,12288]{1,0:T(1,128)S(1)}, s32[1,12288]{1,0:T(1,128)}, u32[]{:S(2)}) copy-start(s32[1,12288]{1,0:T(1,128)} %refs_6_.5) | copy-start | bytes 147460
  2.9 6.8 %copy-start.3 = (s32[1,12288]{1,0:T(1,128)S(1)}, s32[1,12288]{1,0:T(1,128)}, u32[]{:S(2)}) copy-start(s32[1,12288]{1,0:T(1,128)} %refs_7_.5) | copy-start | bytes 147460
  2.9 6.8 %copy-start.4 = (s32[1,12288]{1,0:T(1,128)S(1)}, s32[1,12288]{1,0:T(1,128)}, u32[]{:S(2)}) copy-start(s32[1,12288]{1,0:T(1,128)} %refs_8_.5) | copy-start | bytes 147460
  3.8 9.9 %collective-permute-start = (bf16[128,128]{1,0:T(8,128)(2,1)S(1)}, bf16[128,128]{1,0:T(8,128)(2,1)S(1)}, u32[]{:S(2)}, u32[]{:S(2)}) collective-permute-start(bf16[128,128]{1,0:T(8,128)(2,1)S(1)} %get-tuple-element.41), channel_id=1, source_target_pairs={{0,1},{1,0},{2,3},{3,2},{4,5},{5,4},{6,7},{7,6},{8,9},{9,8},{10,11... | collective-permute-start | bytes 98312 | tf_op jit(solution)/shard_map/ppermute | solution.py:358
  6.4 7.3 %collective-permute-start.1 = (bf16[128,128]{1,0:T(8,128)(2,1)S(1)}, bf16[128,128]{1,0:T(8,128)(2,1)S(1)}, u32[]{:S(2)}, u32[]{:S(2)}) collective-permute-start(bf16[128,128]{1,0:T(8,128)(2,1)S(1)} %get-tuple-element.42), channel_id=1, source_target_pairs={{0,255},{1,2},{2,1},{3,4},{4,3},{5,6},{6,5},{7,8},{8,7},{9,10},{10... | collective-permute-start | bytes 98312 | tf_op jit(solution)/shard_map/ppermute | solution.py:359
  15.8 6.1 %collective-permute-start.2 = (bf16[128,128]{1,0:T(8,128)(2,1)S(1)}, bf16[128,128]{1,0:T(8,128)(2,1)S(1)}, u32[]{:S(2)}, u32[]{:S(2)}) collective-permute-start(bf16[128,128]{1,0:T(8,128)(2,1)S(1)} %get-tuple-element.48), channel_id=1, source_target_pairs={{0,1},{1,0},{2,3},{3,2},{4,5},{5,4},{6,7},{7,6},{8,9},{9,8},{10,11... | collective-permute-start | bytes 98312 | tf_op jit(solution)/shard_map/ppermute | solution.py:358
  15.9 6.0 %collective-permute-start.3 = (bf16[128,128]{1,0:T(8,128)(2,1)S(1)}, bf16[128,128]{1,0:T(8,128)(2,1)S(1)}, u32[]{:S(2)}, u32[]{:S(2)}) collective-permute-start(bf16[128,128]{1,0:T(8,128)(2,1)S(1)} %get-tuple-element.49), channel_id=1, source_target_pairs={{0,255},{1,2},{2,1},{3,4},{4,3},{5,6},{6,5},{7,8},{8,7},{9,10},{10... | collective-permute-start | bytes 98312 | tf_op jit(solution)/shard_map/ppermute | solution.py:359
  51.4 7.3 %copy-start.7 = (s32[1,768]{1,0:T(1,128)S(1)}, s32[1,768]{1,0:T(1,128)}, u32[]{:S(2)}) copy-start(s32[1,768]{1,0:T(1,128)} %dst.6) | copy-start | bytes 9220
  52.8 6.0 %copy-start.6 = (s32[1,768]{1,0:T(1,128)S(1)}, s32[1,768]{1,0:T(1,128)}, u32[]{:S(2)}) copy-start(s32[1,768]{1,0:T(1,128)} %src.6) | copy-start | bytes 9220
  52.8 7.0 %collective-permute-start.6 = (bf16[176,128]{1,0:T(8,128)(2,1)S(1)}, bf16[176,128]{1,0:T(8,128)(2,1)S(1)}, u32[]{:S(2)}, u32[]{:S(2)}) collective-permute-start(bf16[176,128]{1,0:T(8,128)(2,1)S(1)} %get-tuple-element.57.own), channel_id=1, source_target_pairs={{0,3},{1,2},{2,1},{3,0},{4,7},{5,6},{6,5},{7,4},{8,11},{9,10},{10,... | collective-permute-start | bytes 135176 | tf_op jit(solution)/shard_map/ppermute | solution.py:420
  58.3 3.8 %collective-permute-start.5 = (bf16[176,128]{1,0:T(8,128)(2,1)S(1)}, bf16[176,128]{1,0:T(8,128)(2,1)S(1)}, u32[]{:S(2)}, u32[]{:S(2)}) collective-permute-start(bf16[176,128]{1,0:T(8,128)(2,1)S(1)} %get-tuple-element.57.own), channel_id=1, source_target_pairs={{0,2},{1,3},{2,0},{3,1},{4,6},{5,7},{6,4},{7,5},{8,10},{9,11},{10,... | collective-permute-start | bytes 135176 | tf_op jit(solution)/shard_map/ppermute | solution.py:420
  58.3 3.8 %collective-permute-start.4 = (bf16[176,128]{1,0:T(8,128)(2,1)S(1)}, bf16[176,128]{1,0:T(8,128)(2,1)S(1)}, u32[]{:S(2)}, u32[]{:S(2)}) collective-permute-start(bf16[176,128]{1,0:T(8,128)(2,1)S(1)} %get-tuple-element.57.own), channel_id=1, source_target_pairs={{0,1},{1,0},{2,3},{3,2},{4,5},{5,4},{6,7},{7,6},{8,9},{9,8},{10,11... | collective-permute-start | bytes 135176 | tf_op jit(solution)/shard_map/ppermute | solution.py:420
  85.5 7.8 %collective-permute-start.7 = (bf16[128,128]{1,0:T(8,128)(2,1)S(1)}, bf16[128,128]{1,0:T(8,128)(2,1)S(1)}, u32[]{:S(2)}, u32[]{:S(2)}) collective-permute-start(bf16[128,128]{1,0:T(8,128)(2,1)S(1)} %get-tuple-element.68), channel_id=1, source_target_pairs={{0,1},{1,0},{2,3},{3,2},{4,5},{5,4},{6,7},{7,6},{8,9},{9,8},{10,11... | collective-permute-start | bytes 98312 | tf_op jit(solution)/shard_map/ppermute | solution.py:358
  85.8 7.6 %collective-permute-start.8 = (bf16[128,128]{1,0:T(8,128)(2,1)S(1)}, bf16[128,128]{1,0:T(8,128)(2,1)S(1)}, u32[]{:S(2)}, u32[]{:S(2)}) collective-permute-start(bf16[128,128]{1,0:T(8,128)(2,1)S(1)} %get-tuple-element.69), channel_id=1, source_target_pairs={{0,255},{1,2},{2,1},{3,4},{4,3},{5,6},{6,5},{7,8},{8,7},{9,10},{10... | collective-permute-start | bytes 98312 | tf_op jit(solution)/shard_map/ppermute | solution.py:359

commit v3 on v2

--- a/solution.py
+++ b/solution.py
@@ -18,6 +18,7 @@
 GH = 128
 CAP = 4
 SLOTS = 16
+BACK = 3 * CAP
 VMEM_LIMIT = 28 << 20
 
 
@@ -44,6 +45,10 @@
 def rows_hot(index_row, count):
     table = lax.broadcasted_iota(I16, (count, index_row.shape[1]), 0)
     return jnp.where(table == index_row.astype(I16), BF(1), BF(0))
+
+
+def over_back(row):
+    return (row * (65536 // BACK + 1)) >> 16
 
 
 def edge_sum(source_t, target_t, from_hot, to_hot):
@@ -83,8 +88,8 @@
         [jnp.where(odd, to_lower, to_upper), jnp.where(odd, to_upper, to_lower)], axis=1
     )
     picked = dot(rows_t[...], rows_hot(wanted, rows_t.shape[1])).astype(BF)
-    near[...] = picked[:, :GH]
-    far[...] = picked[:, GH:]
+    near[0 : picked.shape[0], :] = picked[:, :GH]
+    far[0 : picked.shape[0], :] = picked[:, GH:]
 
 
 def inner_kernel(layer, rows_t, weights, src, dst, valid, out, first, both, last, ends, sums):
@@ -106,15 +111,24 @@
         out[:, at] = node_update(rows_t[:, at], sums[:, at], both[...], last[...])
 
 
-def end_blocks(place, rows_t, from_near, from_far, first, both, last, src, dst, valid):
+def by_side(place, near, far):
     odd = place[1] % 2 == 1
+    return jnp.where(odd, near, far), jnp.where(odd, far, near)
+
+
+def ghost_rows(place, before, after):
+    nothing = jnp.zeros_like(before)
+    return jnp.where(place[2] == 0, nothing, before), jnp.where(place[3] == 0, nothing, after)
+
+
+def end_blocks(place, rows_t, from_near, from_far, first, both, last, src, dst, valid, turn=False):
     row_count = rows_t.shape[1]
     blocks = row_count // GH
     width = src.shape[1] // blocks
-    near, far = from_near[...], from_far[...]
-    nothing = jnp.zeros_like(near)
-    before = jnp.where(place[2] == 0, nothing, jnp.where(odd, near, far))
-    after = jnp.where(place[3] == 0, nothing, jnp.where(odd, far, near))
+    before, after = by_side(place, from_near[0:128, :], from_far[0:128, :])
+    before, after = ghost_rows(place, before, after)
+    if turn:
+        before, after = before.T, after.T
     head, tail = rows_t[:, 0 : 2 * GH], rows_t[:, row_count - 2 * GH :]
     line = jnp.concatenate([before, head, tail, after], axis=1)
     ends = dot(first[...], line).astype(BF)
@@ -137,19 +151,15 @@
     out[:, count - GH :] = new[:, GH:]
 
 
-def ends_kernel(place, inner, *refs):
-    out = refs[-1]
-    new = end_blocks(place, *refs[:-1])
-    count = out.shape[0]
-    out[GH : count - GH, :] = inner[:, GH : count - GH].T
-    out[0:GH, :] = new[:, :GH].T
-    out[count - GH :, :] = new[:, GH:].T
-
-
 def ends_pick_kernel(place, inner, *refs):
-    lists, out, near, far = refs[-4:]
-    whole_layer(inner, end_blocks(place, *refs[:-4]), out)
-    pick_both(out, lists, place[1] % 2 == 1, near, far)
+    lists, cluster, facts, slot_row, out, near, far, more = refs[-8:]
+    slots = dot(slot_row[...], rows_hot(cluster[...], 128)).astype(BF)
+    whole_layer(inner, end_blocks(place, *refs[:-8], turn=True), out)
+    more[0:128, :] = out[...]
+    more[128:144, :] = slots
+    pick_both(more, lists, place[1] % 2 == 1, near, far)
+    near[144:208, :] = facts[0:64, :]
+    far[144:208, :] = facts[0:64, :]
 
 
 def ends_pool_kernel(place, inner, *refs):
@@ -157,15 +167,26 @@
     whole_layer(inner, end_blocks(place, *refs[:-5]), out)
     member = rows_hot(cluster[...], 128)
     partial = dot(out[...], member, NT).T.astype(BF)
-    parcel[...] = dot(slot_pick[...], jnp.concatenate([partial, facts[...]], axis=0)).astype(BF)
-
-
-def start_kernel(place, nodes, lists, facts, rows_t, near, far):
+    ids = by_side(place, refs[1][144:208, :], refs[2][144:208, :])
+    lane = iota(ids[0].shape, 1)
+    moved = [pltpu.roll(ids[side].astype(F32), CAP * (3 + side), 1) for side in (0, 1)]
+    moved = [jnp.where(lane // CAP == 3 + side, moved[side], 0.0) for side in (0, 1)]
+    added = moved[0] + moved[1]
+    known = jnp.concatenate([added, jnp.zeros_like(added)], axis=0) + facts[...].astype(F32)
+    parcel[...] = dot(
+        slot_pick[...], jnp.concatenate([partial, known.astype(BF)], axis=0)
+    ).astype(BF)
+
+
+def turn_kernel(nodes, rows_t):
     rows_t[...] = nodes[...].T
+
+
+def pick_kernel(place, rows_t, lists, near, far):
     pick_both(rows_t, lists, place[1] % 2 == 1, near, far)
 
 
-def prepare_kernel(cluster, owner, coarse_row, ghosts, slot_pick, facts, slot_of):
+def prepare_kernel(cluster, owner, coarse_row, ghosts, slot_pick, facts, slot_of, slot_row_out):
     member = rows_hot(cluster[...], 128)
     counts = jnp.sum(member.astype(F32), axis=1, keepdims=True)
     owner_row = owner[...].astype(F32)
@@ -176,7 +197,7 @@
     place_row = jnp.sum(jnp.where(same & (sub < lane), 1.0, 0.0), axis=0, keepdims=True)
     slot_row = owner_row * CAP + place_row
     owners = slot_pick.shape[0] // SLOTS
-    slot_of[...] = hot(slot_row == iota((CAP * owners, 128), 0, F32))
+    slot_row_out[...] = jnp.broadcast_to(slot_row, slot_row_out.shape).astype(BF)
     row = iota((owners * SLOTS, 128), 0)
     to, at = row // SLOTS, row % SLOTS
     label = jnp.where(
@@ -189,6 +210,12 @@
         ),
     )
     slot_pick[:, 0:128] = hot(label.astype(F32) == slot_row)
+    back_row = iota(slot_of.shape, 0)
+    back_to = over_back(back_row)
+    back_at = back_row - BACK * back_to
+    slot_of[...] = hot(
+        jnp.where(back_at < CAP, CAP * back_to + back_at, -1).astype(F32) == slot_row
+    )
     fact = jnp.where(
         at == 3 * CAP,
         to,
@@ -269,16 +296,19 @@
     ).astype(BF)
 
 
-def ready_kernel(layer, own_metas, weights, src, dst, back, first, both, last, from_hot, to_hot):
+def ready_kernel(own_metas, weights, src, dst, near, far, *outs):
+    back, first, both, last, from_hot, to_hot, first3, both3, last3 = outs
     owners = own_metas.shape[0]
-    slots = CAP * owners
-    turn = iota((slots, owners), 0)
-    ids = dot(hot(turn // CAP == iota((slots, owners), 1)), own_metas[...])
-    lanes = iota((slots, 128), 1)
-    turns = iota((slots, 128), 0) % CAP
-    named = jnp.sum(jnp.where(lanes == turns, ids, 0.0), axis=1, keepdims=True)
+    total = BACK * owners
+    ids = dot(hot(over_back(iota((total, owners), 0)) == iota((total, owners), 1)), own_metas[...])
+    row = iota((total, 128), 0)
+    at = row - BACK * over_back(row)
+    lanes = iota((total, 128), 1)
+    wanted = jnp.where(at < CAP, at, at + 2 * CAP)
+    named = jnp.sum(jnp.where(lanes == wanted, ids, 0.0), axis=1, keepdims=True)
     back[...] = hot(lanes.astype(F32) == named)
-    first[...], both[...], last[...] = layer_weights([weights[layer, i] for i in range(6)])
+    first[...], both[...], last[...] = layer_weights([weights[2, i] for i in range(6)])
+    first3[...], both3[...], last3[...] = layer_weights([weights[3, i] for i in range(6)])
     from_hot[...] = rows_hot(src[...], 160)
     to_hot[...] = rows_hot(dst[...], 128)
 
@@ -303,11 +333,55 @@
     reply[...] = dot(back[...], new).astype(BF)
 
 
-def lift_kernel(place, rows_t, cluster, slot_of, reply, lists, out, near, far):
-    by_cluster = dot(reply[...], slot_of[...], TN).astype(BF)
+def final_kernel(
+    place,
+    rows_t,
+    reply,
+    slot_of,
+    cluster,
+    early_near,
+    early_far,
+    from_near,
+    from_far,
+    first,
+    both,
+    last,
+    src,
+    dst,
+    valid,
+    out,
+    line,
+    ends,
+    sums,
+):
+    row_count = rows_t.shape[1]
+    blocks = row_count // GH
+    width = src.shape[1] // blocks
+    tables = [slot_of[...]]
+    for at, slots in enumerate(by_side(place, early_near[128:144, :], early_far[128:144, :])):
+        slot = slots.astype(F32).astype(I32)[0:1]
+        tables.append(rows_hot(slot // CAP * BACK + slot % CAP + CAP * (at + 1), reply.shape[0]))
+    coarse = dot(reply[...], jnp.concatenate(tables, axis=1), TN)
     member = rows_hot(cluster[...], 128)
-    out[...] = (rows_t[...].astype(F32) + dot(by_cluster, member)).astype(BF)
-    pick_both(out, lists, place[1] % 2 == 1, near, far)
+    before, after = by_side(place, from_near[...], from_far[...])
+    before = (before.astype(F32) + coarse[:, 128:256]).astype(BF)
+    after = (after.astype(F32) + coarse[:, 256:384]).astype(BF)
+    line[:, 0:GH], line[:, GH + row_count :] = ghost_rows(place, before, after)
+    line[:, GH : GH + row_count] = (
+        rows_t[...].astype(F32) + dot(coarse[:, 0:128].astype(BF), member)
+    ).astype(BF)
+    ends[...] = dot(first[...], line[...]).astype(BF)
+    for b in range(blocks):
+        sums[:, b * GH : (b + 1) * GH] = edge_sum(
+            ends[0:128, b * GH : (b + 3) * GH],
+            ends[128:256, (b + 1) * GH : (b + 2) * GH],
+            *local_edges(b, row_count, src, dst, valid, width),
+        )
+    step = row_count // 2
+    for start in range(0, row_count, step):
+        own = line[:, GH + start : GH + start + step]
+        new = node_update(own, sums[:, start : start + step], both[...], last[...])
+        out[start : start + step, :] = new.T
 
 
 def run(kernel, outs, args, scalars=0, layer=None, scratch=(), flops=0, name=None):
@@ -371,88 +445,91 @@
         )
         return out, tuple(weights_now)
 
-    slot_pick, facts, slot_of = run(
+    wanted = lists.reshape(-1, 1) == jnp.arange(count, dtype=I32)[None, :]
+    picked = dot(wanted.astype(BF), nodes).astype(BF)
+    odd = sub % 2 == 1
+    ghosts = swap(
+        jnp.where(odd, picked[:GH], picked[GH:]), jnp.where(odd, picked[GH:], picked[:GH])
+    )
+    (states,) = run(turn_kernel, [rows_t], (nodes,), flops=3 * 10**8, name="turn")
+    slot_pick, facts, slot_of, slot_row = run(
         prepare_kernel,
-        [(doms * SLOTS, 256), (128, 128), (CAP * doms, 128)],
+        [(doms * SLOTS, 256), (128, 128), (doms * BACK, 128), (16, 128)],
         (cluster_of, owner.reshape(1, -1), coarse_row, coarse_ghosts),
-        flops=3 * 10**9,
+        flops=10**9,
         name="prepare",
     )
-    states, near, far = run(
-        start_kernel,
-        [rows_t, ghost, ghost],
-        (place, nodes, lists, facts),
-        scalars=1,
-        flops=10**9,
-        name="start",
-    )
-    ghosts = swap(near, far)
     middle, now = inner(states, 0)
+    early = (GH + 16 + doms, GH)
     states, near, far = run(
         ends_pick_kernel,
-        [rows_t, ghost, ghost],
-        (place, middle, states) + ghosts + now + edges + (lists,),
+        [rows_t, early, early],
+        (place, middle, states) + ghosts + now + edges + (lists, cluster_of, facts, slot_row),
         scalars=1,
+        scratch=[pltpu.VMEM((width + 16, count), BF)],
         flops=10**9,
         name="ends_pick",
     )
-    ghosts = swap(near, far)
+    early = swap(near, far)
     middle, now = inner(states, 1)
     states, parcel = run(
         ends_pool_kernel,
         [rows_t, (doms * SLOTS, width)],
-        (place, middle, states) + ghosts + now + edges + (cluster_of, slot_pick, facts),
+        (place, middle, states) + early + now + edges + (cluster_of, slot_pick, facts),
         scalars=1,
         flops=10**9,
         name="ends_pool",
     )
-    got = lax.all_to_all(
-        parcel.reshape(doms, SLOTS, width), "dom", split_axis=0, concat_axis=0, tiled=True
-    ).reshape(doms * SLOTS, width)
+    ghosts = swap(
+        *run(pick_kernel, [ghost, ghost], (place, states, lists), scalars=1, flops=10**9, name="pick")
+    )
+
+    def exchange(rows):
+        shape = rows.shape
+        rows = rows.reshape(doms, shape[0] // doms, width)
+        rows = lax.all_to_all(rows, "dom", split_axis=0, concat_axis=0, tiled=True)
+        return rows.reshape(shape)
+
     part, own_metas = run(
         received_kernel,
         [(176, width), (doms, width)],
-        (place, got),
+        (place, exchange(parcel)),
         scalars=1,
         flops=10**9,
         name="received",
     )
-    others = [lax.ppermute(part, "sub", [(i, i ^ k) for i in range(subs)]) for k in (1, 2, 3)]
-    ready = run(
+    others = {
+        k: lax.ppermute(part, "sub", [(i, i ^ k) for i in range(subs)]) for k in (1, 3, 2)
+    }
+    back, *ready = run(
         ready_kernel,
-        [(doms * CAP, width)] + forms + [(160, coarse_src.shape[1]), (128, coarse_src.shape[1])],
-        (own_metas, weights, coarse_src, coarse_dst),
-        layer=2,
+        [(doms * BACK, width)]
+        + forms
+        + [(160, coarse_src.shape[1]), (128, coarse_src.shape[1])]
+        + forms,
+        (own_metas, weights, coarse_src, coarse_dst) + ghosts,
         flops=10**9,
         name="ready",
     )
     coarse, reply = run(
         coarse_kernel,
-        [(128, width), (doms * CAP, width)],
-        (part, *others, *ready),
+        [(128, width), (doms * BACK, width)],
+        (part, others[1], others[2], others[3], back, *ready[:5]),
         flops=10**9,
         name="coarse",
     )
-    reply = lax.all_to_all(
-        reply.reshape(doms, CAP, width), "dom", split_axis=0, concat_axis=0, tiled=True
-    ).reshape(doms * CAP, width)
-    states, near, far = run(
-        lift_kernel,
-        [rows_t, ghost, ghost],
-        (place, states, cluster_of, slot_of, reply, lists),
+    (last,) = run(
+        final_kernel,
+        [nodes.shape],
+        (place, states, exchange(reply), slot_of, cluster_of) + early + ghosts + tuple(ready[5:8]) + edges,
         scalars=1,
-        flops=10**9,
-        name="lift",
-    )
-    ghosts = swap(near, far)
-    middle, now = inner(states, 3)
-    (last,) = run(
-        ends_kernel,
-        [nodes.shape],
-        (place, middle, states) + ghosts + now + edges,
-        scalars=1,
-        flops=10**9,
-        name="ends",
+        scratch=[
+            pltpu.VMEM((width, count + 2 * GH), BF),
+            pltpu.VMEM((2 * width, count + 2 * GH), BF),
+            pltpu.VMEM(rows_t, BF),
+        ],
+        flops=5 * 10**9,
+        name="final",
     )
     return (last, coarse)
 

time: 96.1 us -> 92.7 us (0.965)
  blocking collectives: 47.4 us -> 21.7 us
  starting transfers between devices: 18 us -> 29 us
  waiting for transfers between devices: 3.12 us -> 13.2 us
  matrix products: 0 us -> 1.6 us
  local copies, waits for them, and re-layouts: 1.43 us -> 0.16 us
    all_to_all x2 -> x1, blocking collectives: 47.4 us -> 21.7 us  [exchange(): rows = lax.all_to_all(rows, 'dom', split_axis=0, concat_axis=0, tiled=True)]
    all_to_all x0 -> x1, starting transfers between devices: none -> 14 us  [exchange(): rows = lax.all_to_all(rows, 'dom', split_axis=0, concat_axis=0, tiled=True)]
    all_to_all x0 -> x1, waiting for transfers between devices: none -> 9.83 us  [exchange(): rows = lax.all_to_all(rows, 'dom', split_axis=0, concat_axis=0, tiled=True)]
    ppermute x3, starting transfers between devices: 5.95 us -> 3.63 us  [on_device(): lax.ppermute(part, 'sub', [(i, i ^ k) for i in range(subs)])]
    dot_general x0 -> x1, matrix products: none -> 1.6 us  [dot(): return lax.dot_general(left, right, dims, preferred_element_type=F32)]
    unnamed x24, local copies, waits for them, and re-layouts: 1.43 us -> 0.07 us
    ppermute x3, starting transfers between devices: 2.95 us -> 1.64 us  [swap(): from_near = lax.ppermute(near, ('dom', 'sub'), near_pairs)]
    pallas_call x12 -> x11, Pallas kernels: 25 us -> 24.9 us  [run(): pl.pallas_call(kernel if layer is None else functools.partial(kernel, lay...]
  transfers between devices with their start and end apart: 9 -> 10, of which waited for: 2 -> 4; matrix products, arithmetic and copies ran while one was open for 0% -> 0% of each run, Pallas kernels for 13% -> 13%
where the time goes in v3:
time: 92.7 us; the launch traced here: 91.6 us
  starting transfers between devices  29 us (31%)
  Pallas kernels  24.9 us (27%)
  blocking collectives  21.7 us (23%)
  waiting for transfers between devices  13.2 us (14%)
  matrix products  1.6 us (2%)
    pallas_call x11, Pallas kernels, run(): pl.pallas_call(kernel if layer is None else functools.partial(kernel, lay...  24.9 us
    all_to_all x1, blocking collectives, exchange(): rows = lax.all_to_all(rows, 'dom', split_axis=0, concat_axis=0, tiled=True)  21.7 us
    all_to_all x1, starting transfers between devices, exchange(): rows = lax.all_to_all(rows, 'dom', split_axis=0, concat_axis=0, tiled=True)  14 us
    all_to_all x1, waiting for transfers between devices, exchange(): rows = lax.all_to_all(rows, 'dom', split_axis=0, concat_axis=0, tiled=True)  9.83 us
    ppermute x3, starting transfers between devices, swap(): from_far = lax.ppermute(far, ('dom', 'sub'), far_pairs)  9.81 us
    ppermute x3, starting transfers between devices, on_device(): lax.ppermute(part, 'sub', [(i, i ^ k) for i in range(subs)])  3.63 us
    ppermute x3, waiting for transfers between devices, on_device(): lax.ppermute(part, 'sub', [(i, i ^ k) for i in range(subs)])  2.59 us
  transfers between devices with their start and end apart: 10, of which 4 were waited for; matrix products, arithmetic and copies ran while one was open for 0% of the time, Pallas kernels for 13%

profile of v3, /device:TPU:1, one launch (start us, length us, event | category | flops | bytes accessed | tf_op | source)
XLA Modules:
  0.0 91.6 jit_solution(1059345672327893122)
XLA Ops:
  0.7 1.6 %fusion.1 = bf16[256,128]{1,0:T(8,128)(2,1)S(1)} fusion(bf16[2048,128]{1,0:T(8,128)(2,1)} %nodes.1, s32[256]{0:T(256)} %bitcast.11), kind=kOutput, calls=%fused_computation.2 | convolution fusion | flops 134774784 | bytes 590848 | tf_op jit(solution)/shard_map/dot_general | solution.py:26
  2.3 5.8 %collective-permute-start.1 = (bf16[128,128]{1,0:T(8,128)(2,1)S(1)}, bf16[128,128]{1,0:T(8,128)(2,1)S(1)}, u32[]{:S(2)}, u32[]{:S(2)}) collective-permute-start(bf16[128,128]{1,0:T(8,128)(2,1)S(1)} %get-tuple-element.66), channel_id=1, source_target_pairs={{0,255},{1,2},{2,1},{3,4},{4,3},{5,6},{6,5},{7,8},{8,7},{9,10},{10... | collective-permute-start | bytes 98312 | tf_op jit(solution)/shard_map/ppermute | solution.py:433
  8.2 0.2 turn.1.rows_t.refs_0_
  8.5 3.9 %inner.2 = (bf16[128,2048]{1,0:T(8,128)(2,1)S(1)}, bf16[256,128]{1,0:T(8,128)(2,1)S(1)}, bf16[128,256]{1,0:T(8,128)(2,1)S(1)}, bf16[128,128]{1,0:T(8,128)(2,1)S(1)}) custom-call(bf16[128,2048]{1,0:T(8,128)(2,1)S(1)} %turn.1.rows_t.refs_0_, bf16[4,6,128,128]{3,2,1,0:T(8,128)(2,1)S(1)} %copy-done, s32[1,12288]{1,0:T(1,128)S(1)} %copy-done.2, ...), custom_call_target="tpu_custom_call" | custom-call | flops 4000000000 | bytes 1048576 | tf_op jit(solution)/shard_map/inner/pallas_call | solution.py:391
  12.5 1.0 %prepare.1 = (bf16[1024,256]{1,0:T(8,128)(2,1)S(1)}, bf16[128,128]{1,0:T(8,128)(2,1)S(1)}, bf16[768,128]{1,0:T(8,128)(2,1)S(1)}, bf16[16,128]{1,0:T(8,128)(2,1)S(1)}) custom-call(s32[1,2048]{1,0:T(1,128)S(1)} %copy-done.5, s32[1,128]{1,0:T(1,128)S(1)} %bitcast.14, s32[1,128]{1,0:T(1,128)S(1)} %copy-done.11, s32[1,2,16]{2,1,0:T(2,128)S(1)} %copy-done.8), custom_call_target="tpu_custom_call" | custom-call | flops 1000000000 | bytes 1048576 | tf_op jit(solution)/shard_map/prepare/pallas_call | solution.py:391
  13.5 2.2 %ends_pick.1 = (bf16[128,2048]{1,0:T(8,128)(2,1)S(1)}, bf16[208,128]{1,0:T(8,128)(2,1)S(1)}, bf16[208,128]{1,0:T(8,128)(2,1)S(1)}) custom-call(s32[4]{0:T(128)S(1)} %pad_add_fusion.place, bf16[128,2048]{1,0:T(8,128)(2,1)S(1)} %get-tuple-element.34.inner, bf16[128,2048]{1,0:T(8,128)(2,1)S(1)} %turn.1.rows_t.refs_0_, ...), custom_call_target="tpu_custom_call" | custom-call | flops 1000000000 | bytes 1048576 | tf_op jit(solution)/shard_map/ends_pick/pallas_call | solution.py:391
  15.7 1.5 %collective-permute-start.2 = (bf16[208,128]{1,0:T(8,128)(2,1)S(1)}, bf16[208,128]{1,0:T(8,128)(2,1)S(1)}, u32[]{:S(2)}, u32[]{:S(2)}) collective-permute-start(bf16[208,128]{1,0:T(8,128)(2,1)S(1)} %get-tuple-element.42), channel_id=1, source_target_pairs={{0,1},{1,0},{2,3},{3,2},{4,5},{5,4},{6,7},{7,6},{8,9},{9,8},{10,11... | collective-permute-start | bytes 159752 | tf_op jit(solution)/shard_map/ppermute | solution.py:432
  17.3 0.7 collective-permute-start.3
  17.9 3.9 %inner.3 = (bf16[128,2048]{1,0:T(8,128)(2,1)S(1)}, bf16[256,128]{1,0:T(8,128)(2,1)S(1)}, bf16[128,256]{1,0:T(8,128)(2,1)S(1)}, bf16[128,128]{1,0:T(8,128)(2,1)S(1)}) custom-call(bf16[128,2048]{1,0:T(8,128)(2,1)S(1)} %get-tuple-element.40.rows_t.refs_0_, bf16[4,6,128,128]{3,2,1,0:T(8,128)(2,1)S(1)} %copy-done, s32[1,12288]{1,0:T(1,128)S(1)} %copy-done.2, ...), custom_call_target="tpu_custom_call" | custom-call | flops 4000000000 | bytes 1048576 | tf_op jit(solution)/shard_map/inner/pallas_call | solution.py:391
  21.9 0.8 collective-permute-done.3.refs_2_.early_far
  22.6 3.2 %ends_pool.1 = (bf16[128,2048]{1,0:T(8,128)(2,1)S(1)}, bf16[1024,128]{1,0:T(8,128)(2,1)}) custom-call(s32[4]{0:T(128)S(1)} %pad_add_fusion.place, bf16[128,2048]{1,0:T(8,128)(2,1)S(1)} %get-tuple-element.41.inner, bf16[128,2048]{1,0:T(8,128)(2,1)S(1)} %get-tuple-element.40.rows_t.refs_0_, bf16[208,128]{1,0:T(8,128)(2,1)S(1)} %collective-permute-done.2.refs_1_.early_near, ...), custom_call_target="tpu_custom_call" | custom-call | flops 1000000000 | bytes 1048576 | tf_op jit(solution)/shard_map/ends_pool/pallas_call | solution.py:391
  25.8 14.0 %all-to-all-start = ((bf16[64,16,128]{2,1,0:T(8,128)(2,1)}), bf16[64,16,128]{2,1,0:T(8,128)(2,1)S(1)}, u32[]{:S(2)}, u32[]{:S(2)}) async-start(bf16[64,16,128]{2,1,0:T(8,128)(2,1)} %bitcast.7), calls=%async_computation | async-start | bytes 524288 | tf_op jit(solution)/shard_map/all_to_all | solution.py:490
  39.8 0.9 pick.1
  40.8 3.3 %collective-permute-start.8 = (bf16[128,128]{1,0:T(8,128)(2,1)S(1)}, bf16[128,128]{1,0:T(8,128)(2,1)S(1)}, u32[]{:S(2)}, u32[]{:S(2)}) collective-permute-start(bf16[128,128]{1,0:T(8,128)(2,1)S(1)} %get-tuple-element.53), channel_id=1, source_target_pairs={{0,255},{1,2},{2,1},{3,4},{4,3},{5,6},{6,5},{7,8},{8,7},{9,10},{10... | collective-permute-start | bytes 98312 | tf_op jit(solution)/shard_map/ppermute | solution.py:433
  44.1 9.8 %all-to-all-done = bf16[64,16,128]{2,1,0:T(8,128)(2,1)S(1)} async-done(((bf16[64,16,128]{2,1,0:T(8,128)(2,1)}), bf16[64,16,128]{2,1,0:T(8,128)(2,1)S(1)}, u32[]{:S(2)}, u32[]{:S(2)}) %all-to-all-start) | async-done | bytes 262176 | tf_op jit(solution)/shard_map/all_to_all | solution.py:490
  53.9 1.3 %received.1 = (bf16[176,128]{1,0:T(8,128)(2,1)S(1)}, bf16[64,128]{1,0:T(8,128)(2,1)S(1)}) custom-call(s32[4]{0:T(128)S(1)} %pad_add_fusion.place, bf16[1024,128]{1,0:T(8,128)(2,1)S(1)} %bitcast.10), custom_call_target="tpu_custom_call" | custom-call | flops 1000000000 | bytes 1048576 | tf_op jit(solution)/shard_map/received/pallas_call | solution.py:391
  55.3 2.9 %collective-permute-start.6 = (bf16[176,128]{1,0:T(8,128)(2,1)S(1)}, bf16[176,128]{1,0:T(8,128)(2,1)S(1)}, u32[]{:S(2)}, u32[]{:S(2)}) collective-permute-start(bf16[176,128]{1,0:T(8,128)(2,1)S(1)} %get-tuple-element.50.own), channel_id=1, source_target_pairs={{0,3},{1,2},{2,1},{3,0},{4,7},{5,6},{6,5},{7,4},{8,11},{9,10},{10,... | collective-permute-start | bytes 135176 | tf_op jit(solution)/shard_map/ppermute | solution.py:502
  58.2 0.8 collective-permute-start.4
  58.9 0.5 ready.1
  59.4 0.6 collective-permute-done.6.other3
  60.1 2.0 %collective-permute-done.5.other2 = bf16[176,128]{1,0:T(8,128)(2,1)S(1)} collective-permute-done((bf16[176,128]{1,0:T(8,128)(2,1)S(1)}, bf16[176,128]{1,0:T(8,128)(2,1)S(1)}, u32[]{:S(2)}, u32[]{:S(2)}) %collective-permute-start.5) | collective-permute-done | bytes 45088 | tf_op jit(solution)/shard_map/ppermute | solution.py:502
  62.0 1.7 %coarse.1 = (bf16[128,128]{1,0:T(8,128)(2,1)}, bf16[768,128]{1,0:T(8,128)(2,1)S(1)}) custom-call(bf16[176,128]{1,0:T(8,128)(2,1)S(1)} %get-tuple-element.50.own, bf16[176,128]{1,0:T(8,128)(2,1)S(1)} %collective-permute-done.4.other1, bf16[176,128]{1,0:T(8,128)(2,1)S(1)} %collective-permute-done.5.other2, bf16[176,128]{1,0:T(8,128)(2,1)S(1)} %collective-permute-done.6.other3, ...), custom_call_target="tpu_custom_call" | custom-call | flops 1000000000 | bytes 1048576 | tf_op jit(solution)/shard_map/coarse/pallas_call | solution.py:391
  63.8 21.7 %all_to_all.10 = bf16[64,12,128]{2,1,0:T(8,128)(2,1)S(1)} all-to-all(bf16[64,12,128]{2,1,0:T(8,128)(2,1)S(1)} %reshape.23), channel_id=1, replica_groups=mesh['dom'=64,'sub'=4] {'dom'}, dimensions={0} | all-to-all | bytes 393216 | tf_op jit(solution)/shard_map/all_to_all | solution.py:490
  85.5 6.1 %final.1 = bf16[2048,128]{1,0:T(8,128)(2,1)} custom-call(s32[4]{0:T(128)S(1)} %pad_add_fusion.place, bf16[128,2048]{1,0:T(8,128)(2,1)S(1)} %get-tuple-element.48.rows_t, bf16[768,128]{1,0:T(8,128)(2,1)S(1)} %reshape.24.reply, bf16[768,128]{1,0:T(8,128)(2,1)S(1)} %get-tuple-element.61.slot_of, s32[1,2048]{1,0:T(1,128)S(1)} %copy-done.5, ...), custom_call_target="tpu_custom_call" | custom-call | flops 5000000000 | bytes 1048576 | tf_op jit(solution)/shard_map/final/pallas_call | solution.py:391
  (37 shorter events, 0.4 us)
Async XLA Ops:
  0.6 7.5 %copy-start.1 = (bf16[2048,128]{1,0:T(8,128)(2,1)S(1)}, bf16[2048,128]{1,0:T(8,128)(2,1)}, u32[]{:S(2)}) copy-start(bf16[2048,128]{1,0:T(8,128)(2,1)} %nodes.1) | copy-start | bytes 1572868
  2.3 6.2 %copy-start = (bf16[4,6,128,128]{3,2,1,0:T(8,128)(2,1)S(1)}, bf16[4,6,128,128]{3,2,1,0:T(8,128)(2,1)}, u32[]{:S(2)}) copy-start(bf16[4,6,128,128]{3,2,1,0:T(8,128)(2,1)} %weights.5) | copy-start | bytes 2359300
  2.3 6.2 %copy-start.2 = (s32[1,12288]{1,0:T(1,128)S(1)}, s32[1,12288]{1,0:T(1,128)}, u32[]{:S(2)}) copy-start(s32[1,12288]{1,0:T(1,128)} %src.7) | copy-start | bytes 147460
  2.3 6.2 %copy-start.3 = (s32[1,12288]{1,0:T(1,128)S(1)}, s32[1,12288]{1,0:T(1,128)}, u32[]{:S(2)}) copy-start(s32[1,12288]{1,0:T(1,128)} %dst.7) | copy-start | bytes 147460
  2.3 6.1 %copy-start.4 = (s32[1,12288]{1,0:T(1,128)S(1)}, s32[1,12288]{1,0:T(1,128)}, u32[]{:S(2)}) copy-start(s32[1,12288]{1,0:T(1,128)} %valid.5) | copy-start | bytes 147460
  2.3 11.2 %collective-permute-start.1 = (bf16[128,128]{1,0:T(8,128)(2,1)S(1)}, bf16[128,128]{1,0:T(8,128)(2,1)S(1)}, u32[]{:S(2)}, u32[]{:S(2)}) collective-permute-start(bf16[128,128]{1,0:T(8,128)(2,1)S(1)} %get-tuple-element.66), channel_id=1, source_target_pairs={{0,255},{1,2},{2,1},{3,4},{4,3},{5,6},{6,5},{7,8},{8,7},{9,10},{10... | collective-permute-start | bytes 98312 | tf_op jit(solution)/shard_map/ppermute | solution.py:433
  8.1 5.4 %collective-permute-start = (bf16[128,128]{1,0:T(8,128)(2,1)S(1)}, bf16[128,128]{1,0:T(8,128)(2,1)S(1)}, u32[]{:S(2)}, u32[]{:S(2)}) collective-permute-start(bf16[128,128]{1,0:T(8,128)(2,1)S(1)} %get-tuple-element.67), channel_id=1, source_target_pairs={{0,1},{1,0},{2,3},{3,2},{4,5},{5,4},{6,7},{7,6},{8,9},{9,8},{10,11... | collective-permute-start | bytes 98312 | tf_op jit(solution)/shard_map/ppermute | solution.py:432
  8.5 4.0 %copy-start.5 = (s32[1,2048]{1,0:T(1,128)S(1)}, s32[1,2048]{1,0:T(1,128)}, u32[]{:S(2)}) copy-start(s32[1,2048]{1,0:T(1,128)} %cluster.3) | copy-start | bytes 24580
  8.5 4.0 %copy-start.8 = (s32[1,2,16]{2,1,0:T(2,128)S(1)}, s32[1,2,16]{2,1,0:T(2,128)}, u32[]{:S(2)}) copy-start(s32[1,2,16]{2,1,0:T(2,128)} %ghosts.1) | copy-start | bytes 388
  8.5 4.0 %copy-start.10 = (s32[1,128,1]{1,2,0:T(1,128)S(1)}, s32[1,128,1]{1,2,0:T(1,128)}, u32[]{:S(2)}) copy-start(s32[1,128,1]{1,2,0:T(1,128)} %param.19) | copy-start | bytes 1540
  8.5 4.0 %copy-start.11 = (s32[1,128]{1,0:T(1,128)S(1)}, s32[1,128]{1,0:T(1,128)}, u32[]{:S(2)}) copy-start(s32[1,128]{1,0:T(1,128)} %coarse_row.1) | copy-start | bytes 1540
  12.5 1.1 %copy-start.9 = (s32[1,2,128]{2,1,0:T(2,128)S(1)}, s32[1,2,128]{2,1,0:T(2,128)}, u32[]{:S(2)}) copy-start(s32[1,2,128]{2,1,0:T(2,128)} %param.17) | copy-start | bytes 3076
  15.7 6.1 %collective-permute-start.2 = (bf16[208,128]{1,0:T(8,128)(2,1)S(1)}, bf16[208,128]{1,0:T(8,128)(2,1)S(1)}, u32[]{:S(2)}, u32[]{:S(2)}) collective-permute-start(bf16[208,128]{1,0:T(8,128)(2,1)S(1)} %get-tuple-element.42), channel_id=1, source_target_pairs={{0,1},{1,0},{2,3},{3,2},{4,5},{5,4},{6,7},{7,6},{8,9},{9,8},{10,11... | collective-permute-start | bytes 159752 | tf_op jit(solution)/shard_map/ppermute | solution.py:432
  17.3 5.4 %collective-permute-start.3 = (bf16[208,128]{1,0:T(8,128)(2,1)S(1)}, bf16[208,128]{1,0:T(8,128)(2,1)S(1)}, u32[]{:S(2)}, u32[]{:S(2)}) collective-permute-start(bf16[208,128]{1,0:T(8,128)(2,1)S(1)} %get-tuple-element.43), channel_id=1, source_target_pairs={{0,255},{1,2},{2,1},{3,4},{4,3},{5,6},{6,5},{7,8},{8,7},{9,10},{10... | collective-permute-start | bytes 159752 | tf_op jit(solution)/shard_map/ppermute | solution.py:433
  25.8 28.1 %all-to-all-start = ((bf16[64,16,128]{2,1,0:T(8,128)(2,1)}), bf16[64,16,128]{2,1,0:T(8,128)(2,1)S(1)}, u32[]{:S(2)}, u32[]{:S(2)}) async-start(bf16[64,16,128]{2,1,0:T(8,128)(2,1)} %bitcast.7), calls=%async_computation | async-start | bytes 524288 | tf_op jit(solution)/shard_map/all_to_all | solution.py:490
  40.7 18.3 %collective-permute-start.7 = (bf16[128,128]{1,0:T(8,128)(2,1)S(1)}, bf16[128,128]{1,0:T(8,128)(2,1)S(1)}, u32[]{:S(2)}, u32[]{:S(2)}) collective-permute-start(bf16[128,128]{1,0:T(8,128)(2,1)S(1)} %get-tuple-element.52), channel_id=1, source_target_pairs={{0,1},{1,0},{2,3},{3,2},{4,5},{5,4},{6,7},{7,6},{8,9},{9,8},{10,11... | collective-permute-start | bytes 98312 | tf_op jit(solution)/shard_map/ppermute | solution.py:432
  40.8 18.2 %collective-permute-start.8 = (bf16[128,128]{1,0:T(8,128)(2,1)S(1)}, bf16[128,128]{1,0:T(8,128)(2,1)S(1)}, u32[]{:S(2)}, u32[]{:S(2)}) collective-permute-start(bf16[128,128]{1,0:T(8,128)(2,1)S(1)} %get-tuple-element.53), channel_id=1, source_target_pairs={{0,255},{1,2},{2,1},{3,4},{4,3},{5,6},{6,5},{7,8},{8,7},{9,10},{10... | collective-permute-start | bytes 98312 | tf_op jit(solution)/shard_map/ppermute | solution.py:433
  53.9 5.0 %copy-start.6 = (s32[1,768]{1,0:T(1,128)S(1)}, s32[1,768]{1,0:T(1,128)}, u32[]{:S(2)}) copy-start(s32[1,768]{1,0:T(1,128)} %src.6) | copy-start | bytes 9220
  53.9 5.0 %copy-start.7 = (s32[1,768]{1,0:T(1,128)S(1)}, s32[1,768]{1,0:T(1,128)}, u32[]{:S(2)}) copy-start(s32[1,768]{1,0:T(1,128)} %dst.6) | copy-start | bytes 9220
  55.3 4.8 %collective-permute-start.6 = (bf16[176,128]{1,0:T(8,128)(2,1)S(1)}, bf16[176,128]{1,0:T(8,128)(2,1)S(1)}, u32[]{:S(2)}, u32[]{:S(2)}) collective-permute-start(bf16[176,128]{1,0:T(8,128)(2,1)S(1)} %get-tuple-element.50.own), channel_id=1, source_target_pairs={{0,3},{1,2},{2,1},{3,0},{4,7},{5,6},{6,5},{7,4},{8,11},{9,10},{10,... | collective-permute-start | bytes 135176 | tf_op jit(solution)/shard_map/ppermute | solution.py:502
  58.1 3.9 %collective-permute-start.5 = (bf16[176,128]{1,0:T(8,128)(2,1)S(1)}, bf16[176,128]{1,0:T(8,128)(2,1)S(1)}, u32[]{:S(2)}, u32[]{:S(2)}) collective-permute-start(bf16[176,128]{1,0:T(8,128)(2,1)S(1)} %get-tuple-element.50.own), channel_id=1, source_target_pairs={{0,2},{1,3},{2,0},{3,1},{4,6},{5,7},{6,4},{7,5},{8,10},{9,11},{10,... | collective-permute-start | bytes 135176 | tf_op jit(solution)/shard_map/ppermute | solution.py:502
  58.2 3.9 %collective-permute-start.4 = (bf16[176,128]{1,0:T(8,128)(2,1)S(1)}, bf16[176,128]{1,0:T(8,128)(2,1)S(1)}, u32[]{:S(2)}, u32[]{:S(2)}) collective-permute-start(bf16[176,128]{1,0:T(8,128)(2,1)S(1)} %get-tuple-element.50.own), channel_id=1, source_target_pairs={{0,1},{1,0},{2,3},{3,2},{4,5},{5,4},{6,7},{7,6},{8,9},{9,8},{10,11... | collective-permute-start | bytes 135176 | tf_op jit(solution)/shard_map/ppermute | solution.py:502

commit v4 on v3

--- a/solution.py
+++ b/solution.py
@@ -20,6 +20,7 @@
 SLOTS = 16
 BACK = 3 * CAP
 VMEM_LIMIT = 28 << 20
+FINAL_PARTS = 2
 
 
 def dot(left, right, dims=NN):
@@ -51,10 +52,20 @@
     return (row * (65536 // BACK + 1)) >> 16
 
 
-def edge_sum(source_t, target_t, from_hot, to_hot):
+def edge_halves(source_t, target_t, from_hot, to_hot):
     table = jnp.concatenate([source_t, target_t], axis=1)
-    half = dot(table, jnp.concatenate([from_hot, to_hot], axis=0))
+    return dot(table, jnp.concatenate([from_hot, to_hot], axis=0)), to_hot
+
+
+def edge_sum(half, to_hot):
     return dot(half_silu(half).astype(BF), to_hot, NT).astype(BF)
+
+
+def edge_sums(first, last, halves, sums):
+    ahead = halves(first)
+    for b in range(first, last):
+        now, ahead = ahead, halves(b + 1) if b + 1 < last else None
+        sums[:, b * GH : (b + 1) * GH] = edge_sum(*now)
 
 
 def layer_weights(w):
@@ -65,11 +76,14 @@
     return first.astype(BF), both.astype(BF), last.T.astype(BF)
 
 
-def node_update(rows_t, sums_t, both, last):
-    half = dot(both, jnp.concatenate([rows_t, sums_t], axis=0))
-    centred = dot(last, half_silu(half).astype(BF))
-    spread = jnp.mean(centred * centred, axis=0, keepdims=True)
-    return (rows_t.astype(F32) + centred * lax.rsqrt(spread + 1e-5)).astype(BF)
+def node_updates(pieces, both, last):
+    halves = [dot(both, jnp.concatenate(piece, axis=0)) for piece in pieces]
+    centred = [dot(last, half_silu(half).astype(BF)) for half in halves]
+    new = []
+    for (rows_t, _), piece in zip(pieces, centred):
+        spread = jnp.mean(piece * piece, axis=0, keepdims=True)
+        new.append((rows_t.astype(F32) + piece * lax.rsqrt(spread + 1e-5)).astype(BF))
+    return new
 
 
 def local_edges(b, row_count, src, dst, valid, width):
@@ -98,17 +112,20 @@
     width = src.shape[1] // blocks
     first[...], both[...], last[...] = layer_weights([weights[layer, i] for i in range(6)])
     ends[...] = dot(first[...], rows_t[...]).astype(BF)
-    for b in range(1, blocks - 1):
-        at = slice(b * GH, (b + 1) * GH)
-        sums[:, at] = edge_sum(
+
+    def halves(b):
+        return edge_halves(
             ends[0:128, (b - 1) * GH : (b + 2) * GH],
-            ends[128:256, at],
+            ends[128:256, b * GH : (b + 1) * GH],
             *local_edges(b, row_count, src, dst, valid, width),
         )
+
+    edge_sums(1, blocks - 1, halves, sums)
     step = (row_count - 2 * GH) // 2
-    for start in range(GH, row_count - GH, step):
-        at = slice(start, start + step)
-        out[:, at] = node_update(rows_t[:, at], sums[:, at], both[...], last[...])
+    ranges = [slice(start, start + step) for start in (GH, GH + step)]
+    pieces = [(rows_t[:, at], sums[:, at]) for at in ranges]
+    for at, new in zip(ranges, node_updates(pieces, both[...], last[...])):
+        out[:, at] = new
 
 
 def by_side(place, near, far):
@@ -121,19 +138,16 @@
     return jnp.where(place[2] == 0, nothing, before), jnp.where(place[3] == 0, nothing, after)
 
 
-def end_blocks(place, rows_t, from_near, from_far, first, both, last, src, dst, valid, turn=False):
+def end_blocks(place, rows_t, ghosts, first, both, last, src, dst, valid):
     row_count = rows_t.shape[1]
     blocks = row_count // GH
     width = src.shape[1] // blocks
-    before, after = by_side(place, from_near[0:128, :], from_far[0:128, :])
-    before, after = ghost_rows(place, before, after)
-    if turn:
-        before, after = before.T, after.T
+    before, after = ghost_rows(place, *ghosts)
     head, tail = rows_t[:, 0 : 2 * GH], rows_t[:, row_count - 2 * GH :]
     line = jnp.concatenate([before, head, tail, after], axis=1)
     ends = dot(first[...], line).astype(BF)
-    sums = [
-        edge_sum(
+    halves = [
+        edge_halves(
             ends[0:128, at : at + 3 * GH],
             ends[128:256, at + own : at + own + GH],
             *local_edges(b, row_count, src, dst, valid, width),
@@ -141,7 +155,8 @@
         for b, at, own in ((0, 0, GH), (blocks - 1, 3 * GH, GH))
     ]
     own = jnp.concatenate([head[:, :GH], tail[:, GH:]], axis=1)
-    return node_update(own, jnp.concatenate(sums, axis=1), both[...], last[...])
+    sums = jnp.concatenate([edge_sum(*half) for half in halves], axis=1)
+    return node_updates([(own, sums)], both[...], last[...])[0]
 
 
 def whole_layer(inner, new, out):
@@ -154,7 +169,8 @@
 def ends_pick_kernel(place, inner, *refs):
     lists, cluster, facts, slot_row, out, near, far, more = refs[-8:]
     slots = dot(slot_row[...], rows_hot(cluster[...], 128)).astype(BF)
-    whole_layer(inner, end_blocks(place, *refs[:-8], turn=True), out)
+    ghosts = [rows.T for rows in by_side(place, refs[1][...], refs[2][...])]
+    whole_layer(inner, end_blocks(place, refs[0], ghosts, *refs[3:-8]), out)
     more[0:128, :] = out[...]
     more[128:144, :] = slots
     pick_both(more, lists, place[1] % 2 == 1, near, far)
@@ -164,10 +180,11 @@
 
 def ends_pool_kernel(place, inner, *refs):
     cluster, slot_pick, facts, out, parcel = refs[-5:]
-    whole_layer(inner, end_blocks(place, *refs[:-5]), out)
+    ghosts = by_side(place, refs[2][0:128, :], refs[1][0:128, :])
+    whole_layer(inner, end_blocks(place, refs[0], ghosts, *refs[3:-5]), out)
     member = rows_hot(cluster[...], 128)
     partial = dot(out[...], member, NT).T.astype(BF)
-    ids = by_side(place, refs[1][144:208, :], refs[2][144:208, :])
+    ids = by_side(place, refs[2][144:208, :], refs[1][144:208, :])
     lane = iota(ids[0].shape, 1)
     moved = [pltpu.roll(ids[side].astype(F32), CAP * (3 + side), 1) for side in (0, 1)]
     moved = [jnp.where(lane // CAP == 3 + side, moved[side], 0.0) for side in (0, 1)]
@@ -182,8 +199,13 @@
     rows_t[...] = nodes[...].T
 
 
-def pick_kernel(place, rows_t, lists, near, far):
+def pick_kernel(place, rows_t, lists, near, far, meta_pick, spread):
     pick_both(rows_t, lists, place[1] % 2 == 1, near, far)
+    count, total = meta_pick.shape
+    owners = count // 3
+    wide, pick = iota((count, total), 1), iota((count, total), 0)
+    meta_pick[...] = hot(wide == SLOTS * (pick % owners) + 3 * CAP + pick // owners)
+    spread[...] = hot((wide // SLOTS == pick % owners) & (wide % SLOTS // CAP == pick // owners))
 
 
 def prepare_kernel(cluster, owner, coarse_row, ghosts, slot_pick, facts, slot_of, slot_row_out):
@@ -242,18 +264,13 @@
     facts[...] = jnp.where(sub == 127, listed, meta).astype(BF)
 
 
-def received_kernel(place, got, part, own_metas):
+def received_kernel(place, got, meta_pick, spread, part, own_metas):
     total = got.shape[0]
     owners = total // SLOTS
     here = place[0]
-    wide = iota((3 * owners, total), 1)
-    pick = iota((3 * owners, total), 0)
-    metas = dot(
-        hot(wide == SLOTS * (pick % owners) + 3 * CAP + pick // owners), got[...]
-    ).astype(BF)
+    metas = dot(meta_pick[...], got[...]).astype(BF)
     own_metas[...] = metas[0:owners]
-    spread = hot((wide // SLOTS == pick % owners) & (wide % SLOTS // CAP == pick // owners))
-    facts = dot(metas, spread, TN)[0:16]
+    facts = dot(metas, spread[...], TN)[0:16]
     lane = iota((1, total), 1)
     turn = iota((16, total), 0) - iota((16, total), 1) % CAP
 
@@ -328,7 +345,7 @@
     ends = dot(first[...], jnp.concatenate([rows_t, ghosts_t], axis=1)).astype(BF)
     half = dot(ends[0:128, 0:160], from_hot[...]) + dot(ends[128:256, 0:128], to_hot[...])
     sums = dot(half_silu(half).astype(BF), to_hot[...], NT).astype(BF)
-    new = node_update(rows_t, sums, both[...], last[...]).T
+    new = node_updates([(rows_t, sums)], both[...], last[...])[0].T
     out[...] = new
     reply[...] = dot(back[...], new).astype(BF)
 
@@ -339,10 +356,10 @@
     reply,
     slot_of,
     cluster,
+    early_far,
     early_near,
-    early_far,
+    from_far,
     from_near,
-    from_far,
     first,
     both,
     last,
@@ -353,6 +370,8 @@
     line,
     ends,
     sums,
+    done,
+    sems,
 ):
     row_count = rows_t.shape[1]
     blocks = row_count // GH
@@ -371,20 +390,33 @@
         rows_t[...].astype(F32) + dot(coarse[:, 0:128].astype(BF), member)
     ).astype(BF)
     ends[...] = dot(first[...], line[...]).astype(BF)
-    for b in range(blocks):
-        sums[:, b * GH : (b + 1) * GH] = edge_sum(
+    parts = sems.shape[0]
+    step = row_count // parts
+    copies = []
+
+    def halves(b):
+        return edge_halves(
             ends[0:128, b * GH : (b + 3) * GH],
             ends[128:256, (b + 1) * GH : (b + 2) * GH],
             *local_edges(b, row_count, src, dst, valid, width),
         )
-    step = row_count // 2
-    for start in range(0, row_count, step):
-        own = line[:, GH + start : GH + start + step]
-        new = node_update(own, sums[:, start : start + step], both[...], last[...])
-        out[start : start + step, :] = new.T
-
-
-def run(kernel, outs, args, scalars=0, layer=None, scratch=(), flops=0, name=None):
+
+    edge_sums(0, blocks, halves, sums)
+    starts = [part * step for part in range(parts)]
+    pieces = [
+        (line[:, GH + start : GH + start + step], sums[:, start : start + step]) for start in starts
+    ]
+    for part, new in enumerate(node_updates(pieces, both[...], last[...])):
+        start = starts[part]
+        at = pl.ds(start, step)
+        done[at, :] = new.T
+        copies.append(pltpu.make_async_copy(done.at[at, :], out.at[at, :], sems.at[part]))
+        copies[-1].start()
+    for copy in copies:
+        copy.wait()
+
+
+def run(kernel, outs, args, scalars=0, layer=None, scratch=(), flops=0, out_space=pltpu.VMEM, name=None):
     specs = []
     for i in range(len(args)):
         specs.append(pl.BlockSpec(memory_space=pltpu.SMEM if i < scalars else pltpu.VMEM))
@@ -392,7 +424,7 @@
         kernel if layer is None else functools.partial(kernel, layer),
         out_shape=[jax.ShapeDtypeStruct(shape, BF) for shape in outs],
         in_specs=specs,
-        out_specs=[pl.BlockSpec(memory_space=pltpu.VMEM) for _ in outs],
+        out_specs=[pl.BlockSpec(memory_space=out_space) for _ in outs],
         scratch_shapes=scratch,
         compiler_params=pltpu.CompilerParams(vmem_limit_bytes=VMEM_LIMIT),
         cost_estimate=pl.CostEstimate(flops=flops, bytes_accessed=1 << 20, transcendentals=0),
@@ -429,9 +461,9 @@
     far_pairs = [(i, (i + 1 if i % 2 else i - 1) % chain) for i in range(chain)]
 
     def swap(near, far):
+        from_far = lax.ppermute(far, ("dom", "sub"), far_pairs)
         from_near = lax.ppermute(near, ("dom", "sub"), near_pairs)
-        from_far = lax.ppermute(far, ("dom", "sub"), far_pairs)
-        return from_near, from_far
+        return from_far, from_near
 
     def inner(states, layer):
         out, *weights_now = run(
@@ -464,7 +496,7 @@
     states, near, far = run(
         ends_pick_kernel,
         [rows_t, early, early],
-        (place, middle, states) + ghosts + now + edges + (lists, cluster_of, facts, slot_row),
+        (place, middle, states) + ghosts[::-1] + now + edges + (lists, cluster_of, facts, slot_row),
         scalars=1,
         scratch=[pltpu.VMEM((width + 16, count), BF)],
         flops=10**9,
@@ -480,9 +512,15 @@
         flops=10**9,
         name="ends_pool",
     )
-    ghosts = swap(
-        *run(pick_kernel, [ghost, ghost], (place, states, lists), scalars=1, flops=10**9, name="pick")
-    )
+    near, far, meta_pick, spread = run(
+        pick_kernel,
+        [ghost, ghost] + [(3 * doms, doms * SLOTS)] * 2,
+        (place, states, lists),
+        scalars=1,
+        flops=10**9,
+        name="pick",
+    )
+    ghosts = swap(near, far)
 
     def exchange(rows):
         shape = rows.shape
@@ -493,14 +531,12 @@
     part, own_metas = run(
         received_kernel,
         [(176, width), (doms, width)],
-        (place, exchange(parcel)),
+        (place, exchange(parcel), meta_pick, spread),
         scalars=1,
         flops=10**9,
         name="received",
     )
-    others = {
-        k: lax.ppermute(part, "sub", [(i, i ^ k) for i in range(subs)]) for k in (1, 3, 2)
-    }
+    others = [lax.ppermute(part, "sub", [(i, i ^ k) for i in range(subs)]) for k in (1, 2, 3)]
     back, *ready = run(
         ready_kernel,
         [(doms * BACK, width)]
@@ -514,7 +550,7 @@
     coarse, reply = run(
         coarse_kernel,
         [(128, width), (doms * BACK, width)],
-        (part, others[1], others[2], others[3], back, *ready[:5]),
+        (part, *others, back, *ready[:5]),
         flops=10**9,
         name="coarse",
     )
@@ -527,7 +563,10 @@
             pltpu.VMEM((width, count + 2 * GH), BF),
             pltpu.VMEM((2 * width, count + 2 * GH), BF),
             pltpu.VMEM(rows_t, BF),
+            pltpu.VMEM(nodes.shape, BF),
+            pltpu.SemaphoreType.DMA((FINAL_PARTS,)),
         ],
+        out_space=pl.ANY,
         flops=5 * 10**9,
         name="final",
     )

time: 92.7 us -> 91.2 us (0.984)
  Pallas kernels: 24.9 us -> 22.6 us
  starting transfers between devices: 29 us -> 31.2 us
  waiting for transfers between devices: 13.2 us -> 12 us
    pallas_call x11, Pallas kernels: 24.9 us -> 22.6 us  [run(): pl.pallas_call(kernel if layer is None else functools.partial(kernel, lay...]
    all_to_all x1, waiting for transfers between devices: 9.83 us -> 7.62 us  [exchange(): rows = lax.all_to_all(rows, 'dom', split_axis=0, concat_axis=0, tiled=True)]
    ppermute x3, starting transfers between devices: 9.81 us -> 11.8 us  [swap(): from_far = lax.ppermute(far, ('dom', 'sub'), far_pairs)]
    ppermute x3, starting transfers between devices: 3.63 us -> 5.4 us  [on_device(): lax.ppermute(part, 'sub', [(i, i ^ k) for i in range(subs)])]
    all_to_all x1, starting transfers between devices: 14 us -> 12.9 us  [exchange(): rows = lax.all_to_all(rows, 'dom', split_axis=0, concat_axis=0, tiled=True)]
  transfers between devices with their start and end apart: 10 -> 10, of which waited for: 4 -> 4; matrix products, arithmetic and copies ran while one was open for 0% -> 0% of each run, Pallas kernels for 13% -> 12%
where the time goes in v4:
time: 91.2 us; the launch traced here: 90.3 us
  starting transfers between devices  31.2 us (34%)
  Pallas kernels  22.6 us (25%)
  blocking collectives  21.6 us (24%)
  waiting for transfers between devices  12 us (13%)
  matrix products  1.6 us (2%)
  between operations  1.08 us (1%)
    pallas_call x11, Pallas kernels, run(): pl.pallas_call(kernel if layer is None else functools.partial(kernel, lay...  22.6 us
    all_to_all x1, blocking collectives, exchange(): rows = lax.all_to_all(rows, 'dom', split_axis=0, concat_axis=0, tiled=True)  21.6 us
    all_to_all x1, starting transfers between devices, exchange(): rows = lax.all_to_all(rows, 'dom', split_axis=0, concat_axis=0, tiled=True)  12.9 us
    ppermute x3, starting transfers between devices, swap(): from_far = lax.ppermute(far, ('dom', 'sub'), far_pairs)  11.8 us
    all_to_all x1, waiting for transfers between devices, exchange(): rows = lax.all_to_all(rows, 'dom', split_axis=0, concat_axis=0, tiled=True)  7.62 us
    ppermute x3, starting transfers between devices, on_device(): lax.ppermute(part, 'sub', [(i, i ^ k) for i in range(subs)])  5.4 us
    ppermute x3, waiting for transfers between devices, on_device(): lax.ppermute(part, 'sub', [(i, i ^ k) for i in range(subs)])  3.48 us
  transfers between devices with their start and end apart: 10, of which 4 were waited for; matrix products, arithmetic and copies ran while one was open for 0% of the time, Pallas kernels for 12%

profile of v4, /device:TPU:1, one launch (start us, length us, event | category | flops | bytes accessed | tf_op | source)
XLA Modules:
  0.0 90.3 jit_solution(14421390745843805175)
XLA Ops:
  0.7 1.6 %fusion.1 = bf16[256,128]{1,0:T(8,128)(2,1)S(1)} fusion(bf16[2048,128]{1,0:T(8,128)(2,1)} %nodes.1, s32[256]{0:T(256)} %bitcast.11), kind=kOutput, calls=%fused_computation.2 | convolution fusion | flops 134774784 | bytes 590848 | tf_op jit(solution)/shard_map/dot_general | solution.py:27
  2.3 5.8 %collective-permute-start.1 = (bf16[128,128]{1,0:T(8,128)(2,1)S(1)}, bf16[128,128]{1,0:T(8,128)(2,1)S(1)}, u32[]{:S(2)}, u32[]{:S(2)}) collective-permute-start(bf16[128,128]{1,0:T(8,128)(2,1)S(1)} %get-tuple-element.70), channel_id=1, source_target_pairs={{0,255},{1,2},{2,1},{3,4},{4,3},{5,6},{6,5},{7,8},{8,7},{9,10},{10... | collective-permute-start | bytes 98312 | tf_op jit(solution)/shard_map/ppermute | solution.py:464
  8.5 3.2 %inner.2 = (bf16[128,2048]{1,0:T(8,128)(2,1)S(1)}, bf16[256,128]{1,0:T(8,128)(2,1)S(1)}, bf16[128,256]{1,0:T(8,128)(2,1)S(1)}, bf16[128,128]{1,0:T(8,128)(2,1)S(1)}) custom-call(bf16[128,2048]{1,0:T(8,128)(2,1)S(1)} %turn.1.rows_t.refs_0_, bf16[4,6,128,128]{3,2,1,0:T(8,128)(2,1)S(1)} %copy-done, s32[1,12288]{1,0:T(1,128)S(1)} %copy-done.2, ...), custom_call_target="tpu_custom_call" | custom-call | flops 4000000000 | bytes 1048576 | tf_op jit(solution)/shard_map/inner/pallas_call | solution.py:423
  11.8 1.0 %prepare.1 = (bf16[1024,256]{1,0:T(8,128)(2,1)S(1)}, bf16[128,128]{1,0:T(8,128)(2,1)S(1)}, bf16[768,128]{1,0:T(8,128)(2,1)S(1)}, bf16[16,128]{1,0:T(8,128)(2,1)S(1)}) custom-call(s32[1,2048]{1,0:T(1,128)S(1)} %copy-done.5, s32[1,128]{1,0:T(1,128)S(1)} %bitcast.14, s32[1,128]{1,0:T(1,128)S(1)} %copy-done.11, s32[1,2,16]{2,1,0:T(2,128)S(1)} %copy-done.8), custom_call_target="tpu_custom_call" | custom-call | flops 1000000000 | bytes 1048576 | tf_op jit(solution)/shard_map/prepare/pallas_call | solution.py:423
  12.8 2.1 %ends_pick.1 = (bf16[128,2048]{1,0:T(8,128)(2,1)S(1)}, bf16[208,128]{1,0:T(8,128)(2,1)S(1)}, bf16[208,128]{1,0:T(8,128)(2,1)S(1)}) custom-call(s32[4]{0:T(128)S(1)} %pad_add_fusion.place, bf16[128,2048]{1,0:T(8,128)(2,1)S(1)} %get-tuple-element.36.inner, bf16[128,2048]{1,0:T(8,128)(2,1)S(1)} %turn.1.rows_t.refs_0_, ...), custom_call_target="tpu_custom_call" | custom-call | flops 1000000000 | bytes 1048576 | tf_op jit(solution)/shard_map/ends_pick/pallas_call | solution.py:423
  14.9 0.8 collective-permute-start.2
  15.7 1.1 %collective-permute-start.3 = (bf16[208,128]{1,0:T(8,128)(2,1)S(1)}, bf16[208,128]{1,0:T(8,128)(2,1)S(1)}, u32[]{:S(2)}, u32[]{:S(2)}) collective-permute-start(bf16[208,128]{1,0:T(8,128)(2,1)S(1)} %get-tuple-element.45), channel_id=1, source_target_pairs={{0,1},{1,0},{2,3},{3,2},{4,5},{5,4},{6,7},{7,6},{8,9},{9,8},{10,11... | collective-permute-start | bytes 159752 | tf_op jit(solution)/shard_map/ppermute | solution.py:465
  16.8 3.2 %inner.3 = (bf16[128,2048]{1,0:T(8,128)(2,1)S(1)}, bf16[256,128]{1,0:T(8,128)(2,1)S(1)}, bf16[128,256]{1,0:T(8,128)(2,1)S(1)}, bf16[128,128]{1,0:T(8,128)(2,1)S(1)}) custom-call(bf16[128,2048]{1,0:T(8,128)(2,1)S(1)} %get-tuple-element.42.rows_t.refs_0_, bf16[4,6,128,128]{3,2,1,0:T(8,128)(2,1)S(1)} %copy-done, s32[1,12288]{1,0:T(1,128)S(1)} %copy-done.2, ...), custom_call_target="tpu_custom_call" | custom-call | flops 4000000000 | bytes 1048576 | tf_op jit(solution)/shard_map/inner/pallas_call | solution.py:423
  20.0 0.9 %collective-permute-done.2.refs_1_.early_far = bf16[208,128]{1,0:T(8,128)(2,1)S(1)} collective-permute-done((bf16[208,128]{1,0:T(8,128)(2,1)S(1)}, bf16[208,128]{1,0:T(8,128)(2,1)S(1)}, u32[]{:S(2)}, u32[]{:S(2)}) %collective-permute-start.2) | collective-permute-done | bytes 53280 | tf_op jit(solution)/shard_map/ppermute | solution.py:464
  20.9 3.1 %ends_pool.1 = (bf16[128,2048]{1,0:T(8,128)(2,1)S(1)}, bf16[1024,128]{1,0:T(8,128)(2,1)}) custom-call(s32[4]{0:T(128)S(1)} %pad_add_fusion.place, bf16[128,2048]{1,0:T(8,128)(2,1)S(1)} %get-tuple-element.43.inner, bf16[128,2048]{1,0:T(8,128)(2,1)S(1)} %get-tuple-element.42.rows_t.refs_0_, bf16[208,128]{1,0:T(8,128)(2,1)S(1)} %collective-permute-done.2.refs_1_.early_far, ...), custom_call_target="tpu_custom_call" | custom-call | flops 1000000000 | bytes 1048576 | tf_op jit(solution)/shard_map/ends_pool/pallas_call | solution.py:423
  24.0 12.9 %all-to-all-start = ((bf16[64,16,128]{2,1,0:T(8,128)(2,1)}), bf16[64,16,128]{2,1,0:T(8,128)(2,1)S(1)}, u32[]{:S(2)}, u32[]{:S(2)}) async-start(bf16[64,16,128]{2,1,0:T(8,128)(2,1)} %bitcast.7), calls=%async_computation | async-start | bytes 524288 | tf_op jit(solution)/shard_map/all_to_all | solution.py:528
  36.9 1.0 %pick.1 = (bf16[128,128]{1,0:T(8,128)(2,1)S(1)}, bf16[128,128]{1,0:T(8,128)(2,1)S(1)}, bf16[192,1024]{1,0:T(8,128)(2,1)S(1)}, bf16[192,1024]{1,0:T(8,128)(2,1)S(1)}) custom-call(s32[4]{0:T(128)S(1)} %pad_add_fusion.place, bf16[128,2048]{1,0:T(8,128)(2,1)S(1)} %get-tuple-element.50.rows_t, s32[2,128]{1,0:T(2,128)S(1)} %bitcast.13), custom_call_target="tpu_custom_call" | custom-call | flops 1000000000 | bytes 1048576 | tf_op jit(solution)/shard_map/pick/pallas_call | solution.py:423
  38.0 5.2 %collective-permute-start.7 = (bf16[128,128]{1,0:T(8,128)(2,1)S(1)}, bf16[128,128]{1,0:T(8,128)(2,1)S(1)}, u32[]{:S(2)}, u32[]{:S(2)}) collective-permute-start(bf16[128,128]{1,0:T(8,128)(2,1)S(1)} %get-tuple-element.56), channel_id=1, source_target_pairs={{0,255},{1,2},{2,1},{3,4},{4,3},{5,6},{6,5},{7,8},{8,7},{9,10},{10... | collective-permute-start | bytes 98312 | tf_op jit(solution)/shard_map/ppermute | solution.py:464
  43.2 7.6 %all-to-all-done = bf16[64,16,128]{2,1,0:T(8,128)(2,1)S(1)} async-done(((bf16[64,16,128]{2,1,0:T(8,128)(2,1)}), bf16[64,16,128]{2,1,0:T(8,128)(2,1)S(1)}, u32[]{:S(2)}, u32[]{:S(2)}) %all-to-all-start) | async-done | bytes 262176 | tf_op jit(solution)/shard_map/all_to_all | solution.py:528
  50.8 1.3 %received.1 = (bf16[176,128]{1,0:T(8,128)(2,1)S(1)}, bf16[64,128]{1,0:T(8,128)(2,1)S(1)}) custom-call(s32[4]{0:T(128)S(1)} %pad_add_fusion.place, bf16[1024,128]{1,0:T(8,128)(2,1)S(1)} %bitcast.10, bf16[192,1024]{1,0:T(8,128)(2,1)S(1)} %get-tuple-element.52.meta_pick, bf16[192,1024]{1,0:T(8,128)(2,1)S(1)} %get-tuple-element.53.spread), custom_call_target="tpu_custom_call" | custom-call | flops 1000000000 | bytes 1048576 | tf_op jit(solution)/shard_map/received/pallas_call | solution.py:423
  52.1 5.0 %collective-permute-start.6 = (bf16[176,128]{1,0:T(8,128)(2,1)S(1)}, bf16[176,128]{1,0:T(8,128)(2,1)S(1)}, u32[]{:S(2)}, u32[]{:S(2)}) collective-permute-start(bf16[176,128]{1,0:T(8,128)(2,1)S(1)} %get-tuple-element.54.own), channel_id=1, source_target_pairs={{0,3},{1,2},{2,1},{3,0},{4,7},{5,6},{6,5},{7,4},{8,11},{9,10},{10,... | collective-permute-start | bytes 135176 | tf_op jit(solution)/shard_map/ppermute | solution.py:539
  57.1 0.2 collective-permute-start.5
  57.3 0.2 collective-permute-start.4
  57.5 0.5 ready.1
  58.0 0.6 collective-permute-done.6.other3
  58.6 2.9 %collective-permute-done.5.other2 = bf16[176,128]{1,0:T(8,128)(2,1)S(1)} collective-permute-done((bf16[176,128]{1,0:T(8,128)(2,1)S(1)}, bf16[176,128]{1,0:T(8,128)(2,1)S(1)}, u32[]{:S(2)}, u32[]{:S(2)}) %collective-permute-start.5) | collective-permute-done | bytes 45088 | tf_op jit(solution)/shard_map/ppermute | solution.py:539
  61.5 1.7 %coarse.1 = (bf16[128,128]{1,0:T(8,128)(2,1)}, bf16[768,128]{1,0:T(8,128)(2,1)S(1)}) custom-call(bf16[176,128]{1,0:T(8,128)(2,1)S(1)} %get-tuple-element.54.own, bf16[176,128]{1,0:T(8,128)(2,1)S(1)} %collective-permute-done.4.other1, bf16[176,128]{1,0:T(8,128)(2,1)S(1)} %collective-permute-done.5.other2, bf16[176,128]{1,0:T(8,128)(2,1)S(1)} %collective-permute-done.6.other3, ...), custom_call_target="tpu_custom_call" | custom-call | flops 1000000000 | bytes 1048576 | tf_op jit(solution)/shard_map/coarse/pallas_call | solution.py:423
  63.3 21.6 %all_to_all.10 = bf16[64,12,128]{2,1,0:T(8,128)(2,1)S(1)} all-to-all(bf16[64,12,128]{2,1,0:T(8,128)(2,1)S(1)} %reshape.23), channel_id=1, replica_groups=mesh['dom'=64,'sub'=4] {'dom'}, dimensions={0} | all-to-all | bytes 393216 | tf_op jit(solution)/shard_map/all_to_all | solution.py:528
  84.9 5.2 %final.1 = bf16[2048,128]{1,0:T(8,128)(2,1)} custom-call(s32[4]{0:T(128)S(1)} %pad_add_fusion.place, bf16[128,2048]{1,0:T(8,128)(2,1)S(1)} %get-tuple-element.50.rows_t, bf16[768,128]{1,0:T(8,128)(2,1)S(1)} %reshape.24.reply, bf16[768,128]{1,0:T(8,128)(2,1)S(1)} %get-tuple-element.65.slot_of, s32[1,2048]{1,0:T(1,128)S(1)} %copy-done.5, ...), custom_call_target="tpu_custom_call" | custom-call | flops 5000000000 | bytes 1048576 | tf_op jit(solution)/shard_map/final/pallas_call | solution.py:423
  (37 shorter events, 0.5 us)
Async XLA Ops:
  0.6 7.5 %copy-start.1 = (bf16[2048,128]{1,0:T(8,128)(2,1)S(1)}, bf16[2048,128]{1,0:T(8,128)(2,1)}, u32[]{:S(2)}) copy-start(bf16[2048,128]{1,0:T(8,128)(2,1)} %nodes.1) | copy-start | bytes 1572868
  2.3 6.2 %copy-start = (bf16[4,6,128,128]{3,2,1,0:T(8,128)(2,1)S(1)}, bf16[4,6,128,128]{3,2,1,0:T(8,128)(2,1)}, u32[]{:S(2)}) copy-start(bf16[4,6,128,128]{3,2,1,0:T(8,128)(2,1)} %weights.5) | copy-start | bytes 2359300
  2.3 6.2 %copy-start.2 = (s32[1,12288]{1,0:T(1,128)S(1)}, s32[1,12288]{1,0:T(1,128)}, u32[]{:S(2)}) copy-start(s32[1,12288]{1,0:T(1,128)} %src.7) | copy-start | bytes 147460
  2.3 6.2 %copy-start.3 = (s32[1,12288]{1,0:T(1,128)S(1)}, s32[1,12288]{1,0:T(1,128)}, u32[]{:S(2)}) copy-start(s32[1,12288]{1,0:T(1,128)} %dst.7) | copy-start | bytes 147460
  2.3 6.1 %copy-start.4 = (s32[1,12288]{1,0:T(1,128)S(1)}, s32[1,12288]{1,0:T(1,128)}, u32[]{:S(2)}) copy-start(s32[1,12288]{1,0:T(1,128)} %valid.5) | copy-start | bytes 147460
  2.3 10.5 %collective-permute-start.1 = (bf16[128,128]{1,0:T(8,128)(2,1)S(1)}, bf16[128,128]{1,0:T(8,128)(2,1)S(1)}, u32[]{:S(2)}, u32[]{:S(2)}) collective-permute-start(bf16[128,128]{1,0:T(8,128)(2,1)S(1)} %get-tuple-element.70), channel_id=1, source_target_pairs={{0,255},{1,2},{2,1},{3,4},{4,3},{5,6},{6,5},{7,8},{8,7},{9,10},{10... | collective-permute-start | bytes 98312 | tf_op jit(solution)/shard_map/ppermute | solution.py:464
  8.1 4.7 %collective-permute-start = (bf16[128,128]{1,0:T(8,128)(2,1)S(1)}, bf16[128,128]{1,0:T(8,128)(2,1)S(1)}, u32[]{:S(2)}, u32[]{:S(2)}) collective-permute-start(bf16[128,128]{1,0:T(8,128)(2,1)S(1)} %get-tuple-element.71), channel_id=1, source_target_pairs={{0,1},{1,0},{2,3},{3,2},{4,5},{5,4},{6,7},{7,6},{8,9},{9,8},{10,11... | collective-permute-start | bytes 98312 | tf_op jit(solution)/shard_map/ppermute | solution.py:465
  8.5 3.3 %copy-start.5 = (s32[1,2048]{1,0:T(1,128)S(1)}, s32[1,2048]{1,0:T(1,128)}, u32[]{:S(2)}) copy-start(s32[1,2048]{1,0:T(1,128)} %cluster.3) | copy-start | bytes 24580
  8.5 3.3 %copy-start.8 = (s32[1,2,16]{2,1,0:T(2,128)S(1)}, s32[1,2,16]{2,1,0:T(2,128)}, u32[]{:S(2)}) copy-start(s32[1,2,16]{2,1,0:T(2,128)} %ghosts.1) | copy-start | bytes 388
  8.5 3.3 %copy-start.10 = (s32[1,128,1]{1,2,0:T(1,128)S(1)}, s32[1,128,1]{1,2,0:T(1,128)}, u32[]{:S(2)}) copy-start(s32[1,128,1]{1,2,0:T(1,128)} %param.19) | copy-start | bytes 1540
  8.5 3.3 %copy-start.11 = (s32[1,128]{1,0:T(1,128)S(1)}, s32[1,128]{1,0:T(1,128)}, u32[]{:S(2)}) copy-start(s32[1,128]{1,0:T(1,128)} %coarse_row.1) | copy-start | bytes 1540
  11.8 1.1 %copy-start.9 = (s32[1,2,128]{2,1,0:T(2,128)S(1)}, s32[1,2,128]{2,1,0:T(2,128)}, u32[]{:S(2)}) copy-start(s32[1,2,128]{2,1,0:T(2,128)} %param.17) | copy-start | bytes 3076
  14.9 6.0 %collective-permute-start.2 = (bf16[208,128]{1,0:T(8,128)(2,1)S(1)}, bf16[208,128]{1,0:T(8,128)(2,1)S(1)}, u32[]{:S(2)}, u32[]{:S(2)}) collective-permute-start(bf16[208,128]{1,0:T(8,128)(2,1)S(1)} %get-tuple-element.44), channel_id=1, source_target_pairs={{0,255},{1,2},{2,1},{3,4},{4,3},{5,6},{6,5},{7,8},{8,7},{9,10},{10... | collective-permute-start | bytes 159752 | tf_op jit(solution)/shard_map/ppermute | solution.py:464
  15.7 5.2 %collective-permute-start.3 = (bf16[208,128]{1,0:T(8,128)(2,1)S(1)}, bf16[208,128]{1,0:T(8,128)(2,1)S(1)}, u32[]{:S(2)}, u32[]{:S(2)}) collective-permute-start(bf16[208,128]{1,0:T(8,128)(2,1)S(1)} %get-tuple-element.45), channel_id=1, source_target_pairs={{0,1},{1,0},{2,3},{3,2},{4,5},{5,4},{6,7},{7,6},{8,9},{9,8},{10,11... | collective-permute-start | bytes 159752 | tf_op jit(solution)/shard_map/ppermute | solution.py:465
  24.0 26.8 %all-to-all-start = ((bf16[64,16,128]{2,1,0:T(8,128)(2,1)}), bf16[64,16,128]{2,1,0:T(8,128)(2,1)S(1)}, u32[]{:S(2)}, u32[]{:S(2)}) async-start(bf16[64,16,128]{2,1,0:T(8,128)(2,1)} %bitcast.7), calls=%async_computation | async-start | bytes 524288 | tf_op jit(solution)/shard_map/all_to_all | solution.py:528
  38.0 19.5 %collective-permute-start.7 = (bf16[128,128]{1,0:T(8,128)(2,1)S(1)}, bf16[128,128]{1,0:T(8,128)(2,1)S(1)}, u32[]{:S(2)}, u32[]{:S(2)}) collective-permute-start(bf16[128,128]{1,0:T(8,128)(2,1)S(1)} %get-tuple-element.56), channel_id=1, source_target_pairs={{0,255},{1,2},{2,1},{3,4},{4,3},{5,6},{6,5},{7,8},{8,7},{9,10},{10... | collective-permute-start | bytes 98312 | tf_op jit(solution)/shard_map/ppermute | solution.py:464
  43.2 14.3 %collective-permute-start.8 = (bf16[128,128]{1,0:T(8,128)(2,1)S(1)}, bf16[128,128]{1,0:T(8,128)(2,1)S(1)}, u32[]{:S(2)}, u32[]{:S(2)}) collective-permute-start(bf16[128,128]{1,0:T(8,128)(2,1)S(1)} %get-tuple-element.57), channel_id=1, source_target_pairs={{0,1},{1,0},{2,3},{3,2},{4,5},{5,4},{6,7},{7,6},{8,9},{9,8},{10,11... | collective-permute-start | bytes 98312 | tf_op jit(solution)/shard_map/ppermute | solution.py:465
  50.8 6.7 %copy-start.6 = (s32[1,768]{1,0:T(1,128)S(1)}, s32[1,768]{1,0:T(1,128)}, u32[]{:S(2)}) copy-start(s32[1,768]{1,0:T(1,128)} %src.6) | copy-start | bytes 9220
  50.8 6.7 %copy-start.7 = (s32[1,768]{1,0:T(1,128)S(1)}, s32[1,768]{1,0:T(1,128)}, u32[]{:S(2)}) copy-start(s32[1,768]{1,0:T(1,128)} %dst.6) | copy-start | bytes 9220
  52.1 6.5 %collective-permute-start.6 = (bf16[176,128]{1,0:T(8,128)(2,1)S(1)}, bf16[176,128]{1,0:T(8,128)(2,1)S(1)}, u32[]{:S(2)}, u32[]{:S(2)}) collective-permute-start(bf16[176,128]{1,0:T(8,128)(2,1)S(1)} %get-tuple-element.54.own), channel_id=1, source_target_pairs={{0,3},{1,2},{2,1},{3,0},{4,7},{5,6},{6,5},{7,4},{8,11},{9,10},{10,... | collective-permute-start | bytes 135176 | tf_op jit(solution)/shard_map/ppermute | solution.py:539
  57.1 4.4 %collective-permute-start.5 = (bf16[176,128]{1,0:T(8,128)(2,1)S(1)}, bf16[176,128]{1,0:T(8,128)(2,1)S(1)}, u32[]{:S(2)}, u32[]{:S(2)}) collective-permute-start(bf16[176,128]{1,0:T(8,128)(2,1)S(1)} %get-tuple-element.54.own), channel_id=1, source_target_pairs={{0,2},{1,3},{2,0},{3,1},{4,6},{5,7},{6,4},{7,5},{8,10},{9,11},{10,... | collective-permute-start | bytes 135176 | tf_op jit(solution)/shard_map/ppermute | solution.py:539
  57.3 4.2 %collective-permute-start.4 = (bf16[176,128]{1,0:T(8,128)(2,1)S(1)}, bf16[176,128]{1,0:T(8,128)(2,1)S(1)}, u32[]{:S(2)}, u32[]{:S(2)}) collective-permute-start(bf16[176,128]{1,0:T(8,128)(2,1)S(1)} %get-tuple-element.54.own), channel_id=1, source_target_pairs={{0,1},{1,0},{2,3},{3,2},{4,5},{5,4},{6,7},{7,6},{8,9},{9,8},{10,11... | collective-permute-start | bytes 135176 | tf_op jit(solution)/shard_map/ppermute | solution.py:539

commit v5 on v4

--- a/solution.py
+++ b/solution.py
@@ -96,14 +96,12 @@
     return rows_hot(line - b * GH, 3 * GH), rows_hot(to_row, GH)
 
 
-def pick_both(rows_t, lists, odd, near, far):
+def wanted_rows(place, lists):
+    odd = place[1] % 2 == 1
     to_lower, to_upper = lists[0:1, :], lists[1:2, :]
-    wanted = jnp.concatenate(
+    return jnp.concatenate(
         [jnp.where(odd, to_lower, to_upper), jnp.where(odd, to_upper, to_lower)], axis=1
     )
-    picked = dot(rows_t[...], rows_hot(wanted, rows_t.shape[1])).astype(BF)
-    near[0 : picked.shape[0], :] = picked[:, :GH]
-    far[0 : picked.shape[0], :] = picked[:, GH:]
 
 
 def inner_kernel(layer, rows_t, weights, src, dst, valid, out, first, both, last, ends, sums):
@@ -126,6 +124,22 @@
     pieces = [(rows_t[:, at], sums[:, at]) for at in ranges]
     for at, new in zip(ranges, node_updates(pieces, both[...], last[...])):
         out[:, at] = new
+
+
+def inner_pick_kernel(layer, place, lists, rows_t, weights, src, dst, valid, out, *refs):
+    first, both, last, picked, ends, sums = refs
+    inner_kernel(layer, rows_t, weights, src, dst, valid, out, first, both, last, ends, sums)
+    count = out.shape[1]
+    table = rows_hot(wanted_rows(place, lists) - GH, count - 2 * GH)
+    picked[...] = dot(out[:, GH : count - GH], table).astype(BF)
+
+
+def inner_pool_kernel(layer, cluster, rows_t, weights, src, dst, valid, out, *refs):
+    first, both, last, pooled, ends, sums = refs
+    inner_kernel(layer, rows_t, weights, src, dst, valid, out, first, both, last, ends, sums)
+    count = out.shape[1]
+    member = rows_hot(cluster[:, GH : count - GH], 128)
+    pooled[...] = dot(out[:, GH : count - GH], member, NT)
 
 
 def by_side(place, near, far):
@@ -167,23 +181,27 @@
 
 
 def ends_pick_kernel(place, inner, *refs):
-    lists, cluster, facts, slot_row, out, near, far, more = refs[-8:]
-    slots = dot(slot_row[...], rows_hot(cluster[...], 128)).astype(BF)
+    lists, picked, slots, facts, out, near, far = refs[-7:]
     ghosts = [rows.T for rows in by_side(place, refs[1][...], refs[2][...])]
-    whole_layer(inner, end_blocks(place, refs[0], ghosts, *refs[3:-8]), out)
-    more[0:128, :] = out[...]
-    more[128:144, :] = slots
-    pick_both(more, lists, place[1] % 2 == 1, near, far)
-    near[144:208, :] = facts[0:64, :]
-    far[144:208, :] = facts[0:64, :]
+    new = end_blocks(place, refs[0], ghosts, *refs[3:-7])
+    wanted = wanted_rows(place, lists)
+    table = [rows_hot(wanted, GH), rows_hot(wanted - (out.shape[1] - GH), GH)]
+    rows = picked[...].astype(F32) + dot(new, jnp.concatenate(table, axis=0))
+    whole_layer(inner, new, out)
+    for side, ref in enumerate((near, far)):
+        ref[0:128, :] = rows[:, side * GH : (side + 1) * GH].astype(BF)
+        ref[128:144, :] = slots[:, side * GH : (side + 1) * GH]
+        ref[144:208, :] = facts[0:64, :]
 
 
 def ends_pool_kernel(place, inner, *refs):
-    cluster, slot_pick, facts, out, parcel = refs[-5:]
+    cluster, pooled, slot_pick, facts, out, parcel = refs[-6:]
     ghosts = by_side(place, refs[2][0:128, :], refs[1][0:128, :])
-    whole_layer(inner, end_blocks(place, refs[0], ghosts, *refs[3:-5]), out)
-    member = rows_hot(cluster[...], 128)
-    partial = dot(out[...], member, NT).T.astype(BF)
+    new = end_blocks(place, refs[0], ghosts, *refs[3:-6])
+    whole_layer(inner, new, out)
+    count = out.shape[1]
+    named = jnp.concatenate([cluster[:, 0:GH], cluster[:, count - GH :]], axis=1)
+    partial = (pooled[...] + dot(new, rows_hot(named, 128), NT)).T.astype(BF)
     ids = by_side(place, refs[2][144:208, :], refs[1][144:208, :])
     lane = iota(ids[0].shape, 1)
     moved = [pltpu.roll(ids[side].astype(F32), CAP * (3 + side), 1) for side in (0, 1)]
@@ -200,7 +218,8 @@
 
 
 def pick_kernel(place, rows_t, lists, near, far, meta_pick, spread):
-    pick_both(rows_t, lists, place[1] % 2 == 1, near, far)
+    picked = dot(rows_t[...], rows_hot(wanted_rows(place, lists), rows_t.shape[1])).astype(BF)
+    near[...], far[...] = picked[:, :GH], picked[:, GH:]
     count, total = meta_pick.shape
     owners = count // 3
     wide, pick = iota((count, total), 1), iota((count, total), 0)
@@ -208,7 +227,9 @@
     spread[...] = hot((wide // SLOTS == pick % owners) & (wide % SLOTS // CAP == pick // owners))
 
 
-def prepare_kernel(cluster, owner, coarse_row, ghosts, slot_pick, facts, slot_of, slot_row_out):
+def prepare_kernel(
+    place, lists, cluster, owner, coarse_row, ghosts, slot_pick, facts, slot_of, slots
+):
     member = rows_hot(cluster[...], 128)
     counts = jnp.sum(member.astype(F32), axis=1, keepdims=True)
     owner_row = owner[...].astype(F32)
@@ -219,7 +240,8 @@
     place_row = jnp.sum(jnp.where(same & (sub < lane), 1.0, 0.0), axis=0, keepdims=True)
     slot_row = owner_row * CAP + place_row
     owners = slot_pick.shape[0] // SLOTS
-    slot_row_out[...] = jnp.broadcast_to(slot_row, slot_row_out.shape).astype(BF)
+    every = dot(jnp.broadcast_to(slot_row, (16, 128)).astype(BF), member).astype(BF)
+    slots[...] = dot(every, rows_hot(wanted_rows(place, lists), cluster.shape[1])).astype(BF)
     row = iota((owners * SLOTS, 128), 0)
     to, at = row // SLOTS, row % SLOTS
     label = jnp.where(
@@ -416,13 +438,15 @@
         copy.wait()
 
 
-def run(kernel, outs, args, scalars=0, layer=None, scratch=(), flops=0, out_space=pltpu.VMEM, name=None):
+def run(kernel, outs, args, scalars=0, layer=None, scratch=(), flops=0, out_space=pltpu.VMEM, wide=None, name=None):
     specs = []
     for i in range(len(args)):
         specs.append(pl.BlockSpec(memory_space=pltpu.SMEM if i < scalars else pltpu.VMEM))
     return pl.pallas_call(
         kernel if layer is None else functools.partial(kernel, layer),
-        out_shape=[jax.ShapeDtypeStruct(shape, BF) for shape in outs],
+        out_shape=[
+            jax.ShapeDtypeStruct(shape, F32 if i == wide else BF) for i, shape in enumerate(outs)
+        ],
         in_specs=specs,
         out_specs=[pl.BlockSpec(memory_space=out_space) for _ in outs],
         scratch_shapes=scratch,
@@ -465,17 +489,17 @@
         from_near = lax.ppermute(near, ("dom", "sub"), near_pairs)
         return from_far, from_near
 
-    def inner(states, layer):
-        out, *weights_now = run(
-            inner_kernel,
-            [rows_t] + forms,
-            (states, weights) + edges,
+    def inner(kernel, before, states, layer, more, **options):
+        out, first, both, last, extra = run(
+            kernel,
+            [rows_t] + forms + [more],
+            before + (states, weights) + edges,
             layer=layer,
             scratch=[pltpu.VMEM((2 * width, count), BF), pltpu.VMEM(rows_t, BF)],
             flops=4 * 10**9,
-            name="inner",
+            **options,
         )
-        return out, tuple(weights_now)
+        return out, (first, both, last), extra
 
     wanted = lists.reshape(-1, 1) == jnp.arange(count, dtype=I32)[None, :]
     picked = dot(wanted.astype(BF), nodes).astype(BF)
@@ -484,30 +508,34 @@
         jnp.where(odd, picked[:GH], picked[GH:]), jnp.where(odd, picked[GH:], picked[:GH])
     )
     (states,) = run(turn_kernel, [rows_t], (nodes,), flops=3 * 10**8, name="turn")
-    slot_pick, facts, slot_of, slot_row = run(
+    slot_pick, facts, slot_of, slots = run(
         prepare_kernel,
-        [(doms * SLOTS, 256), (128, 128), (doms * BACK, 128), (16, 128)],
-        (cluster_of, owner.reshape(1, -1), coarse_row, coarse_ghosts),
+        [(doms * SLOTS, 256), (128, 128), (doms * BACK, 128), (16, 2 * GH)],
+        (place, lists, cluster_of, owner.reshape(1, -1), coarse_row, coarse_ghosts),
+        scalars=1,
         flops=10**9,
         name="prepare",
     )
-    middle, now = inner(states, 0)
+    middle, now, picked = inner(
+        inner_pick_kernel, (place, lists), states, 0, (width, 2 * GH), scalars=1, name="inner_pick"
+    )
     early = (GH + 16 + doms, GH)
     states, near, far = run(
         ends_pick_kernel,
         [rows_t, early, early],
-        (place, middle, states) + ghosts[::-1] + now + edges + (lists, cluster_of, facts, slot_row),
+        (place, middle, states) + ghosts[::-1] + now + edges + (lists, picked, slots, facts),
         scalars=1,
-        scratch=[pltpu.VMEM((width + 16, count), BF)],
         flops=10**9,
         name="ends_pick",
     )
     early = swap(near, far)
-    middle, now = inner(states, 1)
+    middle, now, pooled = inner(
+        inner_pool_kernel, (cluster_of,), states, 1, (width, 128), wide=4, name="inner_pool"
+    )
     states, parcel = run(
         ends_pool_kernel,
         [rows_t, (doms * SLOTS, width)],
-        (place, middle, states) + early + now + edges + (cluster_of, slot_pick, facts),
+        (place, middle, states) + early + now + edges + (cluster_of, pooled, slot_pick, facts),
         scalars=1,
         flops=10**9,
         name="ends_pool",
@@ -524,7 +552,8 @@
 
     def exchange(rows):
         shape = rows.shape
-        rows = rows.reshape(doms, shape[0] // doms, width)
+        each = 4 if shape[0] // doms % 8 else 8
+        rows = rows.reshape(-1, each, width)
         rows = lax.all_to_all(rows, "dom", split_axis=0, concat_axis=0, tiled=True)
         return rows.reshape(shape)
 

time: 91.2 us -> 89 us (0.976)
  blocking collectives: 21.6 us -> 19.6 us
  Pallas kernels: 22.6 us -> 23.7 us
  starting transfers between devices: 31.2 us -> 30.1 us
    all_to_all x1, blocking collectives: 21.6 us -> 19.6 us  [exchange(): rows = lax.all_to_all(rows, 'dom', split_axis=0, concat_axis=0, tiled=True)]
    all_to_all x1, waiting for transfers between devices: 7.62 us -> 9.19 us  [exchange(): rows = lax.all_to_all(rows, 'dom', split_axis=0, concat_axis=0, tiled=True)]
    ppermute x3, starting transfers between devices: 11.8 us -> 10.2 us  [swap(): from_far = lax.ppermute(far, ('dom', 'sub'), far_pairs)]
    pallas_call x11, Pallas kernels: 22.6 us -> 23.7 us  [run(): pl.pallas_call(kernel if layer is None else functools.partial(kernel, lay...]
  transfers between devices with their start and end apart: 10 -> 10, of which waited for: 4 -> 4; matrix products, arithmetic and copies ran while one was open for 0% -> 0% of each run, Pallas kernels for 12% -> 14%
where the time goes in v5:
time: 89 us; the launch traced here: 88.8 us
  starting transfers between devices  30.1 us (34%)
  Pallas kernels  23.7 us (27%)
  blocking collectives  19.6 us (22%)
  waiting for transfers between devices  12.5 us (14%)
  matrix products  1.6 us (2%)
  between operations  1.08 us (1%)
    pallas_call x11, Pallas kernels, run(): pl.pallas_call(kernel if layer is None else functools.partial(kernel, lay...  23.7 us
    all_to_all x1, blocking collectives, exchange(): rows = lax.all_to_all(rows, 'dom', split_axis=0, concat_axis=0, tiled=True)  19.6 us
    all_to_all x1, starting transfers between devices, exchange(): rows = lax.all_to_all(rows, 'dom', split_axis=0, concat_axis=0, tiled=True)  12.9 us
    ppermute x3, starting transfers between devices, swap(): from_far = lax.ppermute(far, ('dom', 'sub'), far_pairs)  10.2 us
    all_to_all x1, waiting for transfers between devices, exchange(): rows = lax.all_to_all(rows, 'dom', split_axis=0, concat_axis=0, tiled=True)  9.19 us
    ppermute x3, starting transfers between devices, on_device(): lax.ppermute(part, 'sub', [(i, i ^ k) for i in range(subs)])  5.9 us
    ppermute x3, waiting for transfers between devices, on_device(): lax.ppermute(part, 'sub', [(i, i ^ k) for i in range(subs)])  2.67 us
  transfers between devices with their start and end apart: 10, of which 4 were waited for; matrix products, arithmetic and copies ran while one was open for 0% of the time, Pallas kernels for 14%

profile of v5, /device:TPU:1, one launch (start us, length us, event | category | flops | bytes accessed | tf_op | source)
XLA Modules:
  0.0 88.8 jit_solution(4263399035966785077)
XLA Ops:
  0.7 1.6 %fusion.1 = bf16[256,128]{1,0:T(8,128)(2,1)S(1)} fusion(bf16[2048,128]{1,0:T(8,128)(2,1)} %nodes.1, s32[256]{0:T(256)} %bitcast.15), kind=kOutput, calls=%fused_computation.2 | convolution fusion | flops 134774784 | bytes 590848 | tf_op jit(solution)/shard_map/dot_general | solution.py:27
  2.3 5.8 %collective-permute-start.1 = (bf16[128,128]{1,0:T(8,128)(2,1)S(1)}, bf16[128,128]{1,0:T(8,128)(2,1)S(1)}, u32[]{:S(2)}, u32[]{:S(2)}) collective-permute-start(bf16[128,128]{1,0:T(8,128)(2,1)S(1)} %get-tuple-element.74), channel_id=1, source_target_pairs={{0,255},{1,2},{2,1},{3,4},{4,3},{5,6},{6,5},{7,8},{8,7},{9,10},{10... | collective-permute-start | bytes 98312 | tf_op jit(solution)/shard_map/ppermute | solution.py:488
  8.5 4.1 %inner_pick.1 = (bf16[128,2048]{1,0:T(8,128)(2,1)S(1)}, bf16[256,128]{1,0:T(8,128)(2,1)S(1)}, bf16[128,256]{1,0:T(8,128)(2,1)S(1)}, bf16[128,128]{1,0:T(8,128)(2,1)S(1)}, bf16[128,256]{1,0:T(8,128)(2,1)S(1)}) custom-call(s32[4]{0:T(128)S(1)} %pad_add_fusion.place, s32[2,128]{1,0:T(2,128)S(1)} %bitcast.16, bf16[128,2048]{1,0:T(8,128)(2,1)S(1)} %turn.1.rows_t.refs_0_, ...), custom_call_target="tpu_custom_call" | custom-call | flops 4000000000 | bytes 1048576 | tf_op jit(solution)/shard_map/inner_pick/pallas_call | solution.py:445
  12.6 1.8 %prepare.1 = (bf16[1024,256]{1,0:T(8,128)(2,1)S(1)}, bf16[128,128]{1,0:T(8,128)(2,1)S(1)}, bf16[768,128]{1,0:T(8,128)(2,1)S(1)}, bf16[16,256]{1,0:T(8,128)(2,1)S(1)}) custom-call(s32[4]{0:T(128)S(1)} %pad_add_fusion.place, s32[2,128]{1,0:T(2,128)S(1)} %bitcast.17, s32[1,2048]{1,0:T(1,128)S(1)} %copy-done.5, s32[1,128]{1,0:T(1,128)S(1)} %bitcast.20, ...), custom_call_target="tpu_custom_call" | custom-call | flops 1000000000 | bytes 1048576 | tf_op jit(solution)/shard_map/prepare/pallas_call | solution.py:445
  14.4 1.7 %ends_pick.1 = (bf16[128,2048]{1,0:T(8,128)(2,1)S(1)}, bf16[208,128]{1,0:T(8,128)(2,1)S(1)}, bf16[208,128]{1,0:T(8,128)(2,1)S(1)}) custom-call(s32[4]{0:T(128)S(1)} %pad_add_fusion.place, bf16[128,2048]{1,0:T(8,128)(2,1)S(1)} %get-tuple-element.38.inner, bf16[128,2048]{1,0:T(8,128)(2,1)S(1)} %turn.1.rows_t.refs_0_, ...), custom_call_target="tpu_custom_call" | custom-call | flops 1000000000 | bytes 1048576 | tf_op jit(solution)/shard_map/ends_pick/pallas_call | solution.py:445
  16.1 0.8 collective-permute-start.2
  16.9 1.1 %collective-permute-start.3 = (bf16[208,128]{1,0:T(8,128)(2,1)S(1)}, bf16[208,128]{1,0:T(8,128)(2,1)S(1)}, u32[]{:S(2)}, u32[]{:S(2)}) collective-permute-start(bf16[208,128]{1,0:T(8,128)(2,1)S(1)} %get-tuple-element.48), channel_id=1, source_target_pairs={{0,1},{1,0},{2,3},{3,2},{4,5},{5,4},{6,7},{7,6},{8,9},{9,8},{10,11... | collective-permute-start | bytes 159752 | tf_op jit(solution)/shard_map/ppermute | solution.py:489
  18.0 3.5 %inner_pool.1 = (bf16[128,2048]{1,0:T(8,128)(2,1)S(1)}, bf16[256,128]{1,0:T(8,128)(2,1)S(1)}, bf16[128,256]{1,0:T(8,128)(2,1)S(1)}, bf16[128,128]{1,0:T(8,128)(2,1)S(1)}, f32[128,128]{1,0:T(8,128)S(1)}) custom-call(s32[1,2048]{1,0:T(1,128)S(1)} %copy-done.5, bf16[128,2048]{1,0:T(8,128)(2,1)S(1)} %get-tuple-element.45.rows_t.refs_0_, ...), custom_call_target="tpu_custom_call" | custom-call | flops 4000000000 | bytes 1048576 | tf_op jit(solution)/shard_map/inner_pool/pallas_call | solution.py:445
  21.5 0.6 collective-permute-done.2.refs_1_.early_far
  22.1 2.7 %ends_pool.1 = (bf16[128,2048]{1,0:T(8,128)(2,1)S(1)}, bf16[1024,128]{1,0:T(8,128)(2,1)}) custom-call(s32[4]{0:T(128)S(1)} %pad_add_fusion.place, bf16[128,2048]{1,0:T(8,128)(2,1)S(1)} %get-tuple-element.46.inner, bf16[128,2048]{1,0:T(8,128)(2,1)S(1)} %get-tuple-element.45.rows_t.refs_0_, bf16[208,128]{1,0:T(8,128)(2,1)S(1)} %collective-permute-done.2.refs_1_.early_far, ...), custom_call_target="tpu_custom_call" | custom-call | flops 1000000000 | bytes 1048576 | tf_op jit(solution)/shard_map/ends_pool/pallas_call | solution.py:445
  24.9 12.9 %all-to-all-start = ((bf16[128,8,128]{2,1,0:T(8,128)(2,1)}), bf16[128,8,128]{2,1,0:T(8,128)(2,1)S(1)}, u32[]{:S(2)}, u32[]{:S(2)}) async-start(bf16[128,8,128]{2,1,0:T(8,128)(2,1)} %bitcast.7), calls=%async_computation | async-start | bytes 524288 | tf_op jit(solution)/shard_map/all_to_all | solution.py:557
  37.8 1.0 %pick.1 = (bf16[128,128]{1,0:T(8,128)(2,1)S(1)}, bf16[128,128]{1,0:T(8,128)(2,1)S(1)}, bf16[192,1024]{1,0:T(8,128)(2,1)S(1)}, bf16[192,1024]{1,0:T(8,128)(2,1)S(1)}) custom-call(s32[4]{0:T(128)S(1)} %pad_add_fusion.place, bf16[128,2048]{1,0:T(8,128)(2,1)S(1)} %get-tuple-element.54.rows_t, s32[2,128]{1,0:T(2,128)S(1)} %bitcast.19), custom_call_target="tpu_custom_call" | custom-call | flops 1000000000 | bytes 1048576 | tf_op jit(solution)/shard_map/pick/pallas_call | solution.py:445
  38.8 3.6 %collective-permute-start.7 = (bf16[128,128]{1,0:T(8,128)(2,1)S(1)}, bf16[128,128]{1,0:T(8,128)(2,1)S(1)}, u32[]{:S(2)}, u32[]{:S(2)}) collective-permute-start(bf16[128,128]{1,0:T(8,128)(2,1)S(1)} %get-tuple-element.60), channel_id=1, source_target_pairs={{0,255},{1,2},{2,1},{3,4},{4,3},{5,6},{6,5},{7,8},{8,7},{9,10},{10... | collective-permute-start | bytes 98312 | tf_op jit(solution)/shard_map/ppermute | solution.py:488
  42.5 9.2 %all-to-all-done = bf16[128,8,128]{2,1,0:T(8,128)(2,1)S(1)} async-done(((bf16[128,8,128]{2,1,0:T(8,128)(2,1)}), bf16[128,8,128]{2,1,0:T(8,128)(2,1)S(1)}, u32[]{:S(2)}, u32[]{:S(2)}) %all-to-all-start) | async-done | bytes 262176 | tf_op jit(solution)/shard_map/all_to_all | solution.py:557
  51.7 1.3 %received.1 = (bf16[176,128]{1,0:T(8,128)(2,1)S(1)}, bf16[64,128]{1,0:T(8,128)(2,1)S(1)}) custom-call(s32[4]{0:T(128)S(1)} %pad_add_fusion.place, bf16[1024,128]{1,0:T(8,128)(2,1)S(1)} %bitcast.12, bf16[192,1024]{1,0:T(8,128)(2,1)S(1)} %get-tuple-element.56.meta_pick, bf16[192,1024]{1,0:T(8,128)(2,1)S(1)} %get-tuple-element.57.spread), custom_call_target="tpu_custom_call" | custom-call | flops 1000000000 | bytes 1048576 | tf_op jit(solution)/shard_map/received/pallas_call | solution.py:445
  53.0 3.8 %collective-permute-start.6 = (bf16[176,128]{1,0:T(8,128)(2,1)S(1)}, bf16[176,128]{1,0:T(8,128)(2,1)S(1)}, u32[]{:S(2)}, u32[]{:S(2)}) collective-permute-start(bf16[176,128]{1,0:T(8,128)(2,1)S(1)} %get-tuple-element.58.own), channel_id=1, source_target_pairs={{0,3},{1,2},{2,1},{3,0},{4,7},{5,6},{6,5},{7,4},{8,11},{9,10},{10,... | collective-permute-start | bytes 135176 | tf_op jit(solution)/shard_map/ppermute | solution.py:568
  56.8 1.9 %collective-permute-start.5 = (bf16[176,128]{1,0:T(8,128)(2,1)S(1)}, bf16[176,128]{1,0:T(8,128)(2,1)S(1)}, u32[]{:S(2)}, u32[]{:S(2)}) collective-permute-start(bf16[176,128]{1,0:T(8,128)(2,1)S(1)} %get-tuple-element.58.own), channel_id=1, source_target_pairs={{0,2},{1,3},{2,0},{3,1},{4,6},{5,7},{6,4},{7,5},{8,10},{9,11},{10,... | collective-permute-start | bytes 135176 | tf_op jit(solution)/shard_map/ppermute | solution.py:568
  58.7 0.2 collective-permute-start.4
  58.9 0.5 ready.1
  59.4 1.4 %collective-permute-done.5.other2 = bf16[176,128]{1,0:T(8,128)(2,1)S(1)} collective-permute-done((bf16[176,128]{1,0:T(8,128)(2,1)S(1)}, bf16[176,128]{1,0:T(8,128)(2,1)S(1)}, u32[]{:S(2)}, u32[]{:S(2)}) %collective-permute-start.5) | collective-permute-done | bytes 45088 | tf_op jit(solution)/shard_map/ppermute | solution.py:568
  60.9 1.2 %collective-permute-done.4.other1 = bf16[176,128]{1,0:T(8,128)(2,1)S(1)} collective-permute-done((bf16[176,128]{1,0:T(8,128)(2,1)S(1)}, bf16[176,128]{1,0:T(8,128)(2,1)S(1)}, u32[]{:S(2)}, u32[]{:S(2)}) %collective-permute-start.4) | collective-permute-done | bytes 45088 | tf_op jit(solution)/shard_map/ppermute | solution.py:568
  62.1 1.7 %coarse.1 = (bf16[128,128]{1,0:T(8,128)(2,1)}, bf16[768,128]{1,0:T(8,128)(2,1)S(1)}) custom-call(bf16[176,128]{1,0:T(8,128)(2,1)S(1)} %get-tuple-element.58.own, bf16[176,128]{1,0:T(8,128)(2,1)S(1)} %collective-permute-done.4.other1, bf16[176,128]{1,0:T(8,128)(2,1)S(1)} %collective-permute-done.5.other2, bf16[176,128]{1,0:T(8,128)(2,1)S(1)} %collective-permute-done.6.other3, ...), custom_call_target="tpu_custom_call" | custom-call | flops 1000000000 | bytes 1048576 | tf_op jit(solution)/shard_map/coarse/pallas_call | solution.py:445
  63.8 19.6 %all_to_all.10 = bf16[192,4,128]{2,1,0:T(4,128)(2,1)S(1)} all-to-all(bf16[192,4,128]{2,1,0:T(4,128)(2,1)S(1)} %bitcast.14), channel_id=1, replica_groups=mesh['dom'=64,'sub'=4] {'dom'}, dimensions={0} | all-to-all | bytes 393216 | tf_op jit(solution)/shard_map/all_to_all | solution.py:557
  83.4 5.2 %final.1 = bf16[2048,128]{1,0:T(8,128)(2,1)} custom-call(s32[4]{0:T(128)S(1)} %pad_add_fusion.place, bf16[128,2048]{1,0:T(8,128)(2,1)S(1)} %get-tuple-element.54.rows_t, bf16[768,128]{1,0:T(8,128)(2,1)S(1)} %bitcast.13, bf16[768,128]{1,0:T(8,128)(2,1)S(1)} %get-tuple-element.69.slot_of, s32[1,2048]{1,0:T(1,128)S(1)} %copy-done.5, ...), custom_call_target="tpu_custom_call" | custom-call | flops 5000000000 | bytes 1048576 | tf_op jit(solution)/shard_map/final/pallas_call | solution.py:445
  (35 shorter events, 0.4 us)
Async XLA Ops:
  0.6 7.5 %copy-start.1 = (bf16[2048,128]{1,0:T(8,128)(2,1)S(1)}, bf16[2048,128]{1,0:T(8,128)(2,1)}, u32[]{:S(2)}) copy-start(bf16[2048,128]{1,0:T(8,128)(2,1)} %nodes.1) | copy-start | bytes 1572868
  2.3 6.2 %copy-start = (bf16[4,6,128,128]{3,2,1,0:T(8,128)(2,1)S(1)}, bf16[4,6,128,128]{3,2,1,0:T(8,128)(2,1)}, u32[]{:S(2)}) copy-start(bf16[4,6,128,128]{3,2,1,0:T(8,128)(2,1)} %weights.5) | copy-start | bytes 2359300
  2.3 6.2 %copy-start.2 = (s32[1,12288]{1,0:T(1,128)S(1)}, s32[1,12288]{1,0:T(1,128)}, u32[]{:S(2)}) copy-start(s32[1,12288]{1,0:T(1,128)} %src.7) | copy-start | bytes 147460
  2.3 6.2 %copy-start.3 = (s32[1,12288]{1,0:T(1,128)S(1)}, s32[1,12288]{1,0:T(1,128)}, u32[]{:S(2)}) copy-start(s32[1,12288]{1,0:T(1,128)} %dst.7) | copy-start | bytes 147460
  2.3 6.2 %copy-start.4 = (s32[1,12288]{1,0:T(1,128)S(1)}, s32[1,12288]{1,0:T(1,128)}, u32[]{:S(2)}) copy-start(s32[1,12288]{1,0:T(1,128)} %valid.5) | copy-start | bytes 147460
  2.3 6.2 %copy-start.9 = (s32[1,2,128]{2,1,0:T(2,128)S(1)}, s32[1,2,128]{2,1,0:T(2,128)}, u32[]{:S(2)}) copy-start(s32[1,2,128]{2,1,0:T(2,128)} %param.17) | copy-start | bytes 3076
  2.3 12.1 %collective-permute-start.1 = (bf16[128,128]{1,0:T(8,128)(2,1)S(1)}, bf16[128,128]{1,0:T(8,128)(2,1)S(1)}, u32[]{:S(2)}, u32[]{:S(2)}) collective-permute-start(bf16[128,128]{1,0:T(8,128)(2,1)S(1)} %get-tuple-element.74), channel_id=1, source_target_pairs={{0,255},{1,2},{2,1},{3,4},{4,3},{5,6},{6,5},{7,8},{8,7},{9,10},{10... | collective-permute-start | bytes 98312 | tf_op jit(solution)/shard_map/ppermute | solution.py:488
  8.2 6.2 %collective-permute-start = (bf16[128,128]{1,0:T(8,128)(2,1)S(1)}, bf16[128,128]{1,0:T(8,128)(2,1)S(1)}, u32[]{:S(2)}, u32[]{:S(2)}) collective-permute-start(bf16[128,128]{1,0:T(8,128)(2,1)S(1)} %get-tuple-element.75), channel_id=1, source_target_pairs={{0,1},{1,0},{2,3},{3,2},{4,5},{5,4},{6,7},{7,6},{8,9},{9,8},{10,11... | collective-permute-start | bytes 98312 | tf_op jit(solution)/shard_map/ppermute | solution.py:489
  8.5 4.1 %copy-start.5 = (s32[1,2048]{1,0:T(1,128)S(1)}, s32[1,2048]{1,0:T(1,128)}, u32[]{:S(2)}) copy-start(s32[1,2048]{1,0:T(1,128)} %cluster.5) | copy-start | bytes 24580
  8.5 4.1 %copy-start.8 = (s32[1,2,16]{2,1,0:T(2,128)S(1)}, s32[1,2,16]{2,1,0:T(2,128)}, u32[]{:S(2)}) copy-start(s32[1,2,16]{2,1,0:T(2,128)} %ghosts.1) | copy-start | bytes 388
  8.5 4.1 %copy-start.10 = (s32[1,128,1]{1,2,0:T(1,128)S(1)}, s32[1,128,1]{1,2,0:T(1,128)}, u32[]{:S(2)}) copy-start(s32[1,128,1]{1,2,0:T(1,128)} %param.19) | copy-start | bytes 1540
  8.5 4.1 %copy-start.11 = (s32[1,128]{1,0:T(1,128)S(1)}, s32[1,128]{1,0:T(1,128)}, u32[]{:S(2)}) copy-start(s32[1,128]{1,0:T(1,128)} %coarse_row.1) | copy-start | bytes 1540
  16.1 6.0 %collective-permute-start.2 = (bf16[208,128]{1,0:T(8,128)(2,1)S(1)}, bf16[208,128]{1,0:T(8,128)(2,1)S(1)}, u32[]{:S(2)}, u32[]{:S(2)}) collective-permute-start(bf16[208,128]{1,0:T(8,128)(2,1)S(1)} %get-tuple-element.47), channel_id=1, source_target_pairs={{0,255},{1,2},{2,1},{3,4},{4,3},{5,6},{6,5},{7,8},{8,7},{9,10},{10... | collective-permute-start | bytes 159752 | tf_op jit(solution)/shard_map/ppermute | solution.py:488
  16.9 5.2 %collective-permute-start.3 = (bf16[208,128]{1,0:T(8,128)(2,1)S(1)}, bf16[208,128]{1,0:T(8,128)(2,1)S(1)}, u32[]{:S(2)}, u32[]{:S(2)}) collective-permute-start(bf16[208,128]{1,0:T(8,128)(2,1)S(1)} %get-tuple-element.48), channel_id=1, source_target_pairs={{0,1},{1,0},{2,3},{3,2},{4,5},{5,4},{6,7},{7,6},{8,9},{9,8},{10,11... | collective-permute-start | bytes 159752 | tf_op jit(solution)/shard_map/ppermute | solution.py:489
  24.9 26.8 %all-to-all-start = ((bf16[128,8,128]{2,1,0:T(8,128)(2,1)}), bf16[128,8,128]{2,1,0:T(8,128)(2,1)S(1)}, u32[]{:S(2)}, u32[]{:S(2)}) async-start(bf16[128,8,128]{2,1,0:T(8,128)(2,1)} %bitcast.7), calls=%async_computation | async-start | bytes 524288 | tf_op jit(solution)/shard_map/all_to_all | solution.py:557
  38.8 20.1 %collective-permute-start.7 = (bf16[128,128]{1,0:T(8,128)(2,1)S(1)}, bf16[128,128]{1,0:T(8,128)(2,1)S(1)}, u32[]{:S(2)}, u32[]{:S(2)}) collective-permute-start(bf16[128,128]{1,0:T(8,128)(2,1)S(1)} %get-tuple-element.60), channel_id=1, source_target_pairs={{0,255},{1,2},{2,1},{3,4},{4,3},{5,6},{6,5},{7,8},{8,7},{9,10},{10... | collective-permute-start | bytes 98312 | tf_op jit(solution)/shard_map/ppermute | solution.py:488
  42.5 16.4 %collective-permute-start.8 = (bf16[128,128]{1,0:T(8,128)(2,1)S(1)}, bf16[128,128]{1,0:T(8,128)(2,1)S(1)}, u32[]{:S(2)}, u32[]{:S(2)}) collective-permute-start(bf16[128,128]{1,0:T(8,128)(2,1)S(1)} %get-tuple-element.61), channel_id=1, source_target_pairs={{0,1},{1,0},{2,3},{3,2},{4,5},{5,4},{6,7},{7,6},{8,9},{9,8},{10,11... | collective-permute-start | bytes 98312 | tf_op jit(solution)/shard_map/ppermute | solution.py:489
  51.7 7.2 %copy-start.6 = (s32[1,768]{1,0:T(1,128)S(1)}, s32[1,768]{1,0:T(1,128)}, u32[]{:S(2)}) copy-start(s32[1,768]{1,0:T(1,128)} %src.6) | copy-start | bytes 9220
  51.7 7.2 %copy-start.7 = (s32[1,768]{1,0:T(1,128)S(1)}, s32[1,768]{1,0:T(1,128)}, u32[]{:S(2)}) copy-start(s32[1,768]{1,0:T(1,128)} %dst.6) | copy-start | bytes 9220
  53.0 6.4 %collective-permute-start.6 = (bf16[176,128]{1,0:T(8,128)(2,1)S(1)}, bf16[176,128]{1,0:T(8,128)(2,1)S(1)}, u32[]{:S(2)}, u32[]{:S(2)}) collective-permute-start(bf16[176,128]{1,0:T(8,128)(2,1)S(1)} %get-tuple-element.58.own), channel_id=1, source_target_pairs={{0,3},{1,2},{2,1},{3,0},{4,7},{5,6},{6,5},{7,4},{8,11},{9,10},{10,... | collective-permute-start | bytes 135176 | tf_op jit(solution)/shard_map/ppermute | solution.py:568
  56.8 4.1 %collective-permute-start.5 = (bf16[176,128]{1,0:T(8,128)(2,1)S(1)}, bf16[176,128]{1,0:T(8,128)(2,1)S(1)}, u32[]{:S(2)}, u32[]{:S(2)}) collective-permute-start(bf16[176,128]{1,0:T(8,128)(2,1)S(1)} %get-tuple-element.58.own), channel_id=1, source_target_pairs={{0,2},{1,3},{2,0},{3,1},{4,6},{5,7},{6,4},{7,5},{8,10},{9,11},{10,... | collective-permute-start | bytes 135176 | tf_op jit(solution)/shard_map/ppermute | solution.py:568
  58.7 3.4 %collective-permute-start.4 = (bf16[176,128]{1,0:T(8,128)(2,1)S(1)}, bf16[176,128]{1,0:T(8,128)(2,1)S(1)}, u32[]{:S(2)}, u32[]{:S(2)}) collective-permute-start(bf16[176,128]{1,0:T(8,128)(2,1)S(1)} %get-tuple-element.58.own), channel_id=1, source_target_pairs={{0,1},{1,0},{2,3},{3,2},{4,5},{5,4},{6,7},{7,6},{8,9},{9,8},{10,11... | collective-permute-start | bytes 135176 | tf_op jit(solution)/shard_map/ppermute | solution.py:568

commit v6 on v5

--- a/solution.py
+++ b/solution.py
@@ -195,10 +195,9 @@
 
 
 def ends_pool_kernel(place, inner, *refs):
-    cluster, pooled, slot_pick, facts, out, parcel = refs[-6:]
+    cluster, pooled, slot_pick, facts, out, parcel, packed, sems = refs[-8:]
     ghosts = by_side(place, refs[2][0:128, :], refs[1][0:128, :])
-    new = end_blocks(place, refs[0], ghosts, *refs[3:-6])
-    whole_layer(inner, new, out)
+    new = end_blocks(place, refs[0], ghosts, *refs[3:-8])
     count = out.shape[1]
     named = jnp.concatenate([cluster[:, 0:GH], cluster[:, count - GH :]], axis=1)
     partial = (pooled[...] + dot(new, rows_hot(named, 128), NT)).T.astype(BF)
@@ -208,9 +207,17 @@
     moved = [jnp.where(lane // CAP == 3 + side, moved[side], 0.0) for side in (0, 1)]
     added = moved[0] + moved[1]
     known = jnp.concatenate([added, jnp.zeros_like(added)], axis=0) + facts[...].astype(F32)
-    parcel[...] = dot(
-        slot_pick[...], jnp.concatenate([partial, known.astype(BF)], axis=0)
-    ).astype(BF)
+    sent = jnp.concatenate([partial, known.astype(BF)], axis=0)
+    step = packed.shape[0] // 2
+    copies = []
+    for half in range(2):
+        at = pl.ds(half * step, step)
+        packed[at, :] = dot(slot_pick[at, :], sent).astype(BF)
+        copies.append(pltpu.make_async_copy(packed.at[at, :], parcel.at[at, :], sems.at[half]))
+        copies[-1].start()
+    whole_layer(inner, new, out)
+    for copy in copies:
+        copy.wait()
 
 
 def turn_kernel(nodes, rows_t):
@@ -438,7 +445,7 @@
         copy.wait()
 
 
-def run(kernel, outs, args, scalars=0, layer=None, scratch=(), flops=0, out_space=pltpu.VMEM, wide=None, name=None):
+def run(kernel, outs, args, scalars=0, layer=None, scratch=(), flops=0, out_space=pltpu.VMEM, wide=None, loose=None, name=None):
     specs = []
     for i in range(len(args)):
         specs.append(pl.BlockSpec(memory_space=pltpu.SMEM if i < scalars else pltpu.VMEM))
@@ -448,7 +455,9 @@
             jax.ShapeDtypeStruct(shape, F32 if i == wide else BF) for i, shape in enumerate(outs)
         ],
         in_specs=specs,
-        out_specs=[pl.BlockSpec(memory_space=out_space) for _ in outs],
+        out_specs=[
+            pl.BlockSpec(memory_space=pl.ANY if i == loose else out_space) for i in range(len(outs))
+        ],
         scratch_shapes=scratch,
         compiler_params=pltpu.CompilerParams(vmem_limit_bytes=VMEM_LIMIT),
         cost_estimate=pl.CostEstimate(flops=flops, bytes_accessed=1 << 20, transcendentals=0),
@@ -537,6 +546,8 @@
         [rows_t, (doms * SLOTS, width)],
         (place, middle, states) + early + now + edges + (cluster_of, pooled, slot_pick, facts),
         scalars=1,
+        scratch=[pltpu.VMEM((doms * SLOTS, width), BF), pltpu.SemaphoreType.DMA((2,))],
+        loose=1,
         flops=10**9,
         name="ends_pool",
     )

time: 89 us -> 89 us (level)
  no operation moved by 1% of the time
where the time goes in v6:
time: 89 us; the launch traced here: 88.8 us
  starting transfers between devices  30.1 us (34%)
  Pallas kernels  23.7 us (27%)
  blocking collectives  19.6 us (22%)
  waiting for transfers between devices  12.5 us (14%)
  matrix products  1.6 us (2%)
  between operations  1.08 us (1%)
    pallas_call x11, Pallas kernels, run(): pl.pallas_call(kernel if layer is None else functools.partial(kernel, lay...  23.7 us
    all_to_all x1, blocking collectives, exchange(): rows = lax.all_to_all(rows, 'dom', split_axis=0, concat_axis=0, tiled=True)  19.6 us
    all_to_all x1, starting transfers between devices, exchange(): rows = lax.all_to_all(rows, 'dom', split_axis=0, concat_axis=0, tiled=True)  12.9 us
    ppermute x3, starting transfers between devices, swap(): from_far = lax.ppermute(far, ('dom', 'sub'), far_pairs)  10.2 us
    all_to_all x1, waiting for transfers between devices, exchange(): rows = lax.all_to_all(rows, 'dom', split_axis=0, concat_axis=0, tiled=True)  9.18 us
    ppermute x3, starting transfers between devices, on_device(): lax.ppermute(part, 'sub', [(i, i ^ k) for i in range(subs)])  5.9 us
    ppermute x3, waiting for transfers between devices, on_device(): lax.ppermute(part, 'sub', [(i, i ^ k) for i in range(subs)])  2.67 us
  transfers between devices with their start and end apart: 10, of which 4 were waited for; matrix products, arithmetic and copies ran while one was open for 0% of the time, Pallas kernels for 14%

profile of v6, /device:TPU:1, one launch (start us, length us, event | category | flops | bytes accessed | tf_op | source)
XLA Modules:
  0.0 88.8 jit_solution(8310636247907604118)
XLA Ops:
  0.7 1.6 %fusion.1 = bf16[256,128]{1,0:T(8,128)(2,1)S(1)} fusion(bf16[2048,128]{1,0:T(8,128)(2,1)} %nodes.1, s32[256]{0:T(256)} %bitcast.15), kind=kOutput, calls=%fused_computation.2 | convolution fusion | flops 134774784 | bytes 590848 | tf_op jit(solution)/shard_map/dot_general | solution.py:27
  2.3 5.8 %collective-permute-start.1 = (bf16[128,128]{1,0:T(8,128)(2,1)S(1)}, bf16[128,128]{1,0:T(8,128)(2,1)S(1)}, u32[]{:S(2)}, u32[]{:S(2)}) collective-permute-start(bf16[128,128]{1,0:T(8,128)(2,1)S(1)} %get-tuple-element.74), channel_id=1, source_target_pairs={{0,255},{1,2},{2,1},{3,4},{4,3},{5,6},{6,5},{7,8},{8,7},{9,10},{10... | collective-permute-start | bytes 98312 | tf_op jit(solution)/shard_map/ppermute | solution.py:497
  8.5 4.1 %inner_pick.1 = (bf16[128,2048]{1,0:T(8,128)(2,1)S(1)}, bf16[256,128]{1,0:T(8,128)(2,1)S(1)}, bf16[128,256]{1,0:T(8,128)(2,1)S(1)}, bf16[128,128]{1,0:T(8,128)(2,1)S(1)}, bf16[128,256]{1,0:T(8,128)(2,1)S(1)}) custom-call(s32[4]{0:T(128)S(1)} %pad_add_fusion.place, s32[2,128]{1,0:T(2,128)S(1)} %bitcast.16, bf16[128,2048]{1,0:T(8,128)(2,1)S(1)} %turn.1.rows_t.refs_0_, ...), custom_call_target="tpu_custom_call" | custom-call | flops 4000000000 | bytes 1048576 | tf_op jit(solution)/shard_map/inner_pick/pallas_call | solution.py:452
  12.6 1.8 %prepare.1 = (bf16[1024,256]{1,0:T(8,128)(2,1)S(1)}, bf16[128,128]{1,0:T(8,128)(2,1)S(1)}, bf16[768,128]{1,0:T(8,128)(2,1)S(1)}, bf16[16,256]{1,0:T(8,128)(2,1)S(1)}) custom-call(s32[4]{0:T(128)S(1)} %pad_add_fusion.place, s32[2,128]{1,0:T(2,128)S(1)} %bitcast.17, s32[1,2048]{1,0:T(1,128)S(1)} %copy-done.5, s32[1,128]{1,0:T(1,128)S(1)} %bitcast.20, ...), custom_call_target="tpu_custom_call" | custom-call | flops 1000000000 | bytes 1048576 | tf_op jit(solution)/shard_map/prepare/pallas_call | solution.py:452
  14.4 1.7 %ends_pick.1 = (bf16[128,2048]{1,0:T(8,128)(2,1)S(1)}, bf16[208,128]{1,0:T(8,128)(2,1)S(1)}, bf16[208,128]{1,0:T(8,128)(2,1)S(1)}) custom-call(s32[4]{0:T(128)S(1)} %pad_add_fusion.place, bf16[128,2048]{1,0:T(8,128)(2,1)S(1)} %get-tuple-element.38.inner, bf16[128,2048]{1,0:T(8,128)(2,1)S(1)} %turn.1.rows_t.refs_0_, ...), custom_call_target="tpu_custom_call" | custom-call | flops 1000000000 | bytes 1048576 | tf_op jit(solution)/shard_map/ends_pick/pallas_call | solution.py:452
  16.1 0.8 collective-permute-start.2
  16.9 1.1 %collective-permute-start.3 = (bf16[208,128]{1,0:T(8,128)(2,1)S(1)}, bf16[208,128]{1,0:T(8,128)(2,1)S(1)}, u32[]{:S(2)}, u32[]{:S(2)}) collective-permute-start(bf16[208,128]{1,0:T(8,128)(2,1)S(1)} %get-tuple-element.48), channel_id=1, source_target_pairs={{0,1},{1,0},{2,3},{3,2},{4,5},{5,4},{6,7},{7,6},{8,9},{9,8},{10,11... | collective-permute-start | bytes 159752 | tf_op jit(solution)/shard_map/ppermute | solution.py:498
  18.0 3.5 %inner_pool.1 = (bf16[128,2048]{1,0:T(8,128)(2,1)S(1)}, bf16[256,128]{1,0:T(8,128)(2,1)S(1)}, bf16[128,256]{1,0:T(8,128)(2,1)S(1)}, bf16[128,128]{1,0:T(8,128)(2,1)S(1)}, f32[128,128]{1,0:T(8,128)S(1)}) custom-call(s32[1,2048]{1,0:T(1,128)S(1)} %copy-done.5, bf16[128,2048]{1,0:T(8,128)(2,1)S(1)} %get-tuple-element.45.rows_t.refs_0_, ...), custom_call_target="tpu_custom_call" | custom-call | flops 4000000000 | bytes 1048576 | tf_op jit(solution)/shard_map/inner_pool/pallas_call | solution.py:452
  21.5 0.6 collective-permute-done.2.refs_1_.early_far
  22.1 2.7 %ends_pool.1 = (bf16[128,2048]{1,0:T(8,128)(2,1)S(1)}, bf16[1024,128]{1,0:T(8,128)(2,1)}) custom-call(s32[4]{0:T(128)S(1)} %pad_add_fusion.place, bf16[128,2048]{1,0:T(8,128)(2,1)S(1)} %get-tuple-element.46.inner, bf16[128,2048]{1,0:T(8,128)(2,1)S(1)} %get-tuple-element.45.rows_t.refs_0_, bf16[208,128]{1,0:T(8,128)(2,1)S(1)} %collective-permute-done.2.refs_1_.early_far, ...), custom_call_target="tpu_custom_call" | custom-call | flops 1000000000 | bytes 1048576 | tf_op jit(solution)/shard_map/ends_pool/pallas_call | solution.py:452
  24.9 12.9 %all-to-all-start = ((bf16[128,8,128]{2,1,0:T(8,128)(2,1)}), bf16[128,8,128]{2,1,0:T(8,128)(2,1)S(1)}, u32[]{:S(2)}, u32[]{:S(2)}) async-start(bf16[128,8,128]{2,1,0:T(8,128)(2,1)} %bitcast.7), calls=%async_computation | async-start | bytes 524288 | tf_op jit(solution)/shard_map/all_to_all | solution.py:568
  37.8 1.0 %pick.1 = (bf16[128,128]{1,0:T(8,128)(2,1)S(1)}, bf16[128,128]{1,0:T(8,128)(2,1)S(1)}, bf16[192,1024]{1,0:T(8,128)(2,1)S(1)}, bf16[192,1024]{1,0:T(8,128)(2,1)S(1)}) custom-call(s32[4]{0:T(128)S(1)} %pad_add_fusion.place, bf16[128,2048]{1,0:T(8,128)(2,1)S(1)} %get-tuple-element.54.rows_t, s32[2,128]{1,0:T(2,128)S(1)} %bitcast.19), custom_call_target="tpu_custom_call" | custom-call | flops 1000000000 | bytes 1048576 | tf_op jit(solution)/shard_map/pick/pallas_call | solution.py:452
  38.9 3.6 %collective-permute-start.7 = (bf16[128,128]{1,0:T(8,128)(2,1)S(1)}, bf16[128,128]{1,0:T(8,128)(2,1)S(1)}, u32[]{:S(2)}, u32[]{:S(2)}) collective-permute-start(bf16[128,128]{1,0:T(8,128)(2,1)S(1)} %get-tuple-element.60), channel_id=1, source_target_pairs={{0,255},{1,2},{2,1},{3,4},{4,3},{5,6},{6,5},{7,8},{8,7},{9,10},{10... | collective-permute-start | bytes 98312 | tf_op jit(solution)/shard_map/ppermute | solution.py:497
  42.5 9.2 %all-to-all-done = bf16[128,8,128]{2,1,0:T(8,128)(2,1)S(1)} async-done(((bf16[128,8,128]{2,1,0:T(8,128)(2,1)}), bf16[128,8,128]{2,1,0:T(8,128)(2,1)S(1)}, u32[]{:S(2)}, u32[]{:S(2)}) %all-to-all-start) | async-done | bytes 262176 | tf_op jit(solution)/shard_map/all_to_all | solution.py:568
  51.7 1.3 %received.1 = (bf16[176,128]{1,0:T(8,128)(2,1)S(1)}, bf16[64,128]{1,0:T(8,128)(2,1)S(1)}) custom-call(s32[4]{0:T(128)S(1)} %pad_add_fusion.place, bf16[1024,128]{1,0:T(8,128)(2,1)S(1)} %bitcast.12, bf16[192,1024]{1,0:T(8,128)(2,1)S(1)} %get-tuple-element.56.meta_pick, bf16[192,1024]{1,0:T(8,128)(2,1)S(1)} %get-tuple-element.57.spread), custom_call_target="tpu_custom_call" | custom-call | flops 1000000000 | bytes 1048576 | tf_op jit(solution)/shard_map/received/pallas_call | solution.py:452
  53.0 3.8 %collective-permute-start.6 = (bf16[176,128]{1,0:T(8,128)(2,1)S(1)}, bf16[176,128]{1,0:T(8,128)(2,1)S(1)}, u32[]{:S(2)}, u32[]{:S(2)}) collective-permute-start(bf16[176,128]{1,0:T(8,128)(2,1)S(1)} %get-tuple-element.58.own), channel_id=1, source_target_pairs={{0,3},{1,2},{2,1},{3,0},{4,7},{5,6},{6,5},{7,4},{8,11},{9,10},{10,... | collective-permute-start | bytes 135176 | tf_op jit(solution)/shard_map/ppermute | solution.py:579
  56.8 1.9 %collective-permute-start.5 = (bf16[176,128]{1,0:T(8,128)(2,1)S(1)}, bf16[176,128]{1,0:T(8,128)(2,1)S(1)}, u32[]{:S(2)}, u32[]{:S(2)}) collective-permute-start(bf16[176,128]{1,0:T(8,128)(2,1)S(1)} %get-tuple-element.58.own), channel_id=1, source_target_pairs={{0,2},{1,3},{2,0},{3,1},{4,6},{5,7},{6,4},{7,5},{8,10},{9,11},{10,... | collective-permute-start | bytes 135176 | tf_op jit(solution)/shard_map/ppermute | solution.py:579
  58.7 0.2 collective-permute-start.4
  58.9 0.5 ready.1
  59.4 1.5 %collective-permute-done.5.other2 = bf16[176,128]{1,0:T(8,128)(2,1)S(1)} collective-permute-done((bf16[176,128]{1,0:T(8,128)(2,1)S(1)}, bf16[176,128]{1,0:T(8,128)(2,1)S(1)}, u32[]{:S(2)}, u32[]{:S(2)}) %collective-permute-start.5) | collective-permute-done | bytes 45088 | tf_op jit(solution)/shard_map/ppermute | solution.py:579
  60.9 1.2 %collective-permute-done.4.other1 = bf16[176,128]{1,0:T(8,128)(2,1)S(1)} collective-permute-done((bf16[176,128]{1,0:T(8,128)(2,1)S(1)}, bf16[176,128]{1,0:T(8,128)(2,1)S(1)}, u32[]{:S(2)}, u32[]{:S(2)}) %collective-permute-start.4) | collective-permute-done | bytes 45088 | tf_op jit(solution)/shard_map/ppermute | solution.py:579
  62.1 1.7 %coarse.1 = (bf16[128,128]{1,0:T(8,128)(2,1)}, bf16[768,128]{1,0:T(8,128)(2,1)S(1)}) custom-call(bf16[176,128]{1,0:T(8,128)(2,1)S(1)} %get-tuple-element.58.own, bf16[176,128]{1,0:T(8,128)(2,1)S(1)} %collective-permute-done.4.other1, bf16[176,128]{1,0:T(8,128)(2,1)S(1)} %collective-permute-done.5.other2, bf16[176,128]{1,0:T(8,128)(2,1)S(1)} %collective-permute-done.6.other3, ...), custom_call_target="tpu_custom_call" | custom-call | flops 1000000000 | bytes 1048576 | tf_op jit(solution)/shard_map/coarse/pallas_call | solution.py:452
  63.8 19.6 %all_to_all.10 = bf16[192,4,128]{2,1,0:T(4,128)(2,1)S(1)} all-to-all(bf16[192,4,128]{2,1,0:T(4,128)(2,1)S(1)} %bitcast.14), channel_id=1, replica_groups=mesh['dom'=64,'sub'=4] {'dom'}, dimensions={0} | all-to-all | bytes 393216 | tf_op jit(solution)/shard_map/all_to_all | solution.py:568
  83.4 5.2 %final.1 = bf16[2048,128]{1,0:T(8,128)(2,1)} custom-call(s32[4]{0:T(128)S(1)} %pad_add_fusion.place, bf16[128,2048]{1,0:T(8,128)(2,1)S(1)} %get-tuple-element.54.rows_t, bf16[768,128]{1,0:T(8,128)(2,1)S(1)} %bitcast.13, bf16[768,128]{1,0:T(8,128)(2,1)S(1)} %get-tuple-element.69.slot_of, s32[1,2048]{1,0:T(1,128)S(1)} %copy-done.5, ...), custom_call_target="tpu_custom_call" | custom-call | flops 5000000000 | bytes 1048576 | tf_op jit(solution)/shard_map/final/pallas_call | solution.py:452
  (35 shorter events, 0.4 us)
Async XLA Ops:
  0.6 7.5 %copy-start.1 = (bf16[2048,128]{1,0:T(8,128)(2,1)S(1)}, bf16[2048,128]{1,0:T(8,128)(2,1)}, u32[]{:S(2)}) copy-start(bf16[2048,128]{1,0:T(8,128)(2,1)} %nodes.1) | copy-start | bytes 1572868
  2.3 6.2 %copy-start = (bf16[4,6,128,128]{3,2,1,0:T(8,128)(2,1)S(1)}, bf16[4,6,128,128]{3,2,1,0:T(8,128)(2,1)}, u32[]{:S(2)}) copy-start(bf16[4,6,128,128]{3,2,1,0:T(8,128)(2,1)} %weights.5) | copy-start | bytes 2359300
  2.3 6.2 %copy-start.2 = (s32[1,12288]{1,0:T(1,128)S(1)}, s32[1,12288]{1,0:T(1,128)}, u32[]{:S(2)}) copy-start(s32[1,12288]{1,0:T(1,128)} %src.7) | copy-start | bytes 147460
  2.3 6.2 %copy-start.3 = (s32[1,12288]{1,0:T(1,128)S(1)}, s32[1,12288]{1,0:T(1,128)}, u32[]{:S(2)}) copy-start(s32[1,12288]{1,0:T(1,128)} %dst.7) | copy-start | bytes 147460
  2.3 6.2 %copy-start.4 = (s32[1,12288]{1,0:T(1,128)S(1)}, s32[1,12288]{1,0:T(1,128)}, u32[]{:S(2)}) copy-start(s32[1,12288]{1,0:T(1,128)} %valid.5) | copy-start | bytes 147460
  2.3 6.2 %copy-start.9 = (s32[1,2,128]{2,1,0:T(2,128)S(1)}, s32[1,2,128]{2,1,0:T(2,128)}, u32[]{:S(2)}) copy-start(s32[1,2,128]{2,1,0:T(2,128)} %param.17) | copy-start | bytes 3076
  2.3 12.1 %collective-permute-start.1 = (bf16[128,128]{1,0:T(8,128)(2,1)S(1)}, bf16[128,128]{1,0:T(8,128)(2,1)S(1)}, u32[]{:S(2)}, u32[]{:S(2)}) collective-permute-start(bf16[128,128]{1,0:T(8,128)(2,1)S(1)} %get-tuple-element.74), channel_id=1, source_target_pairs={{0,255},{1,2},{2,1},{3,4},{4,3},{5,6},{6,5},{7,8},{8,7},{9,10},{10... | collective-permute-start | bytes 98312 | tf_op jit(solution)/shard_map/ppermute | solution.py:497
  8.2 6.2 %collective-permute-start = (bf16[128,128]{1,0:T(8,128)(2,1)S(1)}, bf16[128,128]{1,0:T(8,128)(2,1)S(1)}, u32[]{:S(2)}, u32[]{:S(2)}) collective-permute-start(bf16[128,128]{1,0:T(8,128)(2,1)S(1)} %get-tuple-element.75), channel_id=1, source_target_pairs={{0,1},{1,0},{2,3},{3,2},{4,5},{5,4},{6,7},{7,6},{8,9},{9,8},{10,11... | collective-permute-start | bytes 98312 | tf_op jit(solution)/shard_map/ppermute | solution.py:498
  8.5 4.1 %copy-start.5 = (s32[1,2048]{1,0:T(1,128)S(1)}, s32[1,2048]{1,0:T(1,128)}, u32[]{:S(2)}) copy-start(s32[1,2048]{1,0:T(1,128)} %cluster.5) | copy-start | bytes 24580
  8.5 4.1 %copy-start.8 = (s32[1,2,16]{2,1,0:T(2,128)S(1)}, s32[1,2,16]{2,1,0:T(2,128)}, u32[]{:S(2)}) copy-start(s32[1,2,16]{2,1,0:T(2,128)} %ghosts.1) | copy-start | bytes 388
  8.5 4.1 %copy-start.10 = (s32[1,128,1]{1,2,0:T(1,128)S(1)}, s32[1,128,1]{1,2,0:T(1,128)}, u32[]{:S(2)}) copy-start(s32[1,128,1]{1,2,0:T(1,128)} %param.19) | copy-start | bytes 1540
  8.5 4.1 %copy-start.11 = (s32[1,128]{1,0:T(1,128)S(1)}, s32[1,128]{1,0:T(1,128)}, u32[]{:S(2)}) copy-start(s32[1,128]{1,0:T(1,128)} %coarse_row.1) | copy-start | bytes 1540
  16.1 6.0 %collective-permute-start.2 = (bf16[208,128]{1,0:T(8,128)(2,1)S(1)}, bf16[208,128]{1,0:T(8,128)(2,1)S(1)}, u32[]{:S(2)}, u32[]{:S(2)}) collective-permute-start(bf16[208,128]{1,0:T(8,128)(2,1)S(1)} %get-tuple-element.47), channel_id=1, source_target_pairs={{0,255},{1,2},{2,1},{3,4},{4,3},{5,6},{6,5},{7,8},{8,7},{9,10},{10... | collective-permute-start | bytes 159752 | tf_op jit(solution)/shard_map/ppermute | solution.py:497
  16.9 5.2 %collective-permute-start.3 = (bf16[208,128]{1,0:T(8,128)(2,1)S(1)}, bf16[208,128]{1,0:T(8,128)(2,1)S(1)}, u32[]{:S(2)}, u32[]{:S(2)}) collective-permute-start(bf16[208,128]{1,0:T(8,128)(2,1)S(1)} %get-tuple-element.48), channel_id=1, source_target_pairs={{0,1},{1,0},{2,3},{3,2},{4,5},{5,4},{6,7},{7,6},{8,9},{9,8},{10,11... | collective-permute-start | bytes 159752 | tf_op jit(solution)/shard_map/ppermute | solution.py:498
  24.9 26.8 %all-to-all-start = ((bf16[128,8,128]{2,1,0:T(8,128)(2,1)}), bf16[128,8,128]{2,1,0:T(8,128)(2,1)S(1)}, u32[]{:S(2)}, u32[]{:S(2)}) async-start(bf16[128,8,128]{2,1,0:T(8,128)(2,1)} %bitcast.7), calls=%async_computation | async-start | bytes 524288 | tf_op jit(solution)/shard_map/all_to_all | solution.py:568
  38.9 20.1 %collective-permute-start.7 = (bf16[128,128]{1,0:T(8,128)(2,1)S(1)}, bf16[128,128]{1,0:T(8,128)(2,1)S(1)}, u32[]{:S(2)}, u32[]{:S(2)}) collective-permute-start(bf16[128,128]{1,0:T(8,128)(2,1)S(1)} %get-tuple-element.60), channel_id=1, source_target_pairs={{0,255},{1,2},{2,1},{3,4},{4,3},{5,6},{6,5},{7,8},{8,7},{9,10},{10... | collective-permute-start | bytes 98312 | tf_op jit(solution)/shard_map/ppermute | solution.py:497
  42.5 16.4 %collective-permute-start.8 = (bf16[128,128]{1,0:T(8,128)(2,1)S(1)}, bf16[128,128]{1,0:T(8,128)(2,1)S(1)}, u32[]{:S(2)}, u32[]{:S(2)}) collective-permute-start(bf16[128,128]{1,0:T(8,128)(2,1)S(1)} %get-tuple-element.61), channel_id=1, source_target_pairs={{0,1},{1,0},{2,3},{3,2},{4,5},{5,4},{6,7},{7,6},{8,9},{9,8},{10,11... | collective-permute-start | bytes 98312 | tf_op jit(solution)/shard_map/ppermute | solution.py:498
  51.7 7.2 %copy-start.6 = (s32[1,768]{1,0:T(1,128)S(1)}, s32[1,768]{1,0:T(1,128)}, u32[]{:S(2)}) copy-start(s32[1,768]{1,0:T(1,128)} %src.6) | copy-start | bytes 9220
  51.7 7.2 %copy-start.7 = (s32[1,768]{1,0:T(1,128)S(1)}, s32[1,768]{1,0:T(1,128)}, u32[]{:S(2)}) copy-start(s32[1,768]{1,0:T(1,128)} %dst.6) | copy-start | bytes 9220
  53.0 6.4 %collective-permute-start.6 = (bf16[176,128]{1,0:T(8,128)(2,1)S(1)}, bf16[176,128]{1,0:T(8,128)(2,1)S(1)}, u32[]{:S(2)}, u32[]{:S(2)}) collective-permute-start(bf16[176,128]{1,0:T(8,128)(2,1)S(1)} %get-tuple-element.58.own), channel_id=1, source_target_pairs={{0,3},{1,2},{2,1},{3,0},{4,7},{5,6},{6,5},{7,4},{8,11},{9,10},{10,... | collective-permute-start | bytes 135176 | tf_op jit(solution)/shard_map/ppermute | solution.py:579
  56.8 4.1 %collective-permute-start.5 = (bf16[176,128]{1,0:T(8,128)(2,1)S(1)}, bf16[176,128]{1,0:T(8,128)(2,1)S(1)}, u32[]{:S(2)}, u32[]{:S(2)}) collective-permute-start(bf16[176,128]{1,0:T(8,128)(2,1)S(1)} %get-tuple-element.58.own), channel_id=1, source_target_pairs={{0,2},{1,3},{2,0},{3,1},{4,6},{5,7},{6,4},{7,5},{8,10},{9,11},{10,... | collective-permute-start | bytes 135176 | tf_op jit(solution)/shard_map/ppermute | solution.py:579
  58.7 3.4 %collective-permute-start.4 = (bf16[176,128]{1,0:T(8,128)(2,1)S(1)}, bf16[176,128]{1,0:T(8,128)(2,1)S(1)}, u32[]{:S(2)}, u32[]{:S(2)}) collective-permute-start(bf16[176,128]{1,0:T(8,128)(2,1)S(1)} %get-tuple-element.58.own), channel_id=1, source_target_pairs={{0,1},{1,0},{2,3},{3,2},{4,5},{5,4},{6,7},{7,6},{8,9},{9,8},{10,11... | collective-permute-start | bytes 135176 | tf_op jit(solution)/shard_map/ppermute | solution.py:579
